TPU v7x, 32 devices: a whole 2x2x4 slice. The times are simulated.
32 devices in a mesh: af: 8 (over y, x, core), ta: 4 (over z).
Axes of the slice: x: 2, y: 2, z: 4, core: 2. Of those that a mesh axis runs over, the one named last changes fastest.
Arguments:
- samples: bfloat16 [1024, 512, 512], P('ta', 'af'), may hold values from -6 to 6
Outputs:
- visibility: float32 [512, 128, 512], P('ta', 'af')
All inputs are finite; a program needn't handle non-finite values.
Results may differ from a plain program's by a relative error of at most 0.0022.
Values may be sent and summed in bfloat16 or wider, within the bound.
No kernel may reach another device: no remote copies, remote signals or barrier semaphores. Data moves between devices by JAX's collectives and lax.ppermute only.
A program may use at most 128 MiB of HBM per device.

v0:
```python
import math

import jax
import jax.numpy as jnp
from jax import lax
from jax.sharding import PartitionSpec as P

CH = 128
TAPS = 4


def passed_along(value, axis, steps):
    count = lax.axis_size(axis)
    first, last = (max(0, -steps), min(count, count - steps))
    return lax.ppermute(value, axis, [(source, source + steps) for source in range(first, last)])


def tap_window(taps, samp_len):
    points = jnp.arange(taps * samp_len).astype(jnp.float32)
    centre = (taps * samp_len - 1) / 2.0
    shape_part = jnp.sinc((points - centre) / samp_len)
    taper = jnp.square(jnp.sin(math.pi * (points + 0.5) / (taps * samp_len)))
    return (shape_part * taper).reshape(taps, samp_len)


def dft_table(samp_len, channels):
    sample_idx = jnp.arange(samp_len)[:, None]
    chan_idx = jnp.arange(channels)[None, :]
    phase = (sample_idx * chan_idx % samp_len).astype(jnp.float32) * (2.0 * math.pi / samp_len)
    scale = 1.0 / math.sqrt(samp_len)
    both = jnp.stack([jnp.cos(phase) * scale, -jnp.sin(phase) * scale], axis=2)
    return both.reshape(samp_len, 2 * channels).astype(jnp.bfloat16)


def on_device(samples):
    frames, inputs, samp_len = samples.shape
    earlier = passed_along(samples[frames - (TAPS - 1) :], "ta", 1)
    extended = jnp.concatenate([earlier, samples], axis=0)
    weights = tap_window(TAPS, samp_len)
    filtered = jnp.zeros((frames, inputs, samp_len), jnp.float32)
    for tap in range(TAPS):
        filtered = filtered + weights[tap][None, None, :] * extended[tap : tap + frames].astype(
            jnp.float32
        )
    filtered = filtered.astype(jnp.bfloat16)
    table = dft_table(samp_len, CH)
    spectrum = jnp.einsum("nc,fin->cfi", table, filtered, preferred_element_type=jnp.float32)
    spectrum = spectrum.astype(jnp.bfloat16)
    turned = lax.all_to_all(spectrum, "af", split_axis=0, concat_axis=2, tiled=True)
    all_inputs = turned.shape[2]
    local_chans = turned.shape[0] // 2
    total_frames = frames * lax.axis_size("ta")
    lefts = []
    rotated = []
    for channel in range(local_chans):
        real_part = turned[2 * channel]
        imag_part = turned[2 * channel + 1]
        lefts.append(jnp.concatenate([real_part, imag_part], axis=0))
        rotated.append(jnp.concatenate([imag_part, -real_part], axis=0))
    row_idx = jnp.arange(all_inputs)[:, None]
    col_idx = jnp.arange(all_inputs)[None, :]
    upper = row_idx <= col_idx
    results = []
    for channel in range(local_chans):
        left_rows = lefts[channel]
        turn_rows = rotated[channel]
        stacked = jnp.concatenate([left_rows, turn_rows], axis=1)
        product = lax.dot_general(
            stacked, lefts[channel], (((0,), (0,)), ((), ())), preferred_element_type=jnp.float32
        )
        packed = jnp.where(upper, product[:all_inputs], product[all_inputs:]) / total_frames
        results.append(packed)
    return lax.psum_scatter(jnp.stack(results, axis=1), "ta", scatter_dimension=0, tiled=True)


def solution(mesh):
    in_specs = (P("ta", "af", None),)
    out_specs = P("ta", "af", None)
    return jax.shard_map(
        on_device, mesh=mesh, in_specs=in_specs, out_specs=out_specs, check_vma=False
    )
```

profile of v0, /device:TPU:0, one launch (start us, length us, event | category | flops | bytes accessed | tf_op | source)
XLA Modules:
  0.0 518.1 jit_solution(16485606021178841243)
XLA Ops:
  6.5 0.9 slice.253
  7.5 4.9 collective-permute-start
  12.5 1.1 multiply_convert_fusion
  13.6 0.2 copy.16
  13.8 0.1 reshape.156
  14.0 2.6 collective-permute-done
  16.6 0.7 constant_dynamic-update-slice_fusion.1
  17.2 14.0 %constant_dynamic-update-slice_fusion = bf16[259,64,512]{2,1,0:T(8,128)(2,1)} fusion(bf16[259,64,512]{2,1,0:T(8,128)(2,1)} %constant_dynamic-update-slice_fusion.1, bf16[256,64,512]{2,1,0:T(8,128)(2,1)} %param.1), kind=kLoop, calls=%fused_computation.257 | loop fusion | bytes 33554432 | tf_op jit(solution)/shard_map/concatenate | solution.py:38
  31.2 31.2 %add_convert_fusion = bf16[256,64,512]{2,1,0:T(8,128)(2,1)} fusion(bf16[256,64,512]{2,1,0:T(8,128)(2,1)} %param.1, bf16[259,64,512]{2,1,0:T(8,128)(2,1)} %constant_dynamic-update-slice_fusion, f32[512]{0:T(512)S(1)} %get-tuple-element.38, f32[512]{0:T(512)S(1)} %get-tuple-element.39, f32[512]{0:T(512)S(1)} %get-tuple-element.40, f32[512]{0:T(512)S(1)} %get-tuple-element.37), kind=kLoop, calls=%fused_computation | loop fusion | flops 100663296 | bytes 83894272 | tf_op jit(solution)/shard_map/convert_element_type | solution.py:45
  62.4 20.4 %fusion.2 = bf16[256,256,64]{1,0,2:T(8,128)(2,1)} fusion(bf16[512,256,1]{0,1,2:T(8,128)(2,1)S(1)} %reshape.156, bf16[256,64,512]{2,1,0:T(8,128)(2,1)} %add_convert_fusion), kind=kOutput, calls=%fused_computation.3 | convolution fusion | flops 4299161600 | bytes 25427968 | tf_op jit(solution)/shard_map/nc,fin->cfi/dot_general | solution.py:47
  82.8 11.4 %copy.18 = bf16[256,256,64]{1,2,0:T(8,128)(2,1)} copy(bf16[256,256,64]{1,0,2:T(8,128)(2,1)} %fusion.2) | data formatting | bytes 16777216 | tf_op jit(solution)/shard_map/convert_element_type | solution.py:48
  94.2 97.8 %all_to_all.15 = bf16[256,256,64]{1,2,0:T(8,128)(2,1)S(1)} all-to-all(bf16[256,256,64]{1,2,0:T(8,128)(2,1)} %copy.18), channel_id=1, replica_groups=mesh['af'=8,'ta'=4] {'af'}, dimensions={0} | all-to-all | bytes 16777216 | tf_op jit(solution)/shard_map/all_to_all | solution.py:49
  192.0 0.4 fusion.265
  192.4 0.8 fusion.264
  193.3 0.7 fusion.53
  194.0 1.1 fusion.52
  195.8 0.7 fusion.61
  196.5 1.2 fusion.49
  197.7 0.7 fusion.69
  198.4 1.1 fusion.46
  199.5 0.7 fusion.77
  200.3 1.1 fusion.43
  201.4 0.7 fusion.85
  202.1 1.1 fusion.40
  203.2 0.7 fusion.93
  204.0 1.1 fusion.37
  205.1 0.7 fusion.101
  205.9 1.1 fusion.34
  207.0 0.7 fusion.109
  207.7 1.1 fusion.31
  208.9 0.7 fusion.117
  209.6 1.2 fusion.28
  210.8 0.7 fusion.125
  211.5 1.1 fusion.25
  212.6 0.7 fusion.133
  213.4 1.1 fusion.22
  214.5 0.7 fusion.141
  215.2 1.1 fusion.19
  216.3 0.7 fusion.149
  217.1 1.2 fusion.16
  218.2 0.7 fusion.157
  219.0 1.1 fusion.13
  220.1 0.7 fusion.165
  220.8 1.1 fusion.10
  222.0 0.7 fusion.173
  222.7 1.1 fusion.7
  223.9 280.7 %reduce-scatter.2.cloned.1.call-done = f32[128,16,512]{2,0,1:T(8,128)} async-done(((f32[512,16,512]{2,0,1:T(8,128)}), f32[128,16,512]{2,0,1:T(8,128)}) %reduce-scatter.2.cloned.1.call-update) | async-done | bytes 4194320 | tf_op jit(solution)/shard_map/reduce_scatter | solution.py:73
  504.6 6.6 %copy.19 = f32[128,16,512]{2,1,0:T(8,128)} copy(f32[128,16,512]{2,0,1:T(8,128)} %reduce-scatter.2.cloned.1.call-done) | data formatting | bytes 8388608 | tf_op jit(solution)/shard_map/reduce_scatter | solution.py:73
  (21 shorter events, 0.7 us)
Async XLA Ops:
  6.5 498.1 %reduce-scatter.2.cloned.1.call-start = ((), (), s32[]{:S(2)}) async-start(), calls=%async_computation.2 | async-start | bytes 20971520 | tf_op jit(solution)/shard_map/reduce_scatter | solution.py:73
  7.5 9.1 %collective-permute-start = (bf16[3,64,512]{2,1,0:T(8,128)(2,1)S(1)}, bf16[3,64,512]{2,1,0:T(8,128)(2,1)S(1)}, u32[]{:S(2)}, u32[]{:S(2)}) collective-permute-start(bf16[3,64,512]{2,1,0:T(8,128)(2,1)S(1)} %slice.253), channel_id=1, source_target_pairs={{0,1},{1,2},{2,3},{4,5},{5,6},{6,7},{8,9},{9,10},{10,11},{12,13},{... | collective-permute-start | bytes 589832 | tf_op jit(solution)/shard_map/ppermute | solution.py:15
Sparse Core Ops, SparseCore 0:
  224.0 280.5 reduce-scatter.1
where the time goes:
time: 518 us
  waiting for transfers between devices  283 us (55%)
  blocking collectives  97.8 us (19%)
  other arithmetic  51.1 us (10%)
  local copies, waits for them, and re-layouts  35.1 us (7%)
  matrix products  32.1 us (6%)
  between operations  13.6 us (3%)
    reduce_scatter x1, waiting for transfers between devices, on_device(): lax.psum_scatter(jnp.stack(results, axis=1), 'ta', scatter_dimension=0, t...  281 us
    all_to_all x1, blocking collectives, on_device(): lax.all_to_all(spectrum, 'af', split_axis=0, concat_axis=2, tiled=True)  97.8 us
    convert_element_type x1, other arithmetic, on_device(): filtered = filtered.astype(jnp.bfloat16)  31.2 us
    dot_general x1, matrix products, on_device(): jnp.einsum('nc,fin->cfi', table, filtered, preferred_element_type=jnp.flo...  20.4 us
    unnamed x15, other arithmetic  17 us
    concatenate x1, local copies, waits for them, and re-layouts, on_device(): extended = jnp.concatenate([earlier, samples], axis=0)  14 us
    dot_general x16, matrix products, on_device(): lax.dot_general(stacked, lefts[channel], (((0,), (0,)), ((), ())), prefer...  11.7 us
    convert_element_type x1, local copies, waits for them, and re-layouts, on_device(): spectrum = spectrum.astype(jnp.bfloat16)  11.4 us
  transfers between devices with their start and end apart: 2, of which 2 were waited for; matrix products, arithmetic and copies ran while one was open for 0% of the time, Pallas kernels for 0%

commit v1 on v0

v1 whole, which is shorter than its diff:
```python
import functools
import math

import jax
import jax.numpy as jnp
from jax import lax
from jax.experimental import pallas as pl
from jax.experimental.pallas import tpu as pltpu
from jax.sharding import PartitionSpec as P

CH = 128
TAPS = 4
LANES = 128
ROWS = 16
VMEM = 48 * 1024 * 1024


def chunk_sizes(count):
    if count < 8:
        return [1] * count
    sizes = [1, 2]
    while sum(sizes) < count - 2:
        sizes.append(min(max(1, count // 5), count - 2 - sum(sizes)))
    return sizes + [2]


def tap_window(taps, samp_len):
    points = jnp.arange(taps * samp_len).astype(jnp.float32)
    centre = (taps * samp_len - 1) / 2.0
    shape_part = jnp.sinc((points - centre) / samp_len)
    taper = jnp.square(jnp.sin(math.pi * (points + 0.5) / (taps * samp_len)))
    return (shape_part * taper).reshape(taps, samp_len)


def dft_rows(samp_len, channels):
    sample_idx = jnp.arange(samp_len)[None, :]
    phase = (sample_idx * channels[:, None] % samp_len).astype(jnp.float32) * (
        2.0 * math.pi / samp_len
    )
    scale = 1.0 / math.sqrt(samp_len)
    both = jnp.stack([jnp.cos(phase) * scale, -jnp.sin(phase) * scale], axis=1)
    return both.reshape(-1, samp_len).astype(jnp.bfloat16)


def channelizer_body(widths, x_ref, halo_ref, w_ref, table_ref, *rest):
    outs, (carry, filt, spec) = rest[: len(widths)], rest[len(widths) :]
    block, inputs, samp_len = x_ref.shape
    tiles = block * inputs // LANES
    columns = table_ref.shape[0]

    @pl.when(pl.program_id(0) == 0)
    def _():
        carry[...] = halo_ref[...]

    def fir(group, _):
        rows = pl.ds(pl.multiple_of(group * ROWS, ROWS), ROWS)
        for lane in range(0, samp_len, LANES):
            cols = pl.ds(lane, LANES)
            weights = [
                jnp.broadcast_to(w_ref[p : p + 1, cols], (ROWS, LANES)) for p in range(TAPS)
            ]
            past = [carry[p, rows, cols].astype(jnp.float32) for p in range(TAPS - 1)]
            for f in range(block):
                past.append(x_ref[f, rows, cols].astype(jnp.float32))
                total = weights[0] * past[0]
                for p in range(1, TAPS):
                    total = total + weights[p] * past[p]
                place = pl.ds(pl.multiple_of(f * inputs + group * ROWS, ROWS), ROWS)
                filt[place, cols] = total.astype(jnp.bfloat16)
                past.pop(0)
        return 0

    lax.fori_loop(0, inputs // ROWS, fir, 0)
    carry[...] = x_ref[pl.ds(block - (TAPS - 1), TAPS - 1)]

    step = 2 if tiles % 2 == 0 else 1
    for at in range(0, tiles, step):
        product = lax.dot_general(
            table_ref[...],
            filt[pl.ds(at * LANES, step * LANES), :],
            (((1,), (1,)), ((), ())),
            preferred_element_type=jnp.float32,
        )
        for k in range(step):
            spec[pl.ds((at + k) * columns, columns), :] = product[:, k * LANES : (k + 1) * LANES]

    row = 0
    for out, width in zip(outs, widths):
        for r in range(width):
            out[r] = spec[pl.ds(row + r, tiles, stride=columns), :].astype(jnp.bfloat16)
        row += width


def channelize(samples, halo, window, table, widths):
    frames, inputs, samp_len = samples.shape
    per_tile = LANES // inputs
    block = min(frames, ROWS * per_tile)
    tiles = block // per_tile
    columns = table.shape[0]
    return pl.pallas_call(
        functools.partial(channelizer_body, widths),
        grid=(frames // block,),
        in_specs=[
            pl.BlockSpec((block, inputs, samp_len), lambda b: (b, 0, 0)),
            pl.BlockSpec(halo.shape, lambda b: (0, 0, 0)),
            pl.BlockSpec(window.shape, lambda b: (0, 0)),
            pl.BlockSpec(table.shape, lambda b: (0, 0)),
        ],
        out_specs=[pl.BlockSpec((w, tiles, LANES), lambda b: (0, b, 0)) for w in widths],
        out_shape=[
            jax.ShapeDtypeStruct((w, frames // per_tile, LANES), jnp.bfloat16) for w in widths
        ],
        scratch_shapes=[
            pltpu.VMEM((TAPS - 1, inputs, samp_len), jnp.bfloat16),
            pltpu.VMEM((block * inputs, samp_len), jnp.bfloat16),
            pltpu.VMEM((tiles * columns, LANES), jnp.float32),
        ],
        compiler_params=pltpu.CompilerParams(
            dimension_semantics=("arbitrary",), vmem_limit_bytes=VMEM
        ),
        cost_estimate=pl.CostEstimate(
            flops=2 * frames * inputs * samp_len * columns,
            bytes_accessed=frames * inputs * (samp_len + columns) * 2,
            transcendentals=0,
        ),
        name="channelizer",
    )(samples, halo, window, table)


def correlate_body(groups, inputs, scale, where_ref, *rest):
    sources, (others, own, left, turn) = rest[:groups], rest[groups:]
    per_tile = LANES // inputs
    tiles = sources[0].shape[1]
    total = groups * inputs
    me, block = where_ref[0], where_ref[1]
    half = tiles * per_tile

    for mine in range(per_tile):

        @pl.when(me % per_tile == mine)
        def _(mine=mine):
            for t in range(0, groups, per_tile):
                at = pl.multiple_of((me // per_tile ^ t // per_tile) * LANES, LANES)
                for part in range(2):
                    held = [sources[t + (mine ^ j)][part] for j in range(per_tile)]
                    for g in range(per_tile):
                        value = jnp.concatenate(
                            [h[:, g * inputs : (g + 1) * inputs] for h in held], axis=1
                        )
                        rows = pl.ds(part * half + g * tiles, tiles)
                        left[rows, pl.ds(at, LANES)] = value

    turn[pl.ds(0, half), :] = left[pl.ds(half, half), :]
    turn[pl.ds(half, half), :] = -left[pl.ds(0, half), :]

    size = own.shape[1]
    count = total // size
    row_idx = lax.broadcasted_iota(jnp.int32, (size, total), 0)
    col_idx = lax.broadcasted_iota(jnp.int32, (size, total), 1)
    dims = (((0,), (0,)), ((), ()))
    for i in range(count):
        cols = pl.ds(i * size, size)
        re = lax.dot_general(left[:, cols], left[...], dims, preferred_element_type=jnp.float32)
        im = lax.dot_general(turn[:, cols], left[...], dims, preferred_element_type=jnp.float32)
        packed = jnp.where(row_idx + i * size <= col_idx, re, im) * scale
        if count > 1:
            slot = (i - block - 1 + count) % count

            @pl.when(slot < count - 1)
            def _():
                others[jnp.minimum(slot, count - 2), 0] = packed.astype(jnp.bfloat16)

        @pl.when(block == i)
        def _():
            own[0] = packed


def correlate(where, sources, blocks, inputs, scale):
    width, tiles, _ = sources[0].shape
    chans = width // 2
    groups = len(sources)
    total = groups * inputs
    size = total // blocks
    depth = 2 * tiles * (LANES // inputs)
    return pl.pallas_call(
        functools.partial(correlate_body, groups, inputs, scale),
        grid_spec=pltpu.PrefetchScalarGridSpec(
            num_scalar_prefetch=1,
            grid=(chans,),
            in_specs=[pl.BlockSpec((2, tiles, LANES), lambda c, _: (c, 0, 0))] * groups,
            out_specs=[
                pl.BlockSpec((max(blocks - 1, 1), 1, size, total), lambda c, _: (0, c, 0, 0)),
                pl.BlockSpec((1, size, total), lambda c, _: (c, 0, 0)),
            ],
            scratch_shapes=[pltpu.VMEM((depth, total), jnp.bfloat16)] * 2,
        ),
        out_shape=[
            jax.ShapeDtypeStruct((max(blocks - 1, 1), chans, size, total), jnp.bfloat16),
            jax.ShapeDtypeStruct((chans, size, total), jnp.float32),
        ],
        compiler_params=pltpu.CompilerParams(
            dimension_semantics=("arbitrary",), vmem_limit_bytes=VMEM
        ),
        cost_estimate=pl.CostEstimate(
            flops=chans * 4 * depth * total * total,
            bytes_accessed=chans * (groups * 4 * tiles * LANES + 2 * total * total + 2 * size * total),
            transcendentals=0,
        ),
        name="correlate",
    )(where, *sources)


def line_sum(own, others, axis, block):
    count = lax.axis_size(axis)
    total = own
    held = None
    for t in range(count - 1):
        span = count - 1 - t
        right, left = (t, t + 1), (count - 1 - t, count - 2 - t)
        heading_left = block == left[0]
        if t == 0:
            sends = [others, others]
        else:
            sends = []
            for first, taken, got in ((0, 1, held[0]), (t, 0, held[1])):
                mine = lax.slice_in_dim(others, first, first + span, axis=0)
                came = lax.slice_in_dim(got, taken, taken + span, axis=0)
                sends.append((mine.astype(jnp.float32) + came.astype(jnp.float32)).astype(jnp.bfloat16))
        if count % 2 == 0:
            send = sends[0] if t == 0 else jnp.where(heading_left, sends[1], sends[0])
            got = lax.ppermute(send, axis, [right, left])
            held = [got, got]
            pick = jnp.where(block == right[1], 0, span - 1)
            total = total + lax.dynamic_index_in_dim(got, pick, 0, keepdims=False).astype(jnp.float32)
        else:
            held = [
                lax.ppermute(sends[0], axis, [right]),
                lax.ppermute(sends[1], axis, [left]),
            ]
            total = total + held[0][0].astype(jnp.float32) + held[1][span - 1].astype(jnp.float32)
    return total


def on_device(samples):
    frames, inputs, samp_len = samples.shape
    groups = lax.axis_size("af")
    blocks = lax.axis_size("ta")
    me = lax.axis_index("af")
    block = lax.axis_index("ta")
    local = CH // groups
    sizes = chunk_sizes(local)
    earlier = lax.ppermute(
        samples[frames - (TAPS - 1) :], "ta", [(i, i + 1) for i in range(blocks - 1)]
    )
    window = tap_window(TAPS, samp_len)
    order, widths, first = [], [], 0
    for size in sizes:
        for s in range(groups):
            order.append((me ^ s) * local + first + jnp.arange(size))
            widths.append(2 * size)
        first += size
    table = dft_rows(samp_len, jnp.concatenate(order))
    spectra = channelize(samples, earlier, window, table, widths)
    where = jnp.stack([me, block]).astype(jnp.int32)
    results = []
    for c in range(len(sizes)):
        mine = spectra[c * groups : (c + 1) * groups]
        turned = [mine[0]]
        for s in range(1, groups):
            turned.append(lax.ppermute(mine[s], "af", [(i, i ^ s) for i in range(groups)]))
        others, own = correlate(where, turned, blocks, inputs, 1.0 / (frames * blocks))
        results.append(line_sum(own, others, "ta", block))
    return jnp.transpose(jnp.concatenate(results, axis=0), (1, 0, 2))


def solution(mesh):
    in_specs = (P("ta", "af", None),)
    out_specs = P("ta", "af", None)
    return jax.shard_map(
        on_device, mesh=mesh, in_specs=in_specs, out_specs=out_specs, check_vma=False
    )
```

time: 518 us -> 359 us (0.69)
  waiting for transfers between devices: 283 us -> 155 us
  blocking collectives: 97.8 us -> 0 us
  starting transfers between devices: 4.94 us -> 88.5 us
  Pallas kernels: 0 us -> 63.6 us
  other arithmetic: 51.1 us -> 9.89 us
  matrix products: 32.1 us -> 0 us
  between operations: 13.6 us -> 1.1 us
    reduce_scatter x1 -> x0, waiting for transfers between devices: 281 us -> none  [on_device(): lax.psum_scatter(jnp.stack(results, axis=1), 'ta', scatter_dimension=0, t...]
    ppermute x1 -> x71, waiting for transfers between devices: 2.6 us -> 155 us  [the longest x21 115 us: line_sum(): got = lax.ppermute(send, axis, [right, left])]
    all_to_all x1 -> x0, blocking collectives: 97.8 us -> none  [on_device(): lax.all_to_all(spectrum, 'af', split_axis=0, concat_axis=2, tiled=True)]
    ppermute x1 -> x71, starting transfers between devices: 4.94 us -> 88.5 us  [the longest x49 49.1 us: on_device(): lax.ppermute(mine[s], 'af', [(i, i ^ s) for i in range(groups)])]
    pallas_call x0 -> x8, Pallas kernels: none -> 63.6 us  [the longest x7 32.6 us: correlate(): pl.pallas_call(functools.partial(correlate_body, groups, inputs, scale),...]
    unnamed x1 -> x142, local copies, waits for them, and re-layouts: 0.68 us -> 33.5 us
    dot_general x17 -> x0, matrix products: 32.1 us -> none  [the longest x1 20.4 us: on_device(): jnp.einsum('nc,fin->cfi', table, filtered, preferred_element_type=jnp.flo...]
    convert_element_type x1 -> x0, other arithmetic: 31.2 us -> none  [on_device(): filtered = filtered.astype(jnp.bfloat16)]
  transfers between devices with their start and end apart: 2 -> 71, of which waited for: 2 -> 20; matrix products, arithmetic and copies ran while one was open for 0% -> 3% of each run, Pallas kernels for 0% -> 9%
where the time goes in v1:
time: 359 us; the launch traced here: 358 us
  waiting for transfers between devices  155 us (43%)
  starting transfers between devices  88.5 us (25%)
  Pallas kernels  63.6 us (18%)
  local copies, waits for them, and re-layouts  40.1 us (11%)
  other arithmetic  9.89 us (3%)
    ppermute x21, waiting for transfers between devices, line_sum(): got = lax.ppermute(send, axis, [right, left])  115 us
    ppermute x49, starting transfers between devices, on_device(): lax.ppermute(mine[s], 'af', [(i, i ^ s) for i in range(groups)])  49.1 us
    ppermute x49, waiting for transfers between devices, on_device(): lax.ppermute(mine[s], 'af', [(i, i ^ s) for i in range(groups)])  38.2 us
    ppermute x21, starting transfers between devices, line_sum(): got = lax.ppermute(send, axis, [right, left])  34.4 us
    unnamed x142, local copies, waits for them, and re-layouts  33.5 us
    pallas_call x7, Pallas kernels, correlate(): pl.pallas_call(functools.partial(correlate_body, groups, inputs, scale),...  32.6 us
    pallas_call x1, Pallas kernels, channelize(): pl.pallas_call(functools.partial(channelizer_body, widths), grid=(frames...  31 us
  transfers between devices with their start and end apart: 71, of which 20 were waited for; matrix products, arithmetic and copies ran while one was open for 3% of the time, Pallas kernels for 9%

profile of v1, /device:TPU:0, one launch (start us, length us, event | category | flops | bytes accessed | tf_op | source)
XLA Modules:
  0.0 358.0 jit_solution(12136733384409568373)
XLA Ops:
  0.9 4.9 %collective-permute-start = (bf16[3,64,512]{2,1,0:T(8,128)(2,1)S(1)}, bf16[3,64,512]{2,1,0:T(8,128)(2,1)S(1)}, u32[]{:S(2)}, u32[]{:S(2)}) collective-permute-start(bf16[3,64,512]{2,1,0:T(8,128)(2,1)S(1)} %slice.171), channel_id=1, source_target_pairs={{0,1},{1,2},{2,3},{4,5},{5,6},{6,7},{8,9},{9,10},{10,11},{12,13},{... | collective-permute-start | bytes 589832 | tf_op jit(solution)/shard_map/ppermute | solution.py:252
  10.7 31.0 %channelizer.1 = (bf16[2,128,128]{2,1,0:T(8,128)(2,1)S(1)}, bf16[2,128,128]{2,1,0:T(8,128)(2,1)S(1)}, bf16[2,128,128]{2,1,0:T(8,128)(2,1)S(1)}, bf16[2,128,128]{...) custom-call(bf16[256,64,512]{2,1,0:T(8,128)(2,1)} %x_ref.1, ...), custom_call_target="tpu_custom_call" | custom-call | flops 4294967296 | bytes 25165824 | tf_op jit(solution)/shard_map/channelizer/pallas_call | solution.py:100
  43.6 1.5 collective-permute-start.2
  45.5 1.5 collective-permute-start.4
  48.9 1.8 collective-permute-start.12
  52.0 1.9 collective-permute-start.6
  55.2 4.2 %collective-permute-done.6.rest_6_ = bf16[2,128,128]{2,1,0:T(8,128)(2,1)S(1)} collective-permute-done((bf16[2,128,128]{2,1,0:T(8,128)(2,1)S(1)}, bf16[2,128,128]{2,1,0:T(8,128)(2,1)S(1)}, u32[]{:S(2)}, u32[]{:S(2)}) %collective-permute-start.6) | collective-permute-done | bytes 65568 | tf_op jit(solution)/shard_map/ppermute | solution.py:270
  62.8 2.2 collective-permute-start.16
  67.9 2.1 collective-permute-start.52
  70.0 3.2 collective-permute-done.15.rest_5_
  73.9 2.2 collective-permute-start.53
  80.6 2.6 collective-permute-start.57
  84.9 4.2 %collective-permute-done.55.rest_5_ = bf16[4,128,128]{2,1,0:T(8,128)(2,1)S(1)} collective-permute-done((bf16[4,128,128]{2,1,0:T(8,128)(2,1)S(1)}, bf16[4,128,128]{2,1,0:T(8,128)(2,1)S(1)}, u32[]{:S(2)}, u32[]{:S(2)}) %collective-permute-start.55) | collective-permute-done | bytes 131104 | tf_op jit(solution)/shard_map/ppermute | solution.py:270
  89.7 1.7 collective-permute-start.63
  94.0 1.9 collective-permute-start.22
  99.4 1.5 collective-permute-start.67
  102.4 3.1 collective-permute-done.66.rest_6_
  108.1 1.8 collective-permute-start.25
  109.9 1.7 collective-permute-start.26
  118.3 2.2 correlate.7
  120.5 5.1 %collective-permute-start.8 = (bf16[3,1,128,512]{3,2,1,0:T(8,128)(2,1)S(1)}, bf16[3,1,128,512]{3,2,1,0:T(8,128)(2,1)}, u32[]{:S(2)}, u32[]{:S(2)}) collective-permute-start(bf16[3,1,128,512]{3,2,1,0:T(8,128)(2,1)S(1)} %get-tuple-element.84), channel_id=1, source_target_pairs={{0,1},{3,2},{4,5},{7,6},{8,9},{11,10},{12,13},{15,14},{16,17},{19,... | collective-permute-start | bytes 1179656 | tf_op jit(solution)/shard_map/ppermute | solution.py:231
  133.0 3.9 %correlate.8 = (bf16[3,2,128,512]{3,2,1,0:T(8,128)(2,1)S(1)}, f32[2,128,512]{2,1,0:T(8,128)S(1)}) custom-call(s32[2]{0:T(128)S(1)} %pad_add_fusion.where_ref, bf16[4,128,128]{2,1,0:T(8,128)(2,1)S(1)} %copy-done.4, bf16[4,128,128]{2,1,0:T(8,128)(2,1)S(1)} %copy-done.6, bf16[4,128,128]{2,1,0:T(8,128)(2,1)S(1)} %copy-done.8, ...), custom_call_target="tpu_custom_call" | custom-call | flops 1073741824 | bytes 2359296 | tf_op jit(solution)/shard_map/correlate/pallas_call | solution.py:185
  139.9 3.9 %correlate.12 = (bf16[3,2,128,512]{3,2,1,0:T(8,128)(2,1)S(1)}, f32[2,128,512]{2,1,0:T(8,128)S(1)}) custom-call(s32[2]{0:T(128)S(1)} %pad_add_fusion.where_ref, bf16[4,128,128]{2,1,0:T(8,128)(2,1)S(1)} %copy-done.2, bf16[4,128,128]{2,1,0:T(8,128)(2,1)S(1)} %copy-done.12, bf16[4,128,128]{2,1,0:T(8,128)(2,1)S(1)} %copy-done.14, ...), custom_call_target="tpu_custom_call" | custom-call | flops 1073741824 | bytes 2359296 | tf_op jit(solution)/shard_map/correlate/pallas_call | solution.py:185
  144.0 4.8 %correlate.13 = (bf16[3,2,128,512]{3,2,1,0:T(8,128)(2,1)S(1)}, f32[2,128,512]{2,1,0:T(8,128)S(1)}) custom-call(s32[2]{0:T(128)S(1)} %pad_add_fusion.where_ref, bf16[4,128,128]{2,1,0:T(8,128)(2,1)S(1)} %get-tuple-element.135.rest_0_, bf16[4,128,128]{2,1,0:T(8,128)(2,1)S(1)} %copy-done.34, bf16[4,128,128]{2,1,0:T(8,128)(2,1)S(1)} %copy-done.36, ...), custom_call_target="tpu_custom_call" | custom-call | flops 1073741824 | bytes 2359296 | tf_op jit(solution)/shard_map/correlate/pallas_call | solution.py:185
  150.9 1.7 collective-permute-start.36
  155.1 9.9 %collective-permute-done.34.rest_4_ = bf16[6,128,128]{2,1,0:T(8,128)(2,1)S(1)} collective-permute-done((bf16[6,128,128]{2,1,0:T(8,128)(2,1)S(1)}, bf16[6,128,128]{2,1,0:T(8,128)(2,1)S(1)}, u32[]{:S(2)}, u32[]{:S(2)}) %collective-permute-start.34) | collective-permute-done | bytes 196640 | tf_op jit(solution)/shard_map/ppermute | solution.py:270
  165.0 1.7 collective-permute-start.42
  166.7 2.0 collective-permute-done.35.rest_5_
  171.0 2.2 collective-permute-start.18
  173.9 6.5 %correlate.9 = (bf16[3,3,128,512]{3,2,1,0:T(8,128)(2,1)S(1)}, f32[3,128,512]{2,1,0:T(8,128)S(1)}) custom-call(s32[2]{0:T(128)S(1)} %pad_add_fusion.where_ref, bf16[6,128,128]{2,1,0:T(8,128)(2,1)S(1)} %get-tuple-element.95.rest_0_, bf16[6,128,128]{2,1,0:T(8,128)(2,1)S(1)} %collective-permute-done.21.rest_1_, ...), custom_call_target="tpu_custom_call" | custom-call | flops 1610612736 | bytes 3538944 | tf_op jit(solution)/shard_map/correlate/pallas_call | solution.py:185
  180.4 5.6 %correlate.10 = (bf16[3,3,128,512]{3,2,1,0:T(8,128)(2,1)S(1)}, f32[3,128,512]{2,1,0:T(8,128)S(1)}) custom-call(s32[2]{0:T(128)S(1)} %pad_add_fusion.where_ref, bf16[6,128,128]{2,1,0:T(8,128)(2,1)S(1)} %get-tuple-element.105.rest_0_, bf16[6,128,128]{2,1,0:T(8,128)(2,1)S(1)} %collective-permute-done.31.rest_1_, ...), custom_call_target="tpu_custom_call" | custom-call | flops 1610612736 | bytes 3538944 | tf_op jit(solution)/shard_map/correlate/pallas_call | solution.py:185
  187.4 2.2 collective-permute-start.47
  189.7 3.0 collective-permute-start.58
  192.8 8.9 %collective-permute-done.45.rest_5_ = bf16[6,128,128]{2,1,0:T(8,128)(2,1)S(1)} collective-permute-done((bf16[6,128,128]{2,1,0:T(8,128)(2,1)S(1)}, bf16[6,128,128]{2,1,0:T(8,128)(2,1)S(1)}, u32[]{:S(2)}, u32[]{:S(2)}) %collective-permute-start.45) | collective-permute-done | bytes 196640 | tf_op jit(solution)/shard_map/ppermute | solution.py:270
  201.7 2.8 collective-permute-start.68
  207.2 5.6 %correlate.11 = (bf16[3,3,128,512]{3,2,1,0:T(8,128)(2,1)S(1)}, f32[3,128,512]{2,1,0:T(8,128)S(1)}) custom-call(s32[2]{0:T(128)S(1)} %pad_add_fusion.where_ref, bf16[6,128,128]{2,1,0:T(8,128)(2,1)S(1)} %copy-done, bf16[6,128,128]{2,1,0:T(8,128)(2,1)S(1)} %collective-permute-done.41.rest_1_, bf16[6,128,128]{2,1,0:T(8,128)(2,1)S(1)} %collective-permute-done.42.rest_2_, ...), custom_call_target="tpu_custom_call" | custom-call | flops 1610612736 | bytes 3538944 | tf_op jit(solution)/shard_map/correlate/pallas_call | solution.py:185
  213.0 4.4 %collective-permute-start.38 = (bf16[3,3,128,512]{3,2,1,0:T(8,128)(2,1)S(1)}, bf16[3,3,128,512]{3,2,1,0:T(8,128)(2,1)S(1)}, u32[]{:S(2)}, u32[]{:S(2)}) collective-permute-start(bf16[3,3,128,512]{3,2,1,0:T(8,128)(2,1)S(1)} %get-tuple-element.114), channel_id=1, source_target_pairs={{0,1},{3,2},{4,5},{7,6},{8,9},{11,10},{12,13},{15,14},{16,17},{19,... | collective-permute-start | bytes 3538952 | tf_op jit(solution)/shard_map/ppermute | solution.py:231
  218.5 1.6 collective-permute-start.48
  220.1 1.5 fusion.6
  222.5 5.0 %collective-permute-done.68 = bf16[3,2,128,512]{3,2,1,0:T(8,128)(2,1)S(1)} collective-permute-done((bf16[3,2,128,512]{3,2,1,0:T(8,128)(2,1)S(1)}, bf16[3,2,128,512]{3,2,1,0:T(8,128)(2,1)S(1)}, u32[]{:S(2)}, u32[]{:S(2)}) %collective-permute-start.68) | collective-permute-done | bytes 786464 | tf_op jit(solution)/shard_map/ppermute | solution.py:231
  228.4 24.4 %collective-permute-done.28 = bf16[3,3,128,512]{3,2,1,0:T(8,128)(2,1)S(1)} collective-permute-done((bf16[3,3,128,512]{3,2,1,0:T(8,128)(2,1)S(1)}, bf16[3,3,128,512]{3,2,1,0:T(8,128)(2,1)S(1)}, u32[]{:S(2)}, u32[]{:S(2)}) %collective-permute-start.28) | collective-permute-done | bytes 1179680 | tf_op jit(solution)/shard_map/ppermute | solution.py:231
  253.9 24.2 %collective-permute-done.38 = bf16[3,3,128,512]{3,2,1,0:T(8,128)(2,1)S(1)} collective-permute-done((bf16[3,3,128,512]{3,2,1,0:T(8,128)(2,1)S(1)}, bf16[3,3,128,512]{3,2,1,0:T(8,128)(2,1)S(1)}, u32[]{:S(2)}, u32[]{:S(2)}) %collective-permute-start.38) | collective-permute-done | bytes 1179680 | tf_op jit(solution)/shard_map/ppermute | solution.py:231
  279.2 22.7 %collective-permute-done.48 = bf16[3,3,128,512]{3,2,1,0:T(8,128)(2,1)S(1)} collective-permute-done((bf16[3,3,128,512]{3,2,1,0:T(8,128)(2,1)S(1)}, bf16[3,3,128,512]{3,2,1,0:T(8,128)(2,1)S(1)}, u32[]{:S(2)}, u32[]{:S(2)}) %collective-permute-start.48) | collective-permute-done | bytes 1179680 | tf_op jit(solution)/shard_map/ppermute | solution.py:231
  306.7 12.5 %collective-permute-done.20 = bf16[1,2,128,512]{3,2,1,0:T(8,128)(2,1)S(1)} collective-permute-done((bf16[1,2,128,512]{3,2,1,0:T(8,128)(2,1)S(1)}, bf16[1,2,128,512]{3,2,1,0:T(8,128)(2,1)S(1)}, u32[]{:S(2)}, u32[]{:S(2)}) %collective-permute-start.20) | collective-permute-done | bytes 262176 | tf_op jit(solution)/shard_map/ppermute | solution.py:231
  326.2 12.7 %collective-permute-done.30 = bf16[1,3,128,512]{3,2,1,0:T(8,128)(2,1)S(1)} collective-permute-done((bf16[1,3,128,512]{3,2,1,0:T(8,128)(2,1)S(1)}, bf16[1,3,128,512]{3,2,1,0:T(8,128)(2,1)S(1)}, u32[]{:S(2)}, u32[]{:S(2)}) %collective-permute-start.30) | collective-permute-done | bytes 393248 | tf_op jit(solution)/shard_map/ppermute | solution.py:231
  339.1 8.2 %collective-permute-done.40 = bf16[1,3,128,512]{3,2,1,0:T(8,128)(2,1)S(1)} collective-permute-done((bf16[1,3,128,512]{3,2,1,0:T(8,128)(2,1)S(1)}, bf16[1,3,128,512]{3,2,1,0:T(8,128)(2,1)S(1)}, u32[]{:S(2)}, u32[]{:S(2)}) %collective-permute-start.40) | collective-permute-done | bytes 393248 | tf_op jit(solution)/shard_map/ppermute | solution.py:231
  347.5 5.5 %collective-permute-done.50 = bf16[1,3,128,512]{3,2,1,0:T(8,128)(2,1)S(1)} collective-permute-done((bf16[1,3,128,512]{3,2,1,0:T(8,128)(2,1)S(1)}, bf16[1,3,128,512]{3,2,1,0:T(8,128)(2,1)S(1)}, u32[]{:S(2)}, u32[]{:S(2)}) %collective-permute-start.50) | collective-permute-done | bytes 393248 | tf_op jit(solution)/shard_map/ppermute | solution.py:231
  353.6 4.4 %copy.4 = f32[128,16,512]{2,1,0:T(8,128)} copy(f32[128,16,512]{2,0,1:T(8,128)S(1)} %bitcast.74) | data formatting | bytes 8388608 | tf_op jit(solution)/shard_map/transpose | solution.py:273
  (298 shorter events, 82.4 us)
Async XLA Ops:
  47.8 14.4 %collective-permute-start.11 = (bf16[4,128,128]{2,1,0:T(8,128)(2,1)S(1)}, bf16[4,128,128]{2,1,0:T(8,128)(2,1)S(1)}, u32[]{:S(2)}, u32[]{:S(2)}) collective-permute-start(bf16[4,128,128]{2,1,0:T(8,128)(2,1)S(1)} %get-tuple-element.86), channel_id=1, source_target_pairs={{0,4},{4,0},{8,12},{12,8},{16,20},{20,16},{24,28},{28,24},{1,5},{5... | collective-permute-start | bytes 393224 | tf_op jit(solution)/shard_map/ppermute | solution.py:270
  48.9 16.2 %collective-permute-start.12 = (bf16[4,128,128]{2,1,0:T(8,128)(2,1)S(1)}, bf16[4,128,128]{2,1,0:T(8,128)(2,1)S(1)}, u32[]{:S(2)}, u32[]{:S(2)}) collective-permute-start(bf16[4,128,128]{2,1,0:T(8,128)(2,1)S(1)} %get-tuple-element.87), channel_id=1, source_target_pairs={{0,8},{4,12},{8,0},{12,4},{16,24},{20,28},{24,16},{28,20},{1,9},{5... | collective-permute-start | bytes 393224 | tf_op jit(solution)/shard_map/ppermute | solution.py:270
  51.3 15.2 %collective-permute-start.13 = (bf16[4,128,128]{2,1,0:T(8,128)(2,1)S(1)}, bf16[4,128,128]{2,1,0:T(8,128)(2,1)S(1)}, u32[]{:S(2)}, u32[]{:S(2)}) collective-permute-start(bf16[4,128,128]{2,1,0:T(8,128)(2,1)S(1)} %get-tuple-element.88), channel_id=1, source_target_pairs={{0,12},{4,8},{8,4},{12,0},{16,28},{20,24},{24,20},{28,16},{1,13},{... | collective-permute-start | bytes 393224 | tf_op jit(solution)/shard_map/ppermute | solution.py:270
  62.8 13.3 %collective-permute-start.16 = (bf16[4,128,128]{2,1,0:T(8,128)(2,1)S(1)}, bf16[4,128,128]{2,1,0:T(8,128)(2,1)S(1)}, u32[]{:S(2)}, u32[]{:S(2)}) collective-permute-start(bf16[4,128,128]{2,1,0:T(8,128)(2,1)S(1)} %get-tuple-element.91), channel_id=1, source_target_pairs={{0,24},{4,28},{8,16},{12,20},{16,8},{20,12},{24,0},{28,4},{1,25},{... | collective-permute-start | bytes 393224 | tf_op jit(solution)/shard_map/ppermute | solution.py:270
  67.9 12.0 %collective-permute-start.52 = (bf16[4,128,128]{2,1,0:T(8,128)(2,1)S(1)}, bf16[4,128,128]{2,1,0:T(8,128)(2,1)S(1)}, u32[]{:S(2)}, u32[]{:S(2)}) collective-permute-start(bf16[4,128,128]{2,1,0:T(8,128)(2,1)S(1)} %get-tuple-element.127), channel_id=1, source_target_pairs={{0,8},{4,12},{8,0},{12,4},{16,24},{20,28},{24,16},{28,20},{1,9},{5... | collective-permute-start | bytes 393224 | tf_op jit(solution)/shard_map/ppermute | solution.py:270
  78.9 12.4 %collective-permute-start.56 = (bf16[4,128,128]{2,1,0:T(8,128)(2,1)S(1)}, bf16[4,128,128]{2,1,0:T(8,128)(2,1)S(1)}, u32[]{:S(2)}, u32[]{:S(2)}) collective-permute-start(bf16[4,128,128]{2,1,0:T(8,128)(2,1)S(1)} %get-tuple-element.131), channel_id=1, source_target_pairs={{0,24},{4,28},{8,16},{12,20},{16,8},{20,12},{24,0},{28,4},{1,25},{... | collective-permute-start | bytes 393224 | tf_op jit(solution)/shard_map/ppermute | solution.py:270
  80.6 11.9 %collective-permute-start.57 = (bf16[4,128,128]{2,1,0:T(8,128)(2,1)S(1)}, bf16[4,128,128]{2,1,0:T(8,128)(2,1)S(1)}, u32[]{:S(2)}, u32[]{:S(2)}) collective-permute-start(bf16[4,128,128]{2,1,0:T(8,128)(2,1)S(1)} %get-tuple-element.132), channel_id=1, source_target_pairs={{0,28},{4,24},{8,20},{12,16},{16,12},{20,8},{24,4},{28,0},{1,29},{... | collective-permute-start | bytes 393224 | tf_op jit(solution)/shard_map/ppermute | solution.py:270
  93.2 16.7 %collective-permute-start.21 = (bf16[6,128,128]{2,1,0:T(8,128)(2,1)S(1)}, bf16[6,128,128]{2,1,0:T(8,128)(2,1)S(1)}, u32[]{:S(2)}, u32[]{:S(2)}) collective-permute-start(bf16[6,128,128]{2,1,0:T(8,128)(2,1)S(1)} %get-tuple-element.96), channel_id=1, source_target_pairs={{0,4},{4,0},{8,12},{12,8},{16,20},{20,16},{24,28},{28,24},{1,5},{5... | collective-permute-start | bytes 589832 | tf_op jit(solution)/shard_map/ppermute | solution.py:270
  94.0 26.5 %collective-permute-start.22 = (bf16[6,128,128]{2,1,0:T(8,128)(2,1)S(1)}, bf16[6,128,128]{2,1,0:T(8,128)(2,1)S(1)}, u32[]{:S(2)}, u32[]{:S(2)}) collective-permute-start(bf16[6,128,128]{2,1,0:T(8,128)(2,1)S(1)} %get-tuple-element.97), channel_id=1, source_target_pairs={{0,8},{4,12},{8,0},{12,4},{16,24},{20,28},{24,16},{28,20},{1,9},{5... | collective-permute-start | bytes 589832 | tf_op jit(solution)/shard_map/ppermute | solution.py:270
  102.4 34.5 %collective-permute-start.23 = (bf16[6,128,128]{2,1,0:T(8,128)(2,1)S(1)}, bf16[6,128,128]{2,1,0:T(8,128)(2,1)S(1)}, u32[]{:S(2)}, u32[]{:S(2)}) collective-permute-start(bf16[6,128,128]{2,1,0:T(8,128)(2,1)S(1)} %get-tuple-element.98), channel_id=1, source_target_pairs={{0,12},{4,8},{8,4},{12,0},{16,28},{20,24},{24,20},{28,16},{1,13},{... | collective-permute-start | bytes 589832 | tf_op jit(solution)/shard_map/ppermute | solution.py:270
  105.5 31.5 %collective-permute-start.24 = (bf16[6,128,128]{2,1,0:T(8,128)(2,1)S(1)}, bf16[6,128,128]{2,1,0:T(8,128)(2,1)}, u32[]{:S(2)}, u32[]{:S(2)}) collective-permute-start(bf16[6,128,128]{2,1,0:T(8,128)(2,1)S(1)} %get-tuple-element.99), channel_id=1, source_target_pairs={{0,16},{4,20},{8,24},{12,28},{16,0},{20,4},{24,8},{28,12},{1,17},{... | collective-permute-start | bytes 589832 | tf_op jit(solution)/shard_map/ppermute | solution.py:270
  108.1 30.2 %collective-permute-start.25 = (bf16[6,128,128]{2,1,0:T(8,128)(2,1)S(1)}, bf16[6,128,128]{2,1,0:T(8,128)(2,1)}, u32[]{:S(2)}, u32[]{:S(2)}) collective-permute-start(bf16[6,128,128]{2,1,0:T(8,128)(2,1)S(1)} %get-tuple-element.100), channel_id=1, source_target_pairs={{0,20},{4,16},{8,28},{12,24},{16,4},{20,0},{24,12},{28,8},{1,21},{... | collective-permute-start | bytes 589832 | tf_op jit(solution)/shard_map/ppermute | solution.py:270
  109.9 29.9 %collective-permute-start.26 = (bf16[6,128,128]{2,1,0:T(8,128)(2,1)S(1)}, bf16[6,128,128]{2,1,0:T(8,128)(2,1)}, u32[]{:S(2)}, u32[]{:S(2)}) collective-permute-start(bf16[6,128,128]{2,1,0:T(8,128)(2,1)S(1)} %get-tuple-element.101), channel_id=1, source_target_pairs={{0,24},{4,28},{8,16},{12,20},{16,8},{20,12},{24,0},{28,4},{1,25},{... | collective-permute-start | bytes 589832 | tf_op jit(solution)/shard_map/ppermute | solution.py:270
  120.5 32.8 %collective-permute-start.8 = (bf16[3,1,128,512]{3,2,1,0:T(8,128)(2,1)S(1)}, bf16[3,1,128,512]{3,2,1,0:T(8,128)(2,1)}, u32[]{:S(2)}, u32[]{:S(2)}) collective-permute-start(bf16[3,1,128,512]{3,2,1,0:T(8,128)(2,1)S(1)} %get-tuple-element.84), channel_id=1, source_target_pairs={{0,1},{3,2},{4,5},{7,6},{8,9},{11,10},{12,13},{15,14},{16,17},{19,... | collective-permute-start | bytes 1179656 | tf_op jit(solution)/shard_map/ppermute | solution.py:231
  136.9 11.9 %collective-permute-start.27 = (bf16[6,128,128]{2,1,0:T(8,128)(2,1)S(1)}, bf16[6,128,128]{2,1,0:T(8,128)(2,1)S(1)}, u32[]{:S(2)}, u32[]{:S(2)}) collective-permute-start(bf16[6,128,128]{2,1,0:T(8,128)(2,1)S(1)} %get-tuple-element.102), channel_id=1, source_target_pairs={{0,28},{4,24},{8,20},{12,16},{16,12},{20,8},{24,4},{28,0},{1,29},{... | collective-permute-start | bytes 589832 | tf_op jit(solution)/shard_map/ppermute | solution.py:270
  137.0 12.7 %collective-permute-start.31 = (bf16[6,128,128]{2,1,0:T(8,128)(2,1)S(1)}, bf16[6,128,128]{2,1,0:T(8,128)(2,1)S(1)}, u32[]{:S(2)}, u32[]{:S(2)}) collective-permute-start(bf16[6,128,128]{2,1,0:T(8,128)(2,1)S(1)} %get-tuple-element.106), channel_id=1, source_target_pairs={{0,4},{4,0},{8,12},{12,8},{16,20},{20,16},{24,28},{28,24},{1,5},{5... | collective-permute-start | bytes 589832 | tf_op jit(solution)/shard_map/ppermute | solution.py:270
  138.3 12.6 %collective-permute-start.32 = (bf16[6,128,128]{2,1,0:T(8,128)(2,1)S(1)}, bf16[6,128,128]{2,1,0:T(8,128)(2,1)S(1)}, u32[]{:S(2)}, u32[]{:S(2)}) collective-permute-start(bf16[6,128,128]{2,1,0:T(8,128)(2,1)S(1)} %get-tuple-element.107), channel_id=1, source_target_pairs={{0,8},{4,12},{8,0},{12,4},{16,24},{20,28},{24,16},{28,20},{1,9},{5... | collective-permute-start | bytes 589832 | tf_op jit(solution)/shard_map/ppermute | solution.py:270
  139.7 12.9 %collective-permute-start.33 = (bf16[6,128,128]{2,1,0:T(8,128)(2,1)S(1)}, bf16[6,128,128]{2,1,0:T(8,128)(2,1)S(1)}, u32[]{:S(2)}, u32[]{:S(2)}) collective-permute-start(bf16[6,128,128]{2,1,0:T(8,128)(2,1)S(1)} %get-tuple-element.108), channel_id=1, source_target_pairs={{0,12},{4,8},{8,4},{12,0},{16,28},{20,24},{24,20},{28,16},{1,13},{... | collective-permute-start | bytes 589832 | tf_op jit(solution)/shard_map/ppermute | solution.py:270
  148.8 16.2 %collective-permute-start.34 = (bf16[6,128,128]{2,1,0:T(8,128)(2,1)S(1)}, bf16[6,128,128]{2,1,0:T(8,128)(2,1)S(1)}, u32[]{:S(2)}, u32[]{:S(2)}) collective-permute-start(bf16[6,128,128]{2,1,0:T(8,128)(2,1)S(1)} %copy-done.70), channel_id=1, source_target_pairs={{0,16},{4,20},{8,24},{12,28},{16,0},{20,4},{24,8},{28,12},{1,17},{... | collective-permute-start | bytes 589832 | tf_op jit(solution)/shard_map/ppermute | solution.py:270
  149.7 19.0 %collective-permute-start.35 = (bf16[6,128,128]{2,1,0:T(8,128)(2,1)S(1)}, bf16[6,128,128]{2,1,0:T(8,128)(2,1)S(1)}, u32[]{:S(2)}, u32[]{:S(2)}) collective-permute-start(bf16[6,128,128]{2,1,0:T(8,128)(2,1)S(1)} %copy-done.69), channel_id=1, source_target_pairs={{0,20},{4,16},{8,28},{12,24},{16,4},{20,0},{24,12},{28,8},{1,21},{... | collective-permute-start | bytes 589832 | tf_op jit(solution)/shard_map/ppermute | solution.py:270
  150.9 19.2 %collective-permute-start.36 = (bf16[6,128,128]{2,1,0:T(8,128)(2,1)S(1)}, bf16[6,128,128]{2,1,0:T(8,128)(2,1)S(1)}, u32[]{:S(2)}, u32[]{:S(2)}) collective-permute-start(bf16[6,128,128]{2,1,0:T(8,128)(2,1)S(1)} %copy-done.68), channel_id=1, source_target_pairs={{0,24},{4,28},{8,16},{12,20},{16,8},{20,12},{24,0},{28,4},{1,25},{... | collective-permute-start | bytes 589832 | tf_op jit(solution)/shard_map/ppermute | solution.py:270
  152.6 18.4 %collective-permute-start.37 = (bf16[6,128,128]{2,1,0:T(8,128)(2,1)S(1)}, bf16[6,128,128]{2,1,0:T(8,128)(2,1)S(1)}, u32[]{:S(2)}, u32[]{:S(2)}) collective-permute-start(bf16[6,128,128]{2,1,0:T(8,128)(2,1)S(1)} %copy-done.67), channel_id=1, source_target_pairs={{0,28},{4,24},{8,20},{12,16},{16,12},{20,8},{24,4},{28,0},{1,29},{... | collective-permute-start | bytes 589832 | tf_op jit(solution)/shard_map/ppermute | solution.py:270
  153.3 19.8 %collective-permute-start.41 = (bf16[6,128,128]{2,1,0:T(8,128)(2,1)S(1)}, bf16[6,128,128]{2,1,0:T(8,128)(2,1)S(1)}, u32[]{:S(2)}, u32[]{:S(2)}) collective-permute-start(bf16[6,128,128]{2,1,0:T(8,128)(2,1)S(1)} %copy-done.66), channel_id=1, source_target_pairs={{0,4},{4,0},{8,12},{12,8},{16,20},{20,16},{24,28},{28,24},{1,5},{5... | collective-permute-start | bytes 589832 | tf_op jit(solution)/shard_map/ppermute | solution.py:270
  165.0 21.0 %collective-permute-start.42 = (bf16[6,128,128]{2,1,0:T(8,128)(2,1)S(1)}, bf16[6,128,128]{2,1,0:T(8,128)(2,1)S(1)}, u32[]{:S(2)}, u32[]{:S(2)}) collective-permute-start(bf16[6,128,128]{2,1,0:T(8,128)(2,1)S(1)} %copy-done.65), channel_id=1, source_target_pairs={{0,8},{4,12},{8,0},{12,4},{16,24},{20,28},{24,16},{28,20},{1,9},{5... | collective-permute-start | bytes 589832 | tf_op jit(solution)/shard_map/ppermute | solution.py:270
  168.7 17.8 %collective-permute-start.43 = (bf16[6,128,128]{2,1,0:T(8,128)(2,1)S(1)}, bf16[6,128,128]{2,1,0:T(8,128)(2,1)S(1)}, u32[]{:S(2)}, u32[]{:S(2)}) collective-permute-start(bf16[6,128,128]{2,1,0:T(8,128)(2,1)S(1)} %copy-done.64), channel_id=1, source_target_pairs={{0,12},{4,8},{8,4},{12,0},{16,28},{20,24},{24,20},{28,16},{1,13},{... | collective-permute-start | bytes 589832 | tf_op jit(solution)/shard_map/ppermute | solution.py:270
  170.1 17.3 %collective-permute-start.44 = (bf16[6,128,128]{2,1,0:T(8,128)(2,1)S(1)}, bf16[6,128,128]{2,1,0:T(8,128)(2,1)S(1)}, u32[]{:S(2)}, u32[]{:S(2)}) collective-permute-start(bf16[6,128,128]{2,1,0:T(8,128)(2,1)S(1)} %copy-done.63), channel_id=1, source_target_pairs={{0,16},{4,20},{8,24},{12,28},{16,0},{20,4},{24,8},{28,12},{1,17},{... | collective-permute-start | bytes 589832 | tf_op jit(solution)/shard_map/ppermute | solution.py:270
  171.0 47.5 %collective-permute-start.18 = (bf16[3,2,128,512]{3,2,1,0:T(8,128)(2,1)S(1)}, bf16[3,2,128,512]{3,2,1,0:T(8,128)(2,1)}, u32[]{:S(2)}, u32[]{:S(2)}) collective-permute-start(bf16[3,2,128,512]{3,2,1,0:T(8,128)(2,1)S(1)} %get-tuple-element.94), channel_id=1, source_target_pairs={{0,1},{3,2},{4,5},{7,6},{8,9},{11,10},{12,13},{15,14},{16,17},{19,... | collective-permute-start | bytes 2359304 | tf_op jit(solution)/shard_map/ppermute | solution.py:231
  173.2 16.5 %collective-permute-start.9 = (bf16[2,1,128,512]{3,2,1,0:T(8,128)(2,1)S(1)}, bf16[2,1,128,512]{3,2,1,0:T(8,128)(2,1)S(1)}, u32[]{:S(2)}, u32[]{:S(2)}) collective-permute-start(bf16[2,1,128,512]{3,2,1,0:T(8,128)(2,1)S(1)} %fusion.18), channel_id=1, source_target_pairs={{1,2},{2,1},{5,6},{6,5},{9,10},{10,9},{13,14},{14,13},{17,18},{18,... | collective-permute-start | bytes 786440 | tf_op jit(solution)/shard_map/ppermute | solution.py:231
  186.1 15.6 %collective-permute-start.45 = (bf16[6,128,128]{2,1,0:T(8,128)(2,1)S(1)}, bf16[6,128,128]{2,1,0:T(8,128)(2,1)S(1)}, u32[]{:S(2)}, u32[]{:S(2)}) collective-permute-start(bf16[6,128,128]{2,1,0:T(8,128)(2,1)S(1)} %copy-done.62), channel_id=1, source_target_pairs={{0,20},{4,16},{8,28},{12,24},{16,4},{20,0},{24,12},{28,8},{1,21},{... | collective-permute-start | bytes 589832 | tf_op jit(solution)/shard_map/ppermute | solution.py:270
  186.5 18.0 %collective-permute-start.46 = (bf16[6,128,128]{2,1,0:T(8,128)(2,1)S(1)}, bf16[6,128,128]{2,1,0:T(8,128)(2,1)S(1)}, u32[]{:S(2)}, u32[]{:S(2)}) collective-permute-start(bf16[6,128,128]{2,1,0:T(8,128)(2,1)S(1)} %copy-done.61), channel_id=1, source_target_pairs={{0,24},{4,28},{8,16},{12,20},{16,8},{20,12},{24,0},{28,4},{1,25},{... | collective-permute-start | bytes 589832 | tf_op jit(solution)/shard_map/ppermute | solution.py:270
  187.4 18.4 %collective-permute-start.47 = (bf16[6,128,128]{2,1,0:T(8,128)(2,1)S(1)}, bf16[6,128,128]{2,1,0:T(8,128)(2,1)S(1)}, u32[]{:S(2)}, u32[]{:S(2)}) collective-permute-start(bf16[6,128,128]{2,1,0:T(8,128)(2,1)S(1)} %copy-done.60), channel_id=1, source_target_pairs={{0,28},{4,24},{8,20},{12,16},{16,12},{20,8},{24,4},{28,0},{1,29},{... | collective-permute-start | bytes 589832 | tf_op jit(solution)/shard_map/ppermute | solution.py:270
  189.7 31.9 %collective-permute-start.58 = (bf16[3,2,128,512]{3,2,1,0:T(8,128)(2,1)S(1)}, bf16[3,2,128,512]{3,2,1,0:T(8,128)(2,1)S(1)}, u32[]{:S(2)}, u32[]{:S(2)}) collective-permute-start(bf16[3,2,128,512]{3,2,1,0:T(8,128)(2,1)S(1)} %get-tuple-element.134), channel_id=1, source_target_pairs={{0,1},{3,2},{4,5},{7,6},{8,9},{11,10},{12,13},{15,14},{16,17},{19,... | collective-permute-start | bytes 2359304 | tf_op jit(solution)/shard_map/ppermute | solution.py:231
  201.7 25.8 %collective-permute-start.68 = (bf16[3,2,128,512]{3,2,1,0:T(8,128)(2,1)S(1)}, bf16[3,2,128,512]{3,2,1,0:T(8,128)(2,1)S(1)}, u32[]{:S(2)}, u32[]{:S(2)}) collective-permute-start(bf16[3,2,128,512]{3,2,1,0:T(8,128)(2,1)S(1)} %get-tuple-element.144), channel_id=1, source_target_pairs={{0,1},{3,2},{4,5},{7,6},{8,9},{11,10},{12,13},{15,14},{16,17},{19,... | collective-permute-start | bytes 2359304 | tf_op jit(solution)/shard_map/ppermute | solution.py:231
  204.5 48.3 %collective-permute-start.28 = (bf16[3,3,128,512]{3,2,1,0:T(8,128)(2,1)S(1)}, bf16[3,3,128,512]{3,2,1,0:T(8,128)(2,1)S(1)}, u32[]{:S(2)}, u32[]{:S(2)}) collective-permute-start(bf16[3,3,128,512]{3,2,1,0:T(8,128)(2,1)S(1)} %get-tuple-element.104), channel_id=1, source_target_pairs={{0,1},{3,2},{4,5},{7,6},{8,9},{11,10},{12,13},{15,14},{16,17},{19,... | collective-permute-start | bytes 3538952 | tf_op jit(solution)/shard_map/ppermute | solution.py:231
  213.0 65.0 %collective-permute-start.38 = (bf16[3,3,128,512]{3,2,1,0:T(8,128)(2,1)S(1)}, bf16[3,3,128,512]{3,2,1,0:T(8,128)(2,1)S(1)}, u32[]{:S(2)}, u32[]{:S(2)}) collective-permute-start(bf16[3,3,128,512]{3,2,1,0:T(8,128)(2,1)S(1)} %get-tuple-element.114), channel_id=1, source_target_pairs={{0,1},{3,2},{4,5},{7,6},{8,9},{11,10},{12,13},{15,14},{16,17},{19,... | collective-permute-start | bytes 3538952 | tf_op jit(solution)/shard_map/ppermute | solution.py:231
  218.5 83.4 %collective-permute-start.48 = (bf16[3,3,128,512]{3,2,1,0:T(8,128)(2,1)S(1)}, bf16[3,3,128,512]{3,2,1,0:T(8,128)(2,1)S(1)}, u32[]{:S(2)}, u32[]{:S(2)}) collective-permute-start(bf16[3,3,128,512]{3,2,1,0:T(8,128)(2,1)S(1)} %get-tuple-element.124), channel_id=1, source_target_pairs={{0,1},{3,2},{4,5},{7,6},{8,9},{11,10},{12,13},{15,14},{16,17},{19,... | collective-permute-start | bytes 3538952 | tf_op jit(solution)/shard_map/ppermute | solution.py:231
  221.5 81.4 %collective-permute-start.19 = (bf16[2,2,128,512]{3,2,1,0:T(8,128)(2,1)S(1)}, bf16[2,2,128,512]{3,2,1,0:T(8,128)(2,1)S(1)}, u32[]{:S(2)}, u32[]{:S(2)}) collective-permute-start(bf16[2,2,128,512]{3,2,1,0:T(8,128)(2,1)S(1)} %fusion.6), channel_id=1, source_target_pairs={{1,2},{2,1},{5,6},{6,5},{9,10},{10,9},{13,14},{14,13},{17,18},{18,... | collective-permute-start | bytes 1572872 | tf_op jit(solution)/shard_map/ppermute | solution.py:231
  227.5 76.3 %collective-permute-start.59 = (bf16[2,2,128,512]{3,2,1,0:T(8,128)(2,1)S(1)}, bf16[2,2,128,512]{3,2,1,0:T(8,128)(2,1)S(1)}, u32[]{:S(2)}, u32[]{:S(2)}) collective-permute-start(bf16[2,2,128,512]{3,2,1,0:T(8,128)(2,1)S(1)} %fusion.7), channel_id=1, source_target_pairs={{1,2},{2,1},{5,6},{6,5},{9,10},{10,9},{13,14},{14,13},{17,18},{18,... | collective-permute-start | bytes 1572872 | tf_op jit(solution)/shard_map/ppermute | solution.py:231
  252.8 52.5 %collective-permute-start.69 = (bf16[2,2,128,512]{3,2,1,0:T(8,128)(2,1)S(1)}, bf16[2,2,128,512]{3,2,1,0:T(8,128)(2,1)S(1)}, u32[]{:S(2)}, u32[]{:S(2)}) collective-permute-start(bf16[2,2,128,512]{3,2,1,0:T(8,128)(2,1)S(1)} %fusion.8), channel_id=1, source_target_pairs={{1,2},{2,1},{5,6},{6,5},{9,10},{10,9},{13,14},{14,13},{17,18},{18,... | collective-permute-start | bytes 1572872 | tf_op jit(solution)/shard_map/ppermute | solution.py:231
  278.1 43.6 %collective-permute-start.29 = (bf16[2,3,128,512]{3,2,1,0:T(8,128)(2,1)S(1)}, bf16[2,3,128,512]{3,2,1,0:T(8,128)(2,1)S(1)}, u32[]{:S(2)}, u32[]{:S(2)}) collective-permute-start(bf16[2,3,128,512]{3,2,1,0:T(8,128)(2,1)S(1)} %fusion), channel_id=1, source_target_pairs={{1,2},{2,1},{5,6},{6,5},{9,10},{10,9},{13,14},{14,13},{17,18},{18,... | collective-permute-start | bytes 2359304 | tf_op jit(solution)/shard_map/ppermute | solution.py:231
  301.9 21.3 %collective-permute-start.39 = (bf16[2,3,128,512]{3,2,1,0:T(8,128)(2,1)S(1)}, bf16[2,3,128,512]{3,2,1,0:T(8,128)(2,1)S(1)}, u32[]{:S(2)}, u32[]{:S(2)}) collective-permute-start(bf16[2,3,128,512]{3,2,1,0:T(8,128)(2,1)S(1)} %fusion.1), channel_id=1, source_target_pairs={{1,2},{2,1},{5,6},{6,5},{9,10},{10,9},{13,14},{14,13},{17,18},{18,... | collective-permute-start | bytes 2359304 | tf_op jit(solution)/shard_map/ppermute | solution.py:231
  303.0 21.7 %collective-permute-start.49 = (bf16[2,3,128,512]{3,2,1,0:T(8,128)(2,1)S(1)}, bf16[2,3,128,512]{3,2,1,0:T(8,128)(2,1)S(1)}, u32[]{:S(2)}, u32[]{:S(2)}) collective-permute-start(bf16[2,3,128,512]{3,2,1,0:T(8,128)(2,1)S(1)} %fusion.2), channel_id=1, source_target_pairs={{1,2},{2,1},{5,6},{6,5},{9,10},{10,9},{13,14},{14,13},{17,18},{18,... | collective-permute-start | bytes 2359304 | tf_op jit(solution)/shard_map/ppermute | solution.py:231
  303.8 15.4 %collective-permute-start.20 = (bf16[1,2,128,512]{3,2,1,0:T(8,128)(2,1)S(1)}, bf16[1,2,128,512]{3,2,1,0:T(8,128)(2,1)S(1)}, u32[]{:S(2)}, u32[]{:S(2)}) collective-permute-start(bf16[1,2,128,512]{3,2,1,0:T(8,128)(2,1)S(1)} %fusion.19), channel_id=1, source_target_pairs={{2,3},{1,0},{6,7},{5,4},{10,11},{9,8},{14,15},{13,12},{18,19},{17,... | collective-permute-start | bytes 786440 | tf_op jit(solution)/shard_map/ppermute | solution.py:231
  305.3 48.0 %collective-permute-start.60 = (bf16[1,2,128,512]{3,2,1,0:T(8,128)(2,1)S(1)}, bf16[1,2,128,512]{3,2,1,0:T(8,128)(2,1)S(1)}, u32[]{:S(2)}, u32[]{:S(2)}) collective-permute-start(bf16[1,2,128,512]{3,2,1,0:T(8,128)(2,1)S(1)} %fusion.20), channel_id=1, source_target_pairs={{2,3},{1,0},{6,7},{5,4},{10,11},{9,8},{14,15},{13,12},{18,19},{17,... | collective-permute-start | bytes 786440 | tf_op jit(solution)/shard_map/ppermute | solution.py:231
  319.2 34.2 %collective-permute-start.70 = (bf16[1,2,128,512]{3,2,1,0:T(8,128)(2,1)S(1)}, bf16[1,2,128,512]{3,2,1,0:T(8,128)(2,1)S(1)}, u32[]{:S(2)}, u32[]{:S(2)}) collective-permute-start(bf16[1,2,128,512]{3,2,1,0:T(8,128)(2,1)S(1)} %fusion.21), channel_id=1, source_target_pairs={{2,3},{1,0},{6,7},{5,4},{10,11},{9,8},{14,15},{13,12},{18,19},{17,... | collective-permute-start | bytes 786440 | tf_op jit(solution)/shard_map/ppermute | solution.py:231
  321.9 17.0 %collective-permute-start.30 = (bf16[1,3,128,512]{3,2,1,0:T(8,128)(2,1)S(1)}, bf16[1,3,128,512]{3,2,1,0:T(8,128)(2,1)S(1)}, u32[]{:S(2)}, u32[]{:S(2)}) collective-permute-start(bf16[1,3,128,512]{3,2,1,0:T(8,128)(2,1)S(1)} %fusion.12), channel_id=1, source_target_pairs={{2,3},{1,0},{6,7},{5,4},{10,11},{9,8},{14,15},{13,12},{18,19},{17,... | collective-permute-start | bytes 1179656 | tf_op jit(solution)/shard_map/ppermute | solution.py:231
  323.4 23.9 %collective-permute-start.40 = (bf16[1,3,128,512]{3,2,1,0:T(8,128)(2,1)S(1)}, bf16[1,3,128,512]{3,2,1,0:T(8,128)(2,1)S(1)}, u32[]{:S(2)}, u32[]{:S(2)}) collective-permute-start(bf16[1,3,128,512]{3,2,1,0:T(8,128)(2,1)S(1)} %fusion.13), channel_id=1, source_target_pairs={{2,3},{1,0},{6,7},{5,4},{10,11},{9,8},{14,15},{13,12},{18,19},{17,... | collective-permute-start | bytes 1179656 | tf_op jit(solution)/shard_map/ppermute | solution.py:231
  324.9 28.2 %collective-permute-start.50 = (bf16[1,3,128,512]{3,2,1,0:T(8,128)(2,1)S(1)}, bf16[1,3,128,512]{3,2,1,0:T(8,128)(2,1)S(1)}, u32[]{:S(2)}, u32[]{:S(2)}) collective-permute-start(bf16[1,3,128,512]{3,2,1,0:T(8,128)(2,1)S(1)} %fusion.14), channel_id=1, source_target_pairs={{2,3},{1,0},{6,7},{5,4},{10,11},{9,8},{14,15},{13,12},{18,19},{17,... | collective-permute-start | bytes 1179656 | tf_op jit(solution)/shard_map/ppermute | solution.py:231
  (94 other events, 444.0 us)

commit v2 on v1

v2 whole, which is shorter than its diff:
```python
import functools
import math

import jax
import jax.numpy as jnp
from jax import lax
from jax.experimental import pallas as pl
from jax.experimental.pallas import tpu as pltpu
from jax.sharding import PartitionSpec as P

CH = 128
TAPS = 4
LANES = 128
ROWS = 16
VMEM = 60 * 1024 * 1024


def chunk_sizes(count):
    if count % 16:
        return [count]
    return [4 * (count // 16), 6 * (count // 16), 6 * (count // 16)]


def in_hbm(values):
    return [pltpu.with_memory_space_constraint(v, pltpu.HBM) for v in values]


def tap_window(taps, samp_len):
    points = jnp.arange(taps * samp_len).astype(jnp.float32)
    centre = (taps * samp_len - 1) / 2.0
    shape_part = jnp.sinc((points - centre) / samp_len)
    taper = jnp.square(jnp.sin(math.pi * (points + 0.5) / (taps * samp_len)))
    return (shape_part * taper).reshape(taps, samp_len)


def dft_rows(samp_len, channels):
    sample_idx = jnp.arange(samp_len)[None, :]
    phase = (sample_idx * channels[:, None] % samp_len).astype(jnp.float32) * (
        2.0 * math.pi / samp_len
    )
    scale = 1.0 / math.sqrt(samp_len)
    both = jnp.stack([jnp.cos(phase) * scale, -jnp.sin(phase) * scale], axis=1)
    return both.reshape(-1, samp_len).astype(jnp.bfloat16)


def channelizer_body(widths, x_ref, halo_ref, w_ref, table_ref, *rest):
    outs, (carry, filt, spec) = rest[: len(widths)], rest[len(widths) :]
    block, inputs, samp_len = x_ref.shape
    tiles = block * inputs // LANES
    columns = table_ref.shape[0]

    @pl.when(pl.program_id(0) == 0)
    def _():
        carry[...] = halo_ref[...]

    def fir(group, _):
        rows = pl.ds(pl.multiple_of(group * ROWS, ROWS), ROWS)
        for lane in range(0, samp_len, LANES):
            cols = pl.ds(lane, LANES)
            weights = [
                jnp.broadcast_to(w_ref[p : p + 1, cols], (ROWS, LANES)) for p in range(TAPS)
            ]
            past = [carry[p, rows, cols].astype(jnp.float32) for p in range(TAPS - 1)]
            for f in range(block):
                past.append(x_ref[f, rows, cols].astype(jnp.float32))
                total = weights[0] * past[0]
                for p in range(1, TAPS):
                    total = total + weights[p] * past[p]
                place = pl.ds(pl.multiple_of(f * inputs + group * ROWS, ROWS), ROWS)
                filt[place, cols] = total.astype(jnp.bfloat16)
                past.pop(0)
        return 0

    lax.fori_loop(0, inputs // ROWS, fir, 0)
    carry[...] = x_ref[pl.ds(block - (TAPS - 1), TAPS - 1)]

    step = 2 if tiles % 2 == 0 else 1
    for at in range(0, tiles, step):
        product = lax.dot_general(
            table_ref[...],
            filt[pl.ds(at * LANES, step * LANES), :],
            (((1,), (1,)), ((), ())),
            preferred_element_type=jnp.float32,
        )
        for k in range(step):
            spec[pl.ds((at + k) * columns, columns), :] = product[:, k * LANES : (k + 1) * LANES]

    row = 0
    for out, (groups, width) in zip(outs, widths):
        for g in range(groups):
            for r in range(width):
                out[g, r] = spec[pl.ds(row, tiles, stride=columns), :].astype(jnp.bfloat16)
                row += 1


def channelize(samples, halo, window, table, widths):
    frames, inputs, samp_len = samples.shape
    per_tile = LANES // inputs
    block = min(frames, ROWS * per_tile)
    tiles = block // per_tile
    columns = table.shape[0]
    return pl.pallas_call(
        functools.partial(channelizer_body, widths),
        grid=(frames // block,),
        in_specs=[
            pl.BlockSpec((block, inputs, samp_len), lambda b: (b, 0, 0)),
            pl.BlockSpec(halo.shape, lambda b: (0, 0, 0)),
            pl.BlockSpec(window.shape, lambda b: (0, 0)),
            pl.BlockSpec(table.shape, lambda b: (0, 0)),
        ],
        out_specs=[pl.BlockSpec(w + (tiles, LANES), lambda b: (0, 0, b, 0)) for w in widths],
        out_shape=[
            pltpu.HBM(w + (frames // per_tile, LANES), jnp.bfloat16) for w in widths
        ],
        scratch_shapes=[
            pltpu.VMEM((TAPS - 1, inputs, samp_len), jnp.bfloat16),
            pltpu.VMEM((block * inputs, samp_len), jnp.bfloat16),
            pltpu.VMEM((tiles * columns, LANES), jnp.float32),
        ],
        compiler_params=pltpu.CompilerParams(
            dimension_semantics=("arbitrary",), vmem_limit_bytes=VMEM
        ),
        cost_estimate=pl.CostEstimate(
            flops=2 * frames * inputs * samp_len * columns,
            bytes_accessed=frames * inputs * (samp_len + columns) * 2,
            transcendentals=0,
        ),
        name="channelizer",
    )(*in_hbm([samples, halo]), window, table)


def correlate_body(inputs, scale, where_ref, source, others, own, left, turn):
    groups, _, tiles, _ = source.shape
    per_tile = LANES // inputs
    total = groups * inputs
    block = where_ref[0]
    half = tiles * per_tile

    for t in range(0, groups, per_tile):
        for part in range(2):
            for g in range(per_tile):
                rows = pl.ds(part * half + g * tiles, tiles)
                left[rows, pl.ds(t * inputs, LANES)] = jnp.concatenate(
                    [source[t + j, part, :, g * inputs : (g + 1) * inputs] for j in range(per_tile)],
                    axis=1,
                )

    turn[pl.ds(0, half), :] = left[pl.ds(half, half), :]
    turn[pl.ds(half, half), :] = -left[pl.ds(0, half), :]

    size = own.shape[1]
    dims = (((0,), (0,)), ((), ()))
    for i in range(total // size):
        cols = pl.ds(i * size, size)
        start = i * size // LANES * LANES
        stop = -(-(i + 1) * size // LANES) * LANES
        re = lax.dot_general(
            left[:, cols], left[:, start:], dims, preferred_element_type=jnp.float32
        )
        im = lax.dot_general(
            turn[:, cols], left[:, :stop], dims, preferred_element_type=jnp.float32
        )
        row_idx = lax.broadcasted_iota(jnp.int32, (size, stop - start), 0) + i * size
        col_idx = lax.broadcasted_iota(jnp.int32, (size, stop - start), 1) + start
        mixed = jnp.where(row_idx <= col_idx, re[:, : stop - start], im[:, start:])
        for value, at in ((im[:, :start], 0), (mixed, start), (re[:, stop - start :], stop)):
            if value.shape[1] == 0:
                continue
            value = value * scale
            place = pl.ds(at, value.shape[1])
            others[i, 0, :, place] = jnp.where(block == i, 0.0, value).astype(jnp.bfloat16)

            @pl.when(block == i)
            def _():
                own[0, :, place] = value


def correlate(block, source, blocks, inputs, scale):
    groups, width, tiles, _ = source.shape
    chans = width // 2
    total = groups * inputs
    size = total // blocks
    depth = 2 * tiles * (LANES // inputs)
    return pl.pallas_call(
        functools.partial(correlate_body, inputs, scale),
        grid_spec=pltpu.PrefetchScalarGridSpec(
            num_scalar_prefetch=1,
            grid=(chans,),
            in_specs=[pl.BlockSpec((groups, 2, tiles, LANES), lambda c, _: (0, c, 0, 0))],
            out_specs=[
                pl.BlockSpec((blocks, 1, size, total), lambda c, _: (0, c, 0, 0)),
                pl.BlockSpec((1, size, total), lambda c, _: (c, 0, 0)),
            ],
            scratch_shapes=[pltpu.VMEM((depth, total), jnp.bfloat16)] * 2,
        ),
        out_shape=[
            pltpu.HBM((blocks, chans, size, total), jnp.bfloat16),
            pltpu.HBM((chans, size, total), jnp.float32),
        ],
        compiler_params=pltpu.CompilerParams(
            dimension_semantics=("arbitrary",), vmem_limit_bytes=VMEM
        ),
        cost_estimate=pl.CostEstimate(
            flops=chans * 4 * depth * total * total,
            bytes_accessed=chans * (groups * 4 * tiles * LANES + 2 * total * total + 2 * size * total),
            transcendentals=0,
        ),
        name="correlate",
    )(block, *in_hbm([source]))


def settle_body(counts, *refs):
    out = refs[-1]
    k = 0
    for c, count in enumerate(counts):
        own, came = refs[2 * c], refs[2 * c + 1]
        for at in range(count):
            out[:, k, :] = own[at] + came[0, at].astype(jnp.float32)
            k += 1


def settle(owns, cames):
    counts = [own.shape[0] for own in owns]
    _, rows, total = owns[0].shape
    tall = min(rows, 32)
    specs, operands = [], []
    for own, came, count in zip(owns, cames, counts):
        operands += [own, came]
        specs.append(pl.BlockSpec((count, tall, total), lambda r: (0, r, 0)))
        specs.append(pl.BlockSpec((1, count, tall, total), lambda r: (0, 0, r, 0)))
    return pl.pallas_call(
        functools.partial(settle_body, counts),
        grid=(rows // tall,),
        in_specs=specs,
        out_specs=pl.BlockSpec((tall, sum(counts), total), lambda r: (r, 0, 0)),
        out_shape=jax.ShapeDtypeStruct((rows, sum(counts), total), jnp.float32),
        compiler_params=pltpu.CompilerParams(
            dimension_semantics=("arbitrary",), vmem_limit_bytes=VMEM
        ),
        cost_estimate=pl.CostEstimate(
            flops=rows * sum(counts) * total,
            bytes_accessed=rows * sum(counts) * total * 10,
            transcendentals=0,
        ),
        name="settle",
    )(*operands)


def on_device(samples):
    frames, inputs, samp_len = samples.shape
    groups = lax.axis_size("af")
    blocks = lax.axis_size("ta")
    local = CH // groups
    sizes = chunk_sizes(local)
    earlier = lax.ppermute(
        samples[frames - (TAPS - 1) :], "ta", [(i, i + 1) for i in range(blocks - 1)]
    )
    window = tap_window(TAPS, samp_len)
    order, widths, first = [], [], 0
    for size in sizes:
        order += [g * local + first + jnp.arange(size) for g in range(groups)]
        widths.append((groups, 2 * size))
        first += size
    table = dft_rows(samp_len, jnp.concatenate(order))
    spectra = channelize(samples, earlier, window, table, widths)
    block = lax.axis_index("ta").astype(jnp.int32)[None]
    owns, cames = [], []
    for spectrum in spectra:
        turned = lax.all_to_all(spectrum, "af", split_axis=0, concat_axis=0, tiled=True)
        others, own = correlate(block, turned, blocks, inputs, 1.0 / (frames * blocks))
        owns.append(own)
        cames.append(lax.psum_scatter(others, "ta", scatter_dimension=0, tiled=True))
    return settle(owns, cames)


def solution(mesh):
    in_specs = (P("ta", "af", None),)
    out_specs = P("ta", "af", None)
    return jax.shard_map(
        on_device, mesh=mesh, in_specs=in_specs, out_specs=out_specs, check_vma=False
    )
```

time: 359 us -> 275 us (0.77)
  blocking collectives: 0 us -> 82.1 us
  starting transfers between devices: 88.5 us -> 8.79 us
  waiting for transfers between devices: 155 us -> 96.3 us
  local copies, waits for them, and re-layouts: 40.1 us -> 5.98 us
  between operations: 1.1 us -> 13.3 us
  other arithmetic: 9.89 us -> 2.01 us
    ppermute x70 -> x0, waiting for transfers between devices: 154 us -> none  [the longest x21 115 us: line_sum(): got = lax.ppermute(send, axis, [right, left])]
    ppermute x70 -> x0, starting transfers between devices: 83.5 us -> none  [the longest x49 49.1 us: on_device(): lax.ppermute(mine[s], 'af', [(i, i ^ s) for i in range(groups)])]
    all_to_all x0 -> x2, blocking collectives: none -> 82.1 us  [on_device(): lax.all_to_all(spectrum, 'af', split_axis=0, concat_axis=0, tiled=True)]
    reduce_scatter x0 -> x3, waiting for transfers between devices: none -> 68.8 us  [on_device(): lax.psum_scatter(others, 'ta', scatter_dimension=0, tiled=True)]
    unnamed x142 -> x8, local copies, waits for them, and re-layouts: 33.5 us -> 3.86 us
    all_to_all x0 -> x1, waiting for transfers between devices: none -> 26.6 us  [on_device(): lax.all_to_all(spectrum, 'af', split_axis=0, concat_axis=0, tiled=True)]
    select_n x14 -> x0, other arithmetic: 5.29 us -> none  [line_sum(): send = sends[0] if t == 0 else jnp.where(heading_left, sends[1], sends[0])]
    pallas_call x7 -> x4, Pallas kernels: 32.6 us -> 37.8 us  [the longest x3 32.1 us: correlate(): pl.pallas_call(functools.partial(correlate_body, inputs, scale), grid_spe...]
  transfers between devices with their start and end apart: 71 -> 5, of which waited for: 20 -> 4; matrix products, arithmetic and copies ran while one was open for 3% -> 1% of each run, Pallas kernels for 9% -> 9%
where the time goes in v2:
time: 275 us
  waiting for transfers between devices  96.3 us (35%)
  blocking collectives  82.1 us (30%)
  Pallas kernels  66.2 us (24%)
  between operations  13.3 us (5%)
  starting transfers between devices  8.79 us (3%)
  local copies, waits for them, and re-layouts  5.98 us (2%)
    all_to_all x2, blocking collectives, on_device(): lax.all_to_all(spectrum, 'af', split_axis=0, concat_axis=0, tiled=True)  82.1 us
    reduce_scatter x3, waiting for transfers between devices, on_device(): lax.psum_scatter(others, 'ta', scatter_dimension=0, tiled=True)  68.8 us
    pallas_call x3, Pallas kernels, correlate(): pl.pallas_call(functools.partial(correlate_body, inputs, scale), grid_spe...  32.1 us
    pallas_call x1, Pallas kernels, channelize(): pl.pallas_call(functools.partial(channelizer_body, widths), grid=(frames...  28.4 us
    all_to_all x1, waiting for transfers between devices, on_device(): lax.all_to_all(spectrum, 'af', split_axis=0, concat_axis=0, tiled=True)  26.6 us
    pallas_call x1, Pallas kernels, settle(): pl.pallas_call(functools.partial(settle_body, counts), grid=(rows // tall...  5.68 us
  transfers between devices with their start and end apart: 5, of which 4 were waited for; matrix products, arithmetic and copies ran while one was open for 1% of the time, Pallas kernels for 9%

profile of v2, /device:TPU:0, one launch (start us, length us, event | category | flops | bytes accessed | tf_op | source)
XLA Modules:
  0.0 274.6 jit_solution(15318926826479839461)
XLA Ops:
  6.5 0.9 slice.3
  7.5 4.9 %collective-permute-start = (bf16[3,64,512]{2,1,0:T(8,128)(2,1)S(1)}, bf16[3,64,512]{2,1,0:T(8,128)(2,1)S(1)}, u32[]{:S(2)}, u32[]{:S(2)}) collective-permute-start(bf16[3,64,512]{2,1,0:T(8,128)(2,1)S(1)} %slice.3), channel_id=1, source_target_pairs={{0,1},{1,2},{2,3},{4,5},{5,6},{6,7},{8,9},{9,10},{10,11},{12,13},{... | collective-permute-start | bytes 589832 | tf_op jit(solution)/shard_map/ppermute | solution.py:255
  12.6 0.1 concatenate.3
  12.7 1.2 multiply_convert_fusion.1
  14.0 0.3 copy.2
  14.2 0.8 convert_element_type.28.table_ref
  15.0 0.7 fusion.11.w_ref
  15.7 0.8 collective-permute-done.halo_ref
  16.6 0.0 copy-start.3
  16.6 0.7 copy-done.3
  17.2 28.4 %channelizer.1 = (bf16[8,8,128,128]{3,2,1,0:T(8,128)(2,1)}, bf16[8,12,128,128]{3,2,1,0:T(8,128)(2,1)}, bf16[8,12,128,128]{3,2,1,0:T(8,128)(2,1)}) custom-call(bf16[256,64,512]{2,1,0:T(8,128)(2,1)} %x_ref.1, bf16[3,64,512]{2,1,0:T(8,128)(2,1)} %copy-done.3, f32[4,512]{1,0:T(4,128)} %fusion.11.w_ref, bf16[256,512]{1,0:T(8,128)(2,1)} %convert_element_type.28.table_ref), custom_call_target="tpu_custom_call" | custom-call | flops 4294967296 | bytes 25165824 | tf_op jit(solution)/shard_map/channelizer/pallas_call | solution.py:102
  45.6 3.7 %all-to-all-start = ((bf16[8,8,128,128]{3,2,1,0:T(8,128)(2,1)}), bf16[8,8,128,128]{3,2,1,0:T(8,128)(2,1)S(1)}, u32[]{:S(2)}, u32[]{:S(2)}) async-start(bf16[8,8,128,128]{3,2,1,0:T(8,128)(2,1)} %get-tuple-element.14), calls=%async_computation | async-start | bytes 4194304 | tf_op jit(solution)/shard_map/all_to_all | solution.py:269
  49.4 0.0 reduce-scatter.4.cloned.1.call-start
  49.4 26.6 %all-to-all-done.source = bf16[8,8,128,128]{3,2,1,0:T(8,128)(2,1)S(1)} async-done(((bf16[8,8,128,128]{3,2,1,0:T(8,128)(2,1)}), bf16[8,8,128,128]{3,2,1,0:T(8,128)(2,1)S(1)}, u32[]{:S(2)}, u32[]{:S(2)}) %all-to-all-start) | async-done | bytes 2097184 | tf_op jit(solution)/shard_map/all_to_all | solution.py:269
  76.0 0.0 copy-start.2
  76.0 1.4 copy-done.2
  77.4 0.0 copy-start.1
  77.4 8.6 %correlate.3 = (bf16[4,4,128,512]{3,2,1,0:T(8,128)(2,1)}, f32[4,128,512]{2,1,0:T(8,128)}) custom-call(s32[1]{0:T(128)} %bitcast.where_ref, bf16[8,8,128,128]{3,2,1,0:T(8,128)(2,1)} %copy-done.2), custom_call_target="tpu_custom_call" | custom-call | flops 2147483648 | bytes 4718592 | tf_op jit(solution)/shard_map/correlate/pallas_call | solution.py:184
  86.0 0.0 reduce-scatter.4.cloned.1.call-update
  86.0 0.0 reduce-scatter.8.cloned.1.call-start
  86.1 0.0 copy-done.1
  86.1 41.0 %all_to_all.15.source = bf16[8,12,128,128]{3,2,1,0:T(8,128)(2,1)} all-to-all(bf16[8,12,128,128]{3,2,1,0:T(8,128)(2,1)S(1)} %copy-done.1), channel_id=1, replica_groups=mesh['af'=8,'ta'=4] {'af'}, dimensions={0} | all-to-all | bytes 6291456 | tf_op jit(solution)/shard_map/all_to_all | solution.py:269
  127.1 11.8 %correlate.5 = (bf16[4,6,128,512]{3,2,1,0:T(8,128)(2,1)}, f32[6,128,512]{2,1,0:T(8,128)}) custom-call(s32[1]{0:T(128)} %bitcast.where_ref, bf16[8,12,128,128]{3,2,1,0:T(8,128)(2,1)} %all_to_all.15.source), custom_call_target="tpu_custom_call" | custom-call | flops 3221225472 | bytes 7077888 | tf_op jit(solution)/shard_map/correlate/pallas_call | solution.py:184
  138.9 0.0 copy-start
  138.9 0.0 reduce-scatter.8.cloned.1.call-update
  138.9 0.0 reduce-scatter.6.cloned.1.call-start
  139.0 1.8 copy-done
  140.8 41.0 %all_to_all.16.source = bf16[8,12,128,128]{3,2,1,0:T(8,128)(2,1)} all-to-all(bf16[8,12,128,128]{3,2,1,0:T(8,128)(2,1)S(1)} %copy-done), channel_id=1, replica_groups=mesh['af'=8,'ta'=4] {'af'}, dimensions={0} | all-to-all | bytes 6291456 | tf_op jit(solution)/shard_map/all_to_all | solution.py:269
  181.8 11.8 %correlate.4 = (bf16[4,6,128,512]{3,2,1,0:T(8,128)(2,1)}, f32[6,128,512]{2,1,0:T(8,128)}) custom-call(s32[1]{0:T(128)} %bitcast.where_ref, bf16[8,12,128,128]{3,2,1,0:T(8,128)(2,1)} %all_to_all.16.source), custom_call_target="tpu_custom_call" | custom-call | flops 3221225472 | bytes 7077888 | tf_op jit(solution)/shard_map/correlate/pallas_call | solution.py:184
  193.5 0.0 reduce-scatter.6.cloned.1.call-update
  193.6 0.0 reduce-scatter.4.cloned.1.call-done.refs_1_
  193.6 6.1 %reduce-scatter.8.cloned.1.call-done.refs_5_ = bf16[1,6,128,512]{3,2,1,0:T(8,128)(2,1)} async-done(((bf16[4,6,128,512]{3,2,1,0:T(8,128)(2,1)}), bf16[1,6,128,512]{3,2,1,0:T(8,128)(2,1)}) %reduce-scatter.8.cloned.1.call-update) | async-done | bytes 786448 | tf_op jit(solution)/shard_map/reduce_scatter | solution.py:272
  199.7 62.7 %reduce-scatter.6.cloned.1.call-done.refs_3_ = bf16[1,6,128,512]{3,2,1,0:T(8,128)(2,1)} async-done(((bf16[4,6,128,512]{3,2,1,0:T(8,128)(2,1)}), bf16[1,6,128,512]{3,2,1,0:T(8,128)(2,1)}) %reduce-scatter.6.cloned.1.call-update) | async-done | bytes 786448 | tf_op jit(solution)/shard_map/reduce_scatter | solution.py:272
  262.4 5.7 %settle.1 = f32[128,16,512]{2,1,0:T(8,128)} custom-call(f32[4,128,512]{2,1,0:T(8,128)} %get-tuple-element.15.refs_0_, bf16[1,4,128,512]{3,2,1,0:T(8,128)(2,1)} %reduce-scatter.4.cloned.1.call-done.refs_1_, f32[6,128,512]{2,1,0:T(8,128)} %get-tuple-element.18.refs_2_, bf16[1,6,128,512]{3,2,1,0:T(8,128)(2,1)} %reduce-scatter.6.cloned.1.call-done.refs_3_, ...), custom_call_target="tpu_custom_call" | custom-call | flops 1048576 | bytes 10485760 | tf_op jit(solution)/shard_map/settle/pallas_call | solution.py:231
  (14 shorter events, 0.1 us)
Async XLA Ops:
  7.5 9.1 %collective-permute-start = (bf16[3,64,512]{2,1,0:T(8,128)(2,1)S(1)}, bf16[3,64,512]{2,1,0:T(8,128)(2,1)S(1)}, u32[]{:S(2)}, u32[]{:S(2)}) collective-permute-start(bf16[3,64,512]{2,1,0:T(8,128)(2,1)S(1)} %slice.3), channel_id=1, source_target_pairs={{0,1},{1,2},{2,3},{4,5},{5,6},{6,7},{8,9},{9,10},{10,11},{12,13},{... | collective-permute-start | bytes 589832 | tf_op jit(solution)/shard_map/ppermute | solution.py:255
  16.6 0.7 copy-start.3
  45.6 30.4 %all-to-all-start = ((bf16[8,8,128,128]{3,2,1,0:T(8,128)(2,1)}), bf16[8,8,128,128]{3,2,1,0:T(8,128)(2,1)S(1)}, u32[]{:S(2)}, u32[]{:S(2)}) async-start(bf16[8,8,128,128]{3,2,1,0:T(8,128)(2,1)} %get-tuple-element.14), calls=%async_computation | async-start | bytes 4194304 | tf_op jit(solution)/shard_map/all_to_all | solution.py:269
  49.4 144.2 %reduce-scatter.4.cloned.1.call-start = ((), (), s32[]{:S(2)}) async-start(), calls=%async_computation.6 | async-start | bytes 2621440 | tf_op jit(solution)/shard_map/reduce_scatter | solution.py:272
  76.0 1.4 copy-start.2
  77.4 8.7 %copy-start.1 = (bf16[8,12,128,128]{3,2,1,0:T(8,128)(2,1)S(1)}, bf16[8,12,128,128]{3,2,1,0:T(8,128)(2,1)}, u32[]{:S(2)}) copy-start(bf16[8,12,128,128]{3,2,1,0:T(8,128)(2,1)} %get-tuple-element.20) | copy-start | bytes 9437188
  86.0 113.7 %reduce-scatter.8.cloned.1.call-start = ((), (), s32[]{:S(2)}) async-start(), calls=%async_computation.8 | async-start | bytes 3932160 | tf_op jit(solution)/shard_map/reduce_scatter | solution.py:272
  138.9 1.9 copy-start
  138.9 123.5 %reduce-scatter.6.cloned.1.call-start = ((), (), s32[]{:S(2)}) async-start(), calls=%async_computation.7 | async-start | bytes 3932160 | tf_op jit(solution)/shard_map/reduce_scatter | solution.py:272
Sparse Core Ops, SparseCore 0:
  86.1 44.2 reduce-scatter.3
  139.0 60.6 reduce-scatter.7
  202.1 60.2 reduce-scatter.5

commit v3 on v2

v3 whole, which is shorter than its diff:
```python
import functools
import math

import jax
import jax.numpy as jnp
import numpy as np
from jax import lax
from jax.experimental import pallas as pl
from jax.experimental.pallas import tpu as pltpu
from jax.sharding import PartitionSpec as P

CH = 128
TAPS = 4
LANES = 128
ROWS = 16
PAD = 8
PER = (2, 1)
VMEM = 60 * 1024 * 1024


def chunk_plan(count, blocks):
    unit = count // 16
    swapped = 4 * unit
    if count % 16 or swapped % blocks or blocks & (blocks - 1):
        return [(count, False)]
    return [(8 * unit, False), (4 * unit, False), (swapped, True)]


def tap_window(taps, samp_len):
    points = np.arange(taps * samp_len, dtype=np.float64)
    centre = (taps * samp_len - 1) / 2.0
    shape_part = np.sinc((points - centre) / samp_len)
    taper = np.square(np.sin(math.pi * (points + 0.5) / (taps * samp_len)))
    return (shape_part * taper).reshape(taps, samp_len).astype(np.float32)


def dft_rows(samp_len, channels):
    sample_idx = np.arange(samp_len)[None, :]
    phase = (sample_idx * channels[:, None] % samp_len) * (2.0 * math.pi / samp_len)
    scale = 1.0 / math.sqrt(samp_len)
    both = np.stack([np.cos(phase) * scale, -np.sin(phase) * scale], axis=1)
    return both.reshape(-1, samp_len).astype(np.float32).astype(jnp.bfloat16)


def channelizer_body(widths, x_ref, halo_ref, w_ref, table_ref, *rest):
    outs, (carry, filt, spec) = rest[: len(widths)], rest[len(widths) :]
    block, inputs, samp_len = x_ref.shape
    tiles = block * inputs // LANES
    columns = table_ref.shape[0]
    pitch = spec.shape[0] // tiles

    @pl.when(pl.program_id(0) == 0)
    def _():
        carry[...] = halo_ref[...]

    def fir(group, _):
        rows = pl.ds(pl.multiple_of(group * ROWS, ROWS), ROWS)
        for lane in range(0, samp_len, LANES):
            cols = pl.ds(lane, LANES)
            weights = [
                jnp.broadcast_to(w_ref[p : p + 1, cols], (ROWS, LANES)) for p in range(TAPS)
            ]
            past = [carry[p, rows, cols].astype(jnp.float32) for p in range(TAPS - 1)]
            for f in range(block):
                past.append(x_ref[f, rows, cols].astype(jnp.float32))
                total = weights[0] * past[0]
                for p in range(1, TAPS):
                    total = total + weights[p] * past[p]
                place = pl.ds(pl.multiple_of(f * inputs + group * ROWS, ROWS), ROWS)
                filt[place, cols] = total.astype(jnp.bfloat16)
                past.pop(0)
        return 0

    lax.fori_loop(0, inputs // ROWS, fir, 0)
    carry[...] = x_ref[pl.ds(block - (TAPS - 1), TAPS - 1)]

    step = 2 if tiles % 2 == 0 else 1
    for at in range(0, tiles, step):
        product = lax.dot_general(
            table_ref[...],
            filt[pl.ds(at * LANES, step * LANES), :],
            (((1,), (1,)), ((), ())),
            preferred_element_type=jnp.float32,
        )
        for k in range(step):
            spec[pl.ds((at + k) * pitch, columns), :] = product[:, k * LANES : (k + 1) * LANES]

    row = 0
    for out, (groups, width) in zip(outs, widths):
        for g in range(groups):
            for r in range(width):
                out[g, r] = spec[pl.ds(row, tiles, stride=pitch), :].astype(jnp.bfloat16)
                row += 1


def channelize(samples, halo, window, table, widths):
    frames, inputs, samp_len = samples.shape
    per_tile = LANES // inputs
    block = min(frames, ROWS * per_tile)
    tiles = block // per_tile
    columns = table.shape[0]
    return pl.pallas_call(
        functools.partial(channelizer_body, widths),
        grid=(frames // block,),
        in_specs=[
            pl.BlockSpec((block, inputs, samp_len), lambda b: (b, 0, 0)),
            pl.BlockSpec(halo.shape, lambda b: (0, 0, 0)),
            pl.BlockSpec(window.shape, lambda b: (0, 0)),
            pl.BlockSpec(table.shape, lambda b: (0, 0)),
        ],
        out_specs=[pl.BlockSpec(w + (tiles, LANES), lambda b: (0, 0, b, 0)) for w in widths],
        out_shape=[
            pltpu.HBM(w + (frames // per_tile, LANES), jnp.bfloat16) for w in widths
        ],
        scratch_shapes=[
            pltpu.VMEM((TAPS - 1, inputs, samp_len), jnp.bfloat16),
            pltpu.VMEM((block * inputs, samp_len), jnp.bfloat16),
            pltpu.VMEM((tiles * (columns + PAD), LANES), jnp.float32),
        ],
        compiler_params=pltpu.CompilerParams(
            dimension_semantics=("arbitrary",), vmem_limit_bytes=VMEM
        ),
        cost_estimate=pl.CostEstimate(
            flops=2 * frames * inputs * samp_len * columns,
            bytes_accessed=frames * inputs * (samp_len + columns) * 2,
            transcendentals=0,
        ),
        name="channelizer",
    )(pltpu.with_memory_space_constraint(samples, pltpu.HBM), halo, window, table)


def correlate_body(inputs, scale, pieces, swapped, gated, tied, where_ref, source, *rest):
    rest, (left, turn) = rest[:-2], rest[-2:]
    own, sent = rest[gated + tied], rest[gated + tied + 1 : len(rest) - gated]
    groups, width, tiles, _ = source.shape
    per_tile = LANES // inputs
    total = groups * inputs
    size = own.shape[1]
    block = where_ref[0]
    half = tiles * per_tile
    depth = 2 * half
    chans = width // (2 * pieces)
    row_idx = lax.broadcasted_iota(jnp.int32, (total, total), 0)
    col_idx = lax.broadcasted_iota(jnp.int32, (total, total), 1)
    dims = (((0,), (0,)), ((), ()))
    for c in range(chans):
        for piece in range(pieces):
            base = piece * depth
            for t in range(0, groups, per_tile):
                for part in range(2):
                    at = 2 * (piece * chans + c) + part
                    for g in range(per_tile):
                        rows = pl.ds(base + part * half + g * tiles, tiles)
                        left[c, rows, pl.ds(t * inputs, LANES)] = jnp.concatenate(
                            [
                                source[t + j, at, :, g * inputs : (g + 1) * inputs]
                                for j in range(per_tile)
                            ],
                            axis=1,
                        )
            turn[c, pl.ds(base, half), :] = left[c, pl.ds(base + half, half), :]
            turn[c, pl.ds(base + half, half), :] = -left[c, pl.ds(base, half), :]
        re = lax.dot_general(left[c], left[c], dims, preferred_element_type=jnp.float32)
        im = lax.dot_general(turn[c], left[c], dims, preferred_element_type=jnp.float32)
        packed = jnp.where(row_idx <= col_idx, re, im) * scale
        for i in range(total // size):
            value = packed[i * size : (i + 1) * size]
            if swapped:
                for s in range(1, total // size):

                    @pl.when(block ^ i == s)
                    def _():
                        sent[s - 1][c] = value.astype(jnp.bfloat16)
            else:
                sent[0][i, c] = jnp.where(block == i, 0.0, value).astype(jnp.bfloat16)

            @pl.when(block == i)
            def _():
                own[c] = value


def correlate(block, source, blocks, inputs, scale, swapped, gate, tied):
    groups, width, tiles, _ = source.shape
    pieces = blocks if swapped else 1
    chans = width // (2 * pieces)
    total = groups * inputs
    size = total // blocks
    depth = 2 * tiles * (LANES // inputs) * pieces
    per = next(p for p in PER if chans % p == 0 and (p == 1 or not swapped))
    whole = pl.BlockSpec(memory_space=pltpu.HBM)
    if swapped:
        sent = [pltpu.HBM((chans, size, total), jnp.bfloat16)] * (blocks - 1)
        sent_specs = [pl.BlockSpec((chans, size, total), lambda c, _: (0, 0, 0))] * (blocks - 1)
        per = chans
    else:
        sent = [pltpu.HBM((blocks, chans, size, total), jnp.bfloat16)]
        sent_specs = [pl.BlockSpec((blocks, per, size, total), lambda c, _: (0, c, 0, 0))]
    return pl.pallas_call(
        functools.partial(correlate_body, inputs, scale, pieces, swapped, len(gate), len(tied)),
        grid_spec=pltpu.PrefetchScalarGridSpec(
            num_scalar_prefetch=1,
            grid=(chans // per,),
            in_specs=[
                pl.BlockSpec((groups, 2 * per * pieces, tiles, LANES), lambda c, _: (0, c, 0, 0))
            ]
            + [whole] * (len(gate) + len(tied)),
            out_specs=[pl.BlockSpec((per, size, total), lambda c, _: (c, 0, 0))]
            + sent_specs
            + [whole] * len(gate),
            scratch_shapes=[pltpu.VMEM((per, depth, total), jnp.bfloat16)] * 2,
        ),
        out_shape=[pltpu.HBM((chans, size, total), jnp.float32)]
        + sent
        + [pltpu.HBM(g.shape, g.dtype) for g in gate],
        input_output_aliases={2 + g: 1 + len(sent) + g for g in range(len(gate))},
        compiler_params=pltpu.CompilerParams(
            dimension_semantics=("arbitrary",), vmem_limit_bytes=VMEM
        ),
        cost_estimate=pl.CostEstimate(
            flops=chans * 4 * depth * total * total,
            bytes_accessed=chans * (groups * 4 * tiles * LANES * pieces + 2 * total * total),
            transcendentals=0,
        ),
        name="correlate",
    )(block, source, *gate, *tied)


def settle_body(parts, where_ref, *refs):
    out, k, at = refs[-1], 0, 0
    for swapped, start, stop, count in parts:
        own, came = refs[at], refs[at + 1 : at + count]
        at += count
        for c in range(start, stop):
            if swapped:
                source, c = c // own.shape[0] ^ where_ref[0], c % own.shape[0]
                value = own[c]
                for s, got in enumerate(came):
                    value = jnp.where(source == s + 1, got[c].astype(jnp.float32), value)
            else:
                value = own[c] + came[0][0, c].astype(jnp.float32)
            out[:, k, :] = value
            k += 1


def settle(block, group, parts, operands, prior, shape):
    rows, _, total = shape
    chans = sum(stop - start for _, start, stop, _ in parts)
    tall = min(rows, 32)
    specs = []
    for value in operands:
        if value.ndim == 4:
            specs.append(pl.BlockSpec((1, value.shape[1], tall, total), lambda r, _: (0, 0, r, 0)))
        else:
            specs.append(pl.BlockSpec((value.shape[0], tall, total), lambda r, _: (0, r, 0)))
    if prior is not None:
        operands = operands + [prior]
        specs.append(pl.BlockSpec(memory_space=pltpu.HBM))
    return pl.pallas_call(
        functools.partial(settle_body, parts),
        grid_spec=pltpu.PrefetchScalarGridSpec(
            num_scalar_prefetch=1,
            grid=(rows // tall,),
            in_specs=specs,
            out_specs=pl.BlockSpec((tall, chans, total), lambda r, _: (r, group, 0)),
        ),
        out_shape=jax.ShapeDtypeStruct(shape, jnp.float32),
        input_output_aliases={} if prior is None else {len(operands): 0},
        compiler_params=pltpu.CompilerParams(
            dimension_semantics=("arbitrary",), vmem_limit_bytes=VMEM
        ),
        cost_estimate=pl.CostEstimate(
            flops=rows * chans * total,
            bytes_accessed=rows * chans * total * 10,
            transcendentals=0,
        ),
        name="settle",
    )(block, *operands)


def on_device(samples):
    frames, inputs, samp_len = samples.shape
    groups = lax.axis_size("af")
    blocks = lax.axis_size("ta")
    local = CH // groups
    plan = chunk_plan(local, blocks)
    count = len(plan)
    block = lax.axis_index("ta").astype(jnp.int32)
    earlier = lax.ppermute(
        samples[frames - (TAPS - 1) :], "ta", [(i, i + 1) for i in range(blocks - 1)]
    )
    window = tap_window(TAPS, samp_len)
    firsts = [sum(size for size, _ in plan[:c]) for c in range(count)]

    def rows_of(first, size):
        return dft_rows(
            samp_len, np.concatenate([g * local + first + np.arange(size) for g in range(groups)])
        )

    tables, widths = [], []
    for first, (size, swapped) in zip(firsts, plan):
        if swapped:
            share = size // blocks
            shares = np.stack([rows_of(first + p * share, share) for p in range(blocks)])
            order = block ^ jnp.arange(blocks, dtype=jnp.int32)
            tables.append(jnp.take(shares, order, axis=0).reshape(-1, samp_len))
            widths += [(groups, 2 * share)] * blocks
        else:
            tables.append(rows_of(first, size))
            widths.append((groups, 2 * size))
    table = jnp.concatenate(tables, axis=0)
    made = list(channelize(samples, earlier, window, table, widths))
    spectra = []
    for _, swapped in plan:
        taken = blocks if swapped else 1
        spectra.append(made[:taken])
        made = made[taken:]

    def partners(values):
        return [
            lax.ppermute(value, "ta", [(i, i ^ (s + 1)) for i in range(blocks)])
            for s, value in enumerate(values)
        ]

    tied = {c: [] for c in range(count)}
    for c in range(count):
        if plan[c][1]:
            spectra[c] = spectra[c][:1] + partners(spectra[c][1:])
            tied[0] += spectra[c][1:]
    operands = []
    for c, (size, swapped) in enumerate(plan):
        ready = spectra[c][0] if not swapped else jnp.concatenate(spectra[c], axis=1)
        turned = lax.all_to_all(ready, "af", split_axis=0, concat_axis=0, tiled=True)
        gate = [spectra[c + 1][0]] if 0 < c < count - 1 else []
        own, *rest = correlate(
            block[None], turned, blocks, inputs, 1.0 / (frames * blocks), swapped, gate, tied[c]
        )
        sent = rest[: len(rest) - len(gate)]
        if gate:
            spectra[c + 1] = [rest[-1]] + spectra[c + 1][1:]
        if swapped:
            came = partners(sent)
            if c + 1 < count:
                tied[c + 1] += came
        else:
            came = [lax.psum_scatter(sent[0], "ta", scatter_dimension=0, tiled=True)]
        operands.append([own] + came)
    shape = (groups * inputs // blocks, local, groups * inputs)
    width = 8 if local % 8 == 0 else local
    result = None
    for group in range(local // width):
        parts, used = [], []
        for c, (size, swapped) in enumerate(plan):
            start = max(group * width - firsts[c], 0)
            stop = min((group + 1) * width - firsts[c], size)
            if start < stop:
                parts.append((swapped, start, stop, len(operands[c])))
                used += operands[c]
        result = settle(block[None], group, parts, used, result, shape)
    return result


def solution(mesh):
    in_specs = (P("ta", "af", None),)
    out_specs = P("ta", "af", None)
    return jax.shard_map(
        on_device, mesh=mesh, in_specs=in_specs, out_specs=out_specs, check_vma=False
    )
```

time: 275 us -> 242 us (0.88)
  blocking collectives: 82.1 us -> 59.5 us
  starting transfers between devices: 8.79 us -> 21.3 us
  Pallas kernels: 66.2 us -> 53.7 us
  waiting for transfers between devices: 96.3 us -> 84.7 us
    ppermute x0 -> x6, waiting for transfers between devices: none -> 43.5 us  [partners(): lax.ppermute(value, 'ta', [(i, i ^ s + 1) for i in range(blocks)])]
    reduce_scatter x3 -> x2, waiting for transfers between devices: 68.8 us -> 32 us  [on_device(): came = [lax.psum_scatter(sent[0], 'ta', scatter_dimension=0, tiled=True)]]
    all_to_all x2, blocking collectives: 82.1 us -> 59.5 us  [on_device(): lax.all_to_all(ready, 'af', split_axis=0, concat_axis=0, tiled=True)]
    all_to_all x1, waiting for transfers between devices: 26.6 us -> 8.31 us  [on_device(): lax.all_to_all(ready, 'af', split_axis=0, concat_axis=0, tiled=True)]
    ppermute x0 -> x6, starting transfers between devices: none -> 11.6 us  [partners(): lax.ppermute(value, 'ta', [(i, i ^ s + 1) for i in range(blocks)])]
    pallas_call x1, Pallas kernels: 28.4 us -> 21.9 us  [channelize(): pl.pallas_call(functools.partial(channelizer_body, widths), grid=(frames...]
    pallas_call x4 -> x5, Pallas kernels: 37.8 us -> 31.8 us  [the longest x3 23.5 us: correlate(): pl.pallas_call(functools.partial(correlate_body, inputs, scale, pieces, s...]
  transfers between devices with their start and end apart: 5 -> 10, of which waited for: 4 -> 6; matrix products, arithmetic and copies ran while one was open for 1% -> 1% of each run, Pallas kernels for 9% -> 7%
where the time goes in v3:
time: 242 us; the launch traced here: 241 us
  waiting for transfers between devices  84.7 us (35%)
  blocking collectives  59.5 us (25%)
  Pallas kernels  53.7 us (22%)
  starting transfers between devices  21.3 us (9%)
  between operations  13.5 us (6%)
  local copies, waits for them, and re-layouts  6.22 us (3%)
    all_to_all x2, blocking collectives, on_device(): lax.all_to_all(ready, 'af', split_axis=0, concat_axis=0, tiled=True)  59.5 us
    ppermute x6, waiting for transfers between devices, partners(): lax.ppermute(value, 'ta', [(i, i ^ s + 1) for i in range(blocks)])  43.5 us
    reduce_scatter x2, waiting for transfers between devices, on_device(): came = [lax.psum_scatter(sent[0], 'ta', scatter_dimension=0, tiled=True)]  32 us
    pallas_call x3, Pallas kernels, correlate(): pl.pallas_call(functools.partial(correlate_body, inputs, scale, pieces, s...  23.5 us
    pallas_call x1, Pallas kernels, channelize(): pl.pallas_call(functools.partial(channelizer_body, widths), grid=(frames...  21.9 us
    ppermute x6, starting transfers between devices, partners(): lax.ppermute(value, 'ta', [(i, i ^ s + 1) for i in range(blocks)])  11.6 us
    all_to_all x1, waiting for transfers between devices, on_device(): lax.all_to_all(ready, 'af', split_axis=0, concat_axis=0, tiled=True)  8.31 us
    pallas_call x2, Pallas kernels, settle(): pl.pallas_call(functools.partial(settle_body, parts), grid_spec=pltpu.Pre...  8.25 us
  transfers between devices with their start and end apart: 10, of which 6 were waited for; matrix products, arithmetic and copies ran while one was open for 1% of the time, Pallas kernels for 7%

profile of v3, /device:TPU:0, one launch (start us, length us, event | category | flops | bytes accessed | tf_op | source)
XLA Modules:
  0.0 241.0 jit_solution(8470823781385706449)
XLA Ops:
  6.5 0.9 slice.3
  7.5 4.9 %collective-permute-start = (bf16[3,64,512]{2,1,0:T(8,128)(2,1)S(1)}, bf16[3,64,512]{2,1,0:T(8,128)(2,1)S(1)}, u32[]{:S(2)}, u32[]{:S(2)}) collective-permute-start(bf16[3,64,512]{2,1,0:T(8,128)(2,1)S(1)} %slice.3), channel_id=1, source_target_pairs={{0,1},{1,2},{2,3},{4,5},{5,6},{6,7},{8,9},{9,10},{10,11},{12,13},{... | collective-permute-start | bytes 589832 | tf_op jit(solution)/shard_map/ppermute | solution.py:288
  12.5 0.1 broadcast_in_dim.22
  12.5 0.1 broadcast_in_dim.23
  12.6 1.4 gather_fusion
  14.0 0.1 bitcast_select_fusion
  14.1 1.7 pad_maximum_fusion.1.table_ref
  15.8 0.8 collective-permute-done.halo_ref
  16.6 0.7 copy-done.8
  17.3 21.9 %channelizer.1 = (bf16[8,16,128,128]{3,2,1,0:T(8,128)(2,1)}, bf16[8,8,128,128]{3,2,1,0:T(8,128)(2,1)}, bf16[8,2,128,128]{3,2,1,0:T(8,128)(2,1)}, bf16[8,2,128,12...) custom-call(bf16[256,64,512]{2,1,0:T(8,128)(2,1)} %x_ref.1, ...), custom_call_target="tpu_custom_call" | custom-call | flops 4294967296 | bytes 25165824 | tf_op jit(solution)/shard_map/channelizer/pallas_call | solution.py:102
  39.2 0.0 copy-start.12
  39.2 4.7 %all-to-all-start.2 = ((bf16[8,16,128,128]{3,2,1,0:T(8,128)(2,1)}), bf16[8,16,128,128]{3,2,1,0:T(8,128)(2,1)}, u32[]{:S(2)}, u32[]{:S(2)}) async-start(bf16[8,16,128,128]{3,2,1,0:T(8,128)(2,1)} %get-tuple-element.32), calls=%async_computation.3 | async-start | bytes 8388608 | tf_op jit(solution)/shard_map/all_to_all | solution.py:332
  43.9 0.0 reduce-scatter.5.cloned.1.call-start
  44.0 0.0 copy-done.14
  44.0 2.5 %collective-permute-start.1 = (bf16[8,2,128,128]{3,2,1,0:T(8,128)(2,1)S(1)}, bf16[8,2,128,128]{3,2,1,0:T(8,128)(2,1)S(1)}, u32[]{:S(2)}, u32[]{:S(2)}) collective-permute-start(bf16[8,2,128,128]{3,2,1,0:T(8,128)(2,1)S(1)} %copy-done.14), channel_id=1, source_target_pairs={{0,1},{1,0},{2,3},{3,2},{4,5},{5,4},{6,7},{7,6},{8,9},{9,8},{10,11... | collective-permute-start | bytes 1572872 | tf_op jit(solution)/shard_map/ppermute | solution.py:320
  46.5 0.0 copy-done.13
  46.6 2.6 %collective-permute-start.2 = (bf16[8,2,128,128]{3,2,1,0:T(8,128)(2,1)S(1)}, bf16[8,2,128,128]{3,2,1,0:T(8,128)(2,1)S(1)}, u32[]{:S(2)}, u32[]{:S(2)}) collective-permute-start(bf16[8,2,128,128]{3,2,1,0:T(8,128)(2,1)S(1)} %copy-done.13), channel_id=1, source_target_pairs={{0,2},{1,3},{2,0},{3,1},{4,6},{5,7},{6,4},{7,5},{8,10},{9,11},{10,... | collective-permute-start | bytes 1572872 | tf_op jit(solution)/shard_map/ppermute | solution.py:320
  49.1 0.0 copy-done.12
  49.1 0.0 collective-permute-start.3
  49.1 20.5 %collective-permute-done.1.rest_0_ = bf16[8,2,128,128]{3,2,1,0:T(8,128)(2,1)S(1)} collective-permute-done((bf16[8,2,128,128]{3,2,1,0:T(8,128)(2,1)S(1)}, bf16[8,2,128,128]{3,2,1,0:T(8,128)(2,1)S(1)}, u32[]{:S(2)}, u32[]{:S(2)}) %collective-permute-start.1) | collective-permute-done | bytes 524320 | tf_op jit(solution)/shard_map/ppermute | solution.py:320
  69.7 15.1 %collective-permute-done.2.rest_1_ = bf16[8,2,128,128]{3,2,1,0:T(8,128)(2,1)S(1)} collective-permute-done((bf16[8,2,128,128]{3,2,1,0:T(8,128)(2,1)S(1)}, bf16[8,2,128,128]{3,2,1,0:T(8,128)(2,1)S(1)}, u32[]{:S(2)}, u32[]{:S(2)}) %collective-permute-start.2) | collective-permute-done | bytes 524320 | tf_op jit(solution)/shard_map/ppermute | solution.py:320
  84.8 0.0 collective-permute-done.3.rest_2_
  84.8 8.3 %all-to-all-done.2.source = bf16[8,16,128,128]{3,2,1,0:T(8,128)(2,1)} async-done(((bf16[8,16,128,128]{3,2,1,0:T(8,128)(2,1)}), bf16[8,16,128,128]{3,2,1,0:T(8,128)(2,1)}, u32[]{:S(2)}, u32[]{:S(2)}) %all-to-all-start.2) | async-done | bytes 4194336 | tf_op jit(solution)/shard_map/all_to_all | solution.py:332
  93.1 0.0 copy-done.2
  93.1 0.0 copy-done.4
  93.1 11.1 %correlate.5 = (f32[8,128,512]{2,1,0:T(8,128)}, bf16[4,8,128,512]{3,2,1,0:T(8,128)(2,1)}) custom-call(s32[1]{0:T(128)} %bitcast.where_ref, bf16[8,16,128,128]{3,2,1,0:T(8,128)(2,1)} %all-to-all-done.2.source, bf16[8,2,128,128]{3,2,1,0:T(8,128)(2,1)} %copy-done.2, bf16[8,2,128,128]{3,2,1,0:T(8,128)(2,1)} %copy-done.4, bf16[8,2,128,128]{3,2,1,0:T(8,128)(2,1)} %copy-done.6), custom_call_target="tpu_custom_call" | custom-call | flops 4294967296 | bytes 8388608 | tf_op jit(solution)/shard_map/correlate/pallas_call | solution.py:198
  104.1 0.0 reduce-scatter.5.cloned.1.call-update
  104.2 0.0 reduce-scatter.3.cloned.1.call-start
  104.2 1.5 copy-done
  105.7 29.8 %all_to_all.15.source = bf16[8,8,128,128]{3,2,1,0:T(8,128)(2,1)} all-to-all(bf16[8,8,128,128]{3,2,1,0:T(8,128)(2,1)S(1)} %copy-done), channel_id=1, replica_groups=mesh['af'=8,'ta'=4] {'af'}, dimensions={0} | all-to-all | bytes 4194304 | tf_op jit(solution)/shard_map/all_to_all | solution.py:332
  135.5 6.7 %correlate.3 = (f32[4,128,512]{2,1,0:T(8,128)}, bf16[4,4,128,512]{3,2,1,0:T(8,128)(2,1)}, bf16[8,2,128,128]{3,2,1,0:T(8,128)(2,1)}) custom-call(s32[1]{0:T(128)} %bitcast.where_ref, bf16[8,8,128,128]{3,2,1,0:T(8,128)(2,1)} %all_to_all.15.source, bf16[8,2,128,128]{3,2,1,0:T(8,128)(2,1)} %get-tuple-element.21.rest_0_), custom_call_target="tpu_custom_call", output_to_operand_aliasing={{2}: (2, {})} | custom-call | flops 2147483648 | bytes 4194304 | tf_op jit(solution)/shard_map/correlate/pallas_call | solution.py:198
  142.2 0.0 reduce-scatter.3.cloned.1.call-update
  142.3 1.0 copy-done.1
  143.3 0.2 copy-done.3
  143.4 0.2 copy-done.5
  143.6 0.2 copy-done.7
  143.7 0.3 pad_maximum_fusion
  144.0 29.8 %all_to_all.16.source = bf16[8,8,128,128]{3,2,1,0:T(8,128)(2,1)} all-to-all(bf16[8,8,128,128]{3,2,1,0:T(8,128)(2,1)S(1)} %pad_maximum_fusion), channel_id=1, replica_groups=mesh['af'=8,'ta'=4] {'af'}, dimensions={0} | all-to-all | bytes 4194304 | tf_op jit(solution)/shard_map/all_to_all | solution.py:332
  173.8 5.7 %correlate.4 = (f32[1,128,512]{2,1,0:T(8,128)}, bf16[1,128,512]{2,1,0:T(8,128)(2,1)}, bf16[1,128,512]{2,1,0:T(8,128)(2,1)}, bf16[1,128,512]{2,1,0:T(8,128)(2,1)}) custom-call(s32[1]{0:T(128)} %bitcast.where_ref, bf16[8,8,128,128]{3,2,1,0:T(8,128)(2,1)} %all_to_all.16.source), custom_call_target="tpu_custom_call" | custom-call | flops 2147483648 | bytes 2621440 | tf_op jit(solution)/shard_map/correlate/pallas_call | solution.py:198
  179.5 3.9 %collective-permute-start.4 = (bf16[1,128,512]{2,1,0:T(8,128)(2,1)}, bf16[1,128,512]{2,1,0:T(8,128)(2,1)S(1)}, u32[]{:S(2)}, u32[]{:S(2)}) collective-permute-start(bf16[1,128,512]{2,1,0:T(8,128)(2,1)} %get-tuple-element.29), channel_id=1, source_target_pairs={{0,1},{1,0},{2,3},{3,2},{4,5},{5,4},{6,7},{7,6},{8,9},{9,8},{10,11... | collective-permute-start | bytes 393224 | tf_op jit(solution)/shard_map/ppermute | solution.py:320
  183.4 1.1 collective-permute-start.5
  184.6 1.4 collective-permute-start.6
  185.9 4.2 %settle.2.refs_6_ = f32[128,16,512]{2,1,0:T(8,128)} custom-call(s32[1]{0:T(128)} %bitcast.where_ref, f32[8,128,512]{2,1,0:T(8,128)} %get-tuple-element.33.refs_0_, bf16[1,8,128,512]{3,2,1,0:T(8,128)(2,1)} %reduce-scatter.5.cloned.1.call-done.refs_1_), custom_call_target="tpu_custom_call" | custom-call | flops 524288 | bytes 5242880 | tf_op jit(solution)/shard_map/settle/pallas_call | solution.py:258
  190.1 0.0 collective-permute-done.4.refs_3_
  190.1 7.9 %collective-permute-done.5.refs_4_ = bf16[1,128,512]{2,1,0:T(8,128)(2,1)S(1)} collective-permute-done((bf16[1,128,512]{2,1,0:T(8,128)(2,1)}, bf16[1,128,512]{2,1,0:T(8,128)(2,1)S(1)}, u32[]{:S(2)}, u32[]{:S(2)}) %collective-permute-start.5) | collective-permute-done | bytes 131104 | tf_op jit(solution)/shard_map/ppermute | solution.py:320
  198.1 0.0 collective-permute-done.6.refs_5_
  198.1 32.0 %reduce-scatter.3.cloned.1.call-done.refs_1_ = bf16[1,4,128,512]{3,2,1,0:T(8,128)(2,1)} async-done(((bf16[4,4,128,512]{3,2,1,0:T(8,128)(2,1)}), bf16[1,4,128,512]{3,2,1,0:T(8,128)(2,1)}) %reduce-scatter.3.cloned.1.call-update) | async-done | bytes 524304 | tf_op jit(solution)/shard_map/reduce_scatter | solution.py:345
  230.1 4.0 %settle.3 = f32[128,16,512]{2,1,0:T(8,128)} custom-call(s32[1]{0:T(128)} %bitcast.where_ref, f32[4,128,512]{2,1,0:T(8,128)} %get-tuple-element.22.refs_0_, bf16[1,4,128,512]{3,2,1,0:T(8,128)(2,1)} %reduce-scatter.3.cloned.1.call-done.refs_1_, f32[1,128,512]{2,1,0:T(8,128)} %get-tuple-element.28.refs_2_, ...), custom_call_target="tpu_custom_call", output_to_operand_aliasing={{}: (7, {})} | custom-call | flops 524288 | bytes 5242880 | tf_op jit(solution)/shard_map/settle/pallas_call | solution.py:258
  (22 shorter events, 0.1 us)
Async XLA Ops:
  7.5 9.1 %collective-permute-start = (bf16[3,64,512]{2,1,0:T(8,128)(2,1)S(1)}, bf16[3,64,512]{2,1,0:T(8,128)(2,1)S(1)}, u32[]{:S(2)}, u32[]{:S(2)}) collective-permute-start(bf16[3,64,512]{2,1,0:T(8,128)(2,1)S(1)} %slice.3), channel_id=1, source_target_pairs={{0,1},{1,2},{2,3},{4,5},{5,6},{6,7},{8,9},{9,10},{10,11},{12,13},{... | collective-permute-start | bytes 589832 | tf_op jit(solution)/shard_map/ppermute | solution.py:288
  16.6 0.7 copy-start.8
  39.2 4.8 %copy-start.14 = (bf16[8,2,128,128]{3,2,1,0:T(8,128)(2,1)S(1)}, bf16[8,2,128,128]{3,2,1,0:T(8,128)(2,1)}, u32[]{:S(2)}) copy-start(bf16[8,2,128,128]{3,2,1,0:T(8,128)(2,1)} %get-tuple-element.25) | copy-start | bytes 1572868
  39.2 7.3 %copy-start.13 = (bf16[8,2,128,128]{3,2,1,0:T(8,128)(2,1)S(1)}, bf16[8,2,128,128]{3,2,1,0:T(8,128)(2,1)}, u32[]{:S(2)}) copy-start(bf16[8,2,128,128]{3,2,1,0:T(8,128)(2,1)} %get-tuple-element.26) | copy-start | bytes 1572868
  39.2 9.9 %copy-start.12 = (bf16[8,2,128,128]{3,2,1,0:T(8,128)(2,1)S(1)}, bf16[8,2,128,128]{3,2,1,0:T(8,128)(2,1)}, u32[]{:S(2)}) copy-start(bf16[8,2,128,128]{3,2,1,0:T(8,128)(2,1)} %get-tuple-element.27) | copy-start | bytes 1572868
  39.2 53.8 %all-to-all-start.2 = ((bf16[8,16,128,128]{3,2,1,0:T(8,128)(2,1)}), bf16[8,16,128,128]{3,2,1,0:T(8,128)(2,1)}, u32[]{:S(2)}, u32[]{:S(2)}) async-start(bf16[8,16,128,128]{3,2,1,0:T(8,128)(2,1)} %get-tuple-element.32), calls=%async_computation.3 | async-start | bytes 8388608 | tf_op jit(solution)/shard_map/all_to_all | solution.py:332
  43.9 142.0 %reduce-scatter.5.cloned.1.call-start = ((), (), s32[]{:S(2)}) async-start(), calls=%async_computation.6 | async-start | bytes 5242880 | tf_op jit(solution)/shard_map/reduce_scatter | solution.py:345
  44.0 25.7 %collective-permute-start.1 = (bf16[8,2,128,128]{3,2,1,0:T(8,128)(2,1)S(1)}, bf16[8,2,128,128]{3,2,1,0:T(8,128)(2,1)S(1)}, u32[]{:S(2)}, u32[]{:S(2)}) collective-permute-start(bf16[8,2,128,128]{3,2,1,0:T(8,128)(2,1)S(1)} %copy-done.14), channel_id=1, source_target_pairs={{0,1},{1,0},{2,3},{3,2},{4,5},{5,4},{6,7},{7,6},{8,9},{9,8},{10,11... | collective-permute-start | bytes 1572872 | tf_op jit(solution)/shard_map/ppermute | solution.py:320
  46.6 38.2 %collective-permute-start.2 = (bf16[8,2,128,128]{3,2,1,0:T(8,128)(2,1)S(1)}, bf16[8,2,128,128]{3,2,1,0:T(8,128)(2,1)S(1)}, u32[]{:S(2)}, u32[]{:S(2)}) collective-permute-start(bf16[8,2,128,128]{3,2,1,0:T(8,128)(2,1)S(1)} %copy-done.13), channel_id=1, source_target_pairs={{0,2},{1,3},{2,0},{3,1},{4,6},{5,7},{6,4},{7,5},{8,10},{9,11},{10,... | collective-permute-start | bytes 1572872 | tf_op jit(solution)/shard_map/ppermute | solution.py:320
  49.1 35.6 %collective-permute-start.3 = (bf16[8,2,128,128]{3,2,1,0:T(8,128)(2,1)S(1)}, bf16[8,2,128,128]{3,2,1,0:T(8,128)(2,1)S(1)}, u32[]{:S(2)}, u32[]{:S(2)}) collective-permute-start(bf16[8,2,128,128]{3,2,1,0:T(8,128)(2,1)S(1)} %copy-done.12), channel_id=1, source_target_pairs={{0,3},{1,2},{2,1},{3,0},{4,7},{5,6},{6,5},{7,4},{8,11},{9,10},{10,... | collective-permute-start | bytes 1572872 | tf_op jit(solution)/shard_map/ppermute | solution.py:320
  69.7 23.4 %copy-start.2 = (bf16[8,2,128,128]{3,2,1,0:T(8,128)(2,1)}, bf16[8,2,128,128]{3,2,1,0:T(8,128)(2,1)S(1)}, u32[]{:S(2)}) copy-start(bf16[8,2,128,128]{3,2,1,0:T(8,128)(2,1)S(1)} %collective-permute-done.1.rest_0_) | copy-start | bytes 1572868
  84.8 8.3 %copy-start.4 = (bf16[8,2,128,128]{3,2,1,0:T(8,128)(2,1)}, bf16[8,2,128,128]{3,2,1,0:T(8,128)(2,1)S(1)}, u32[]{:S(2)}) copy-start(bf16[8,2,128,128]{3,2,1,0:T(8,128)(2,1)S(1)} %collective-permute-done.2.rest_1_) | copy-start | bytes 1572868
  84.8 8.3 %copy-start.6 = (bf16[8,2,128,128]{3,2,1,0:T(8,128)(2,1)}, bf16[8,2,128,128]{3,2,1,0:T(8,128)(2,1)S(1)}, u32[]{:S(2)}) copy-start(bf16[8,2,128,128]{3,2,1,0:T(8,128)(2,1)S(1)} %collective-permute-done.3.rest_2_) | copy-start | bytes 1572868
  104.1 1.6 copy-start
  104.2 125.9 %reduce-scatter.3.cloned.1.call-start = ((), (), s32[]{:S(2)}) async-start(), calls=%async_computation.5 | async-start | bytes 2621440 | tf_op jit(solution)/shard_map/reduce_scatter | solution.py:345
  142.2 1.0 copy-start.1
  142.2 1.2 copy-start.3
  142.2 1.4 copy-start.5
  142.2 1.5 copy-start.7
  179.5 10.7 %collective-permute-start.4 = (bf16[1,128,512]{2,1,0:T(8,128)(2,1)}, bf16[1,128,512]{2,1,0:T(8,128)(2,1)S(1)}, u32[]{:S(2)}, u32[]{:S(2)}) collective-permute-start(bf16[1,128,512]{2,1,0:T(8,128)(2,1)} %get-tuple-element.29), channel_id=1, source_target_pairs={{0,1},{1,0},{2,3},{3,2},{4,5},{5,4},{6,7},{7,6},{8,9},{9,8},{10,11... | collective-permute-start | bytes 393224 | tf_op jit(solution)/shard_map/ppermute | solution.py:320
  183.4 14.6 %collective-permute-start.5 = (bf16[1,128,512]{2,1,0:T(8,128)(2,1)}, bf16[1,128,512]{2,1,0:T(8,128)(2,1)S(1)}, u32[]{:S(2)}, u32[]{:S(2)}) collective-permute-start(bf16[1,128,512]{2,1,0:T(8,128)(2,1)} %get-tuple-element.30), channel_id=1, source_target_pairs={{0,2},{1,3},{2,0},{3,1},{4,6},{5,7},{6,4},{7,5},{8,10},{9,11},{10,... | collective-permute-start | bytes 393224 | tf_op jit(solution)/shard_map/ppermute | solution.py:320
  184.6 13.5 %collective-permute-start.6 = (bf16[1,128,512]{2,1,0:T(8,128)(2,1)}, bf16[1,128,512]{2,1,0:T(8,128)(2,1)S(1)}, u32[]{:S(2)}, u32[]{:S(2)}) collective-permute-start(bf16[1,128,512]{2,1,0:T(8,128)(2,1)} %get-tuple-element.31), channel_id=1, source_target_pairs={{0,3},{1,2},{2,1},{3,0},{4,7},{5,6},{6,5},{7,4},{8,11},{9,10},{10,... | collective-permute-start | bytes 393224 | tf_op jit(solution)/shard_map/ppermute | solution.py:320
  190.1 40.0 %copy-start.9 = (bf16[1,128,512]{2,1,0:T(8,128)(2,1)}, bf16[1,128,512]{2,1,0:T(8,128)(2,1)S(1)}, u32[]{:S(2)}) copy-start(bf16[1,128,512]{2,1,0:T(8,128)(2,1)S(1)} %collective-permute-done.4.refs_3_) | copy-start | bytes 393220
  198.1 32.1 %copy-start.10 = (bf16[1,128,512]{2,1,0:T(8,128)(2,1)}, bf16[1,128,512]{2,1,0:T(8,128)(2,1)S(1)}, u32[]{:S(2)}) copy-start(bf16[1,128,512]{2,1,0:T(8,128)(2,1)S(1)} %collective-permute-done.5.refs_4_) | copy-start | bytes 393220
  198.1 32.0 %copy-start.11 = (bf16[1,128,512]{2,1,0:T(8,128)(2,1)}, bf16[1,128,512]{2,1,0:T(8,128)(2,1)S(1)}, u32[]{:S(2)}) copy-start(bf16[1,128,512]{2,1,0:T(8,128)(2,1)S(1)} %collective-permute-done.6.refs_5_) | copy-start | bytes 393220
Sparse Core Ops, SparseCore 0:
  104.3 78.9 reduce-scatter.4
  185.7 44.3 reduce-scatter.2

commit v4 on v3

--- a/solution.py
+++ b/solution.py
@@ -42,16 +42,21 @@
     return both.reshape(-1, samp_len).astype(np.float32).astype(jnp.bfloat16)
 
 
-def channelizer_body(widths, x_ref, halo_ref, w_ref, table_ref, *rest):
-    outs, (carry, filt, spec) = rest[: len(widths)], rest[len(widths) :]
+def channelizer_body(widths, parts, where_ref, x_ref, halo_ref, w_ref, *rest):
+    tables, rest = rest[:parts], rest[parts:]
+    outs, (carry, table, filt, spec) = rest[: len(widths)], rest[len(widths) :]
     block, inputs, samp_len = x_ref.shape
     tiles = block * inputs // LANES
-    columns = table_ref.shape[0]
+    columns = table.shape[0]
     pitch = spec.shape[0] // tiles
 
     @pl.when(pl.program_id(0) == 0)
     def _():
-        carry[...] = halo_ref[...]
+        carry[...] = halo_ref[pl.ds(halo_ref.shape[0] - (TAPS - 1), TAPS - 1)]
+        row = 0
+        for part in tables:
+            table[pl.ds(row, part.shape[-2]), :] = part[...].reshape(part.shape[-2:])
+            row += part.shape[-2]
 
     def fir(group, _):
         rows = pl.ds(pl.multiple_of(group * ROWS, ROWS), ROWS)
@@ -77,7 +82,7 @@
     step = 2 if tiles % 2 == 0 else 1
     for at in range(0, tiles, step):
         product = lax.dot_general(
-            table_ref[...],
+            table[...],
             filt[pl.ds(at * LANES, step * LANES), :],
             (((1,), (1,)), ((), ())),
             preferred_element_type=jnp.float32,
@@ -93,73 +98,99 @@
                 row += 1
 
 
-def channelize(samples, halo, window, table, widths):
-    frames, inputs, samp_len = samples.shape
+def channelize(where, samples, halo, span, window, fixed, shares, widths):
+    _, inputs, samp_len = samples.shape
     per_tile = LANES // inputs
-    block = min(frames, ROWS * per_tile)
+    start, stop = span
+    block = frame_block(samples.shape[0], inputs)
     tiles = block // per_tile
-    columns = table.shape[0]
+    samples = pltpu.with_memory_space_constraint(samples, pltpu.HBM)
+    if halo is None:
+        halo = samples
+        halo_spec = pl.BlockSpec((TAPS, inputs, samp_len), lambda b, _: (start // TAPS - 1, 0, 0))
+    else:
+        halo_spec = pl.BlockSpec(halo.shape, lambda b, _: (0, 0, 0))
+    tables = [fixed]
+    table_specs = [pl.BlockSpec(fixed.shape, lambda b, _: (0, 0))]
+    columns = fixed.shape[0]
+    if shares is not None:
+        tables += [shares] * shares.shape[0]
+        table_specs += [
+            pl.BlockSpec((1,) + shares.shape[1:], lambda b, at, s=s: (at[0] ^ s, 0, 0))
+            for s in range(shares.shape[0])
+        ]
+        columns += shares.shape[0] * shares.shape[1]
     return pl.pallas_call(
-        functools.partial(channelizer_body, widths),
-        grid=(frames // block,),
-        in_specs=[
-            pl.BlockSpec((block, inputs, samp_len), lambda b: (b, 0, 0)),
-            pl.BlockSpec(halo.shape, lambda b: (0, 0, 0)),
-            pl.BlockSpec(window.shape, lambda b: (0, 0)),
-            pl.BlockSpec(table.shape, lambda b: (0, 0)),
-        ],
-        out_specs=[pl.BlockSpec(w + (tiles, LANES), lambda b: (0, 0, b, 0)) for w in widths],
+        functools.partial(channelizer_body, widths, len(tables)),
+        grid_spec=pltpu.PrefetchScalarGridSpec(
+            num_scalar_prefetch=1,
+            grid=((stop - start) // block,),
+            in_specs=[
+                pl.BlockSpec((block, inputs, samp_len), lambda b, _: (b + start // block, 0, 0)),
+                halo_spec,
+                pl.BlockSpec(window.shape, lambda b, _: (0, 0)),
+            ]
+            + table_specs,
+            out_specs=[pl.BlockSpec(w + (tiles, LANES), lambda b, _: (0, 0, b, 0)) for w in widths],
+            scratch_shapes=[
+                pltpu.VMEM((TAPS - 1, inputs, samp_len), jnp.bfloat16),
+                pltpu.VMEM((columns, samp_len), jnp.bfloat16),
+                pltpu.VMEM((block * inputs, samp_len), jnp.bfloat16),
+                pltpu.VMEM((tiles * (columns + PAD), LANES), jnp.float32),
+            ],
+        ),
         out_shape=[
-            pltpu.HBM(w + (frames // per_tile, LANES), jnp.bfloat16) for w in widths
-        ],
-        scratch_shapes=[
-            pltpu.VMEM((TAPS - 1, inputs, samp_len), jnp.bfloat16),
-            pltpu.VMEM((block * inputs, samp_len), jnp.bfloat16),
-            pltpu.VMEM((tiles * (columns + PAD), LANES), jnp.float32),
+            pltpu.HBM(w + ((stop - start) // per_tile, LANES), jnp.bfloat16) for w in widths
         ],
         compiler_params=pltpu.CompilerParams(
             dimension_semantics=("arbitrary",), vmem_limit_bytes=VMEM
         ),
         cost_estimate=pl.CostEstimate(
-            flops=2 * frames * inputs * samp_len * columns,
-            bytes_accessed=frames * inputs * (samp_len + columns) * 2,
+            flops=2 * (stop - start) * inputs * samp_len * columns,
+            bytes_accessed=(stop - start) * inputs * (samp_len + columns) * 2,
             transcendentals=0,
         ),
         name="channelizer",
-    )(pltpu.with_memory_space_constraint(samples, pltpu.HBM), halo, window, table)
-
-
-def correlate_body(inputs, scale, pieces, swapped, gated, tied, where_ref, source, *rest):
+    )(where, samples, halo, window, *tables)
+
+
+def frame_block(frames, inputs):
+    return min(frames, ROWS * (LANES // inputs))
+
+
+def correlate_body(inputs, scale, count, swapped, gated, tied, where_ref, *rest):
+    sources, rest = rest[:count], rest[count:]
     rest, (left, turn) = rest[:-2], rest[-2:]
     own, sent = rest[gated + tied], rest[gated + tied + 1 : len(rest) - gated]
-    groups, width, tiles, _ = source.shape
+    groups, _, width, tiles, _ = sources[0].shape
     per_tile = LANES // inputs
     total = groups * inputs
     size = own.shape[1]
     block = where_ref[0]
     half = tiles * per_tile
-    depth = 2 * half
-    chans = width // (2 * pieces)
     row_idx = lax.broadcasted_iota(jnp.int32, (total, total), 0)
     col_idx = lax.broadcasted_iota(jnp.int32, (total, total), 1)
     dims = (((0,), (0,)), ((), ()))
-    for c in range(chans):
-        for piece in range(pieces):
-            base = piece * depth
-            for t in range(0, groups, per_tile):
-                for part in range(2):
-                    at = 2 * (piece * chans + c) + part
-                    for g in range(per_tile):
-                        rows = pl.ds(base + part * half + g * tiles, tiles)
-                        left[c, rows, pl.ds(t * inputs, LANES)] = jnp.concatenate(
-                            [
-                                source[t + j, at, :, g * inputs : (g + 1) * inputs]
-                                for j in range(per_tile)
-                            ],
-                            axis=1,
-                        )
-            turn[c, pl.ds(base, half), :] = left[c, pl.ds(base + half, half), :]
-            turn[c, pl.ds(base + half, half), :] = -left[c, pl.ds(base, half), :]
+    for c in range(width // 2):
+        base = 0
+        for source in sources:
+            for piece in range(source.shape[1]):
+                for t in range(0, groups, per_tile):
+                    for part in range(2):
+                        for g in range(per_tile):
+                            rows = pl.ds(base + part * half + g * tiles, tiles)
+                            left[c, rows, pl.ds(t * inputs, LANES)] = jnp.concatenate(
+                                [
+                                    source[
+                                        t + j, piece, 2 * c + part, :, g * inputs : (g + 1) * inputs
+                                    ]
+                                    for j in range(per_tile)
+                                ],
+                                axis=1,
+                            )
+                turn[c, pl.ds(base, half), :] = left[c, pl.ds(base + half, half), :]
+                turn[c, pl.ds(base + half, half), :] = -left[c, pl.ds(base, half), :]
+                base += 2 * half
         re = lax.dot_general(left[c], left[c], dims, preferred_element_type=jnp.float32)
         im = lax.dot_general(turn[c], left[c], dims, preferred_element_type=jnp.float32)
         packed = jnp.where(row_idx <= col_idx, re, im) * scale
@@ -179,10 +210,10 @@
                 own[c] = value
 
 
-def correlate(block, source, blocks, inputs, scale, swapped, gate, tied):
-    groups, width, tiles, _ = source.shape
-    pieces = blocks if swapped else 1
-    chans = width // (2 * pieces)
+def correlate(block, sources, blocks, inputs, scale, swapped, gate, tied):
+    groups, _, width, tiles, _ = sources[0].shape
+    pieces = sum(source.shape[1] for source in sources)
+    chans = width // 2
     total = groups * inputs
     size = total // blocks
     depth = 2 * tiles * (LANES // inputs) * pieces
@@ -196,12 +227,17 @@
         sent = [pltpu.HBM((blocks, chans, size, total), jnp.bfloat16)]
         sent_specs = [pl.BlockSpec((blocks, per, size, total), lambda c, _: (0, c, 0, 0))]
     return pl.pallas_call(
-        functools.partial(correlate_body, inputs, scale, pieces, swapped, len(gate), len(tied)),
+        functools.partial(
+            correlate_body, inputs, scale, len(sources), swapped, len(gate), len(tied)
+        ),
         grid_spec=pltpu.PrefetchScalarGridSpec(
             num_scalar_prefetch=1,
             grid=(chans // per,),
             in_specs=[
-                pl.BlockSpec((groups, 2 * per * pieces, tiles, LANES), lambda c, _: (0, c, 0, 0))
+                pl.BlockSpec(
+                    (groups, source.shape[1], 2 * per, tiles, LANES), lambda c, _: (0, 0, c, 0, 0)
+                )
+                for source in sources
             ]
             + [whole] * (len(gate) + len(tied)),
             out_specs=[pl.BlockSpec((per, size, total), lambda c, _: (c, 0, 0))]
@@ -212,7 +248,9 @@
         out_shape=[pltpu.HBM((chans, size, total), jnp.float32)]
         + sent
         + [pltpu.HBM(g.shape, g.dtype) for g in gate],
-        input_output_aliases={2 + g: 1 + len(sent) + g for g in range(len(gate))},
+        input_output_aliases={
+            1 + len(sources) + g: 1 + len(sent) + g for g in range(len(gate))
+        },
         compiler_params=pltpu.CompilerParams(
             dimension_semantics=("arbitrary",), vmem_limit_bytes=VMEM
         ),
@@ -222,7 +260,24 @@
             transcendentals=0,
         ),
         name="correlate",
-    )(block, source, *gate, *tied)
+    )(block, *sources, *gate, *tied)
+
+
+def hold_body(*refs):
+    del refs
+
+
+def hold(value, tied):
+    whole = pl.BlockSpec(memory_space=pltpu.HBM)
+    return pl.pallas_call(
+        hold_body,
+        in_specs=[whole] * (1 + len(tied)),
+        out_specs=whole,
+        out_shape=pltpu.HBM(value.shape, value.dtype),
+        input_output_aliases={0: 0},
+        cost_estimate=pl.CostEstimate(flops=0, bytes_accessed=0, transcendentals=0),
+        name="hold",
+    )(value, *tied)
 
 
 def settle_body(parts, where_ref, *refs):
@@ -245,7 +300,7 @@
 def settle(block, group, parts, operands, prior, shape):
     rows, _, total = shape
     chans = sum(stop - start for _, start, stop, _ in parts)
-    tall = min(rows, 32)
+    tall = min(rows, 64)
     specs = []
     for value in operands:
         if value.ndim == 4:
@@ -296,24 +351,25 @@
             samp_len, np.concatenate([g * local + first + np.arange(size) for g in range(groups)])
         )
 
-    tables, widths = [], []
+    fixed, shares, widths = [], None, []
     for first, (size, swapped) in zip(firsts, plan):
         if swapped:
             share = size // blocks
             shares = np.stack([rows_of(first + p * share, share) for p in range(blocks)])
-            order = block ^ jnp.arange(blocks, dtype=jnp.int32)
-            tables.append(jnp.take(shares, order, axis=0).reshape(-1, samp_len))
             widths += [(groups, 2 * share)] * blocks
         else:
-            tables.append(rows_of(first, size))
+            fixed.append(rows_of(first, size))
             widths.append((groups, 2 * size))
-    table = jnp.concatenate(tables, axis=0)
-    made = list(channelize(samples, earlier, window, table, widths))
-    spectra = []
-    for _, swapped in plan:
-        taken = blocks if swapped else 1
-        spectra.append(made[:taken])
-        made = made[taken:]
+    fixed = np.concatenate(fixed)
+
+    middle = frames // 2 if frames // frame_block(frames, inputs) % 2 == 0 else 0
+    spans = [(middle, frames)] + ([(0, middle)] if middle else [])
+    halves = []
+    for span in spans:
+        halo = earlier if span[0] == 0 else None
+        halves.append(
+            list(channelize(block[None], samples, halo, span, window, fixed, shares, widths))
+        )
 
     def partners(values):
         return [
@@ -321,15 +377,31 @@
             for s, value in enumerate(values)
         ]
 
+    spectra = [[] for _ in plan]
     tied = {c: [] for c in range(count)}
-    for c in range(count):
-        if plan[c][1]:
-            spectra[c] = spectra[c][:1] + partners(spectra[c][1:])
-            tied[0] += spectra[c][1:]
+    moved = []
+    for half in halves:
+        at, moving = 0, []
+        for c, (_, swapped) in enumerate(plan):
+            if swapped:
+                moving += partners(half[at + 1 : at + blocks])
+                spectra[c] += [half[at]] + moving[1 - blocks :]
+                at += blocks
+            else:
+                spectra[c].append(hold(half[at], moved) if moved and c == 0 else half[at])
+                at += 1
+        moved = moving
+        tied[0] += moving
+
+    def turn(value):
+        return lax.all_to_all(value, "af", split_axis=0, concat_axis=0, tiled=True)
+
     operands = []
     for c, (size, swapped) in enumerate(plan):
-        ready = spectra[c][0] if not swapped else jnp.concatenate(spectra[c], axis=1)
-        turned = lax.all_to_all(ready, "af", split_axis=0, concat_axis=0, tiled=True)
+        if c == 0:
+            turned = [turn(piece)[:, None] for piece in spectra[c]]
+        else:
+            turned = [turn(jnp.stack(spectra[c], axis=1))]
         gate = [spectra[c + 1][0]] if 0 < c < count - 1 else []
         own, *rest = correlate(
             block[None], turned, blocks, inputs, 1.0 / (frames * blocks), swapped, gate, tied[c]

time: 242 us -> 236 us (0.975)
  waiting for transfers between devices: 84.7 us -> 64.2 us
  starting transfers between devices: 21.3 us -> 35.4 us
    ppermute x6 -> x9, waiting for transfers between devices: 43.5 us -> 29.4 us  [partners(): lax.ppermute(value, 'ta', [(i, i ^ s + 1) for i in range(blocks)])]
    ppermute x6 -> x9, starting transfers between devices: 11.6 us -> 22.2 us  [partners(): lax.ppermute(value, 'ta', [(i, i ^ s + 1) for i in range(blocks)])]
    all_to_all x1 -> x2, waiting for transfers between devices: 8.31 us -> 0.01 us  [turn(): return lax.all_to_all(value, 'af', split_axis=0, concat_axis=0, tiled=True)]
    all_to_all x1 -> x2, starting transfers between devices: 4.71 us -> 9.66 us  [turn(): return lax.all_to_all(value, 'af', split_axis=0, concat_axis=0, tiled=True)]
    pallas_call x4 -> x6, Pallas kernels: 45.5 us -> 48.3 us  [the longest x2 24.8 us: channelize(): pl.pallas_call(functools.partial(channelizer_body, widths, len(tables)),...]
    unnamed x30 -> x57, local copies, waits for them, and re-layouts: 3.73 us -> 6.47 us
  transfers between devices with their start and end apart: 10 -> 14, of which waited for: 6 -> 6; matrix products, arithmetic and copies ran while one was open for 1% -> 1% of each run, Pallas kernels for 7% -> 12%
where the time goes in v4:
time: 236 us
  waiting for transfers between devices  64.2 us (27%)
  blocking collectives  60.3 us (26%)
  Pallas kernels  54.4 us (23%)
  starting transfers between devices  35.4 us (15%)
  between operations  13.6 us (6%)
  local copies, waits for them, and re-layouts  7.75 us (3%)
    all_to_all x2, blocking collectives, turn(): return lax.all_to_all(value, 'af', split_axis=0, concat_axis=0, tiled=True)  60.3 us
    reduce_scatter x2, waiting for transfers between devices, on_device(): came = [lax.psum_scatter(sent[0], 'ta', scatter_dimension=0, tiled=True)]  34 us
    ppermute x9, waiting for transfers between devices, partners(): lax.ppermute(value, 'ta', [(i, i ^ s + 1) for i in range(blocks)])  29.4 us
    pallas_call x2, Pallas kernels, channelize(): pl.pallas_call(functools.partial(channelizer_body, widths, len(tables)),...  24.8 us
    pallas_call x3, Pallas kernels, correlate(): pl.pallas_call(functools.partial(correlate_body, inputs, scale, len(sourc...  23.5 us
    ppermute x9, starting transfers between devices, partners(): lax.ppermute(value, 'ta', [(i, i ^ s + 1) for i in range(blocks)])  22.2 us
    all_to_all x2, starting transfers between devices, turn(): return lax.all_to_all(value, 'af', split_axis=0, concat_axis=0, tiled=True)  9.66 us
    unnamed x57, local copies, waits for them, and re-layouts  6.47 us
  transfers between devices with their start and end apart: 14, of which 6 were waited for; matrix products, arithmetic and copies ran while one was open for 1% of the time, Pallas kernels for 12%

profile of v4, /device:TPU:0, one launch (start us, length us, event | category | flops | bytes accessed | tf_op | source)
XLA Modules:
  0.0 235.9 jit_solution(431465861972816263)
XLA Ops:
  6.5 12.5 %channelizer.2 = (bf16[8,16,64,128]{3,2,1,0:T(8,128)(2,1)}, bf16[8,8,64,128]{3,2,1,0:T(8,128)(2,1)}, bf16[8,2,64,128]{3,2,1,0:T(8,128)(2,1)}, bf16[8,2,64,128]{3...) custom-call(s32[1]{0:T(128)} %bitcast.where_ref, bf16[256,64,512]{2,1,0:T(8,128)(2,1)} %x_ref.3, ...), custom_call_target="tpu_custom_call" | custom-call | flops 2147483648 | bytes 12582912 | tf_op jit(solution)/shard_map/channelizer/pallas_call | solution.py:123
  19.0 5.3 %all-to-all-start.2 = ((bf16[8,16,64,128]{3,2,1,0:T(8,128)(2,1)}), bf16[8,16,64,128]{3,2,1,0:T(8,128)(2,1)S(1)}, u32[]{:S(2)}, u32[]{:S(2)}) async-start(bf16[8,16,64,128]{3,2,1,0:T(8,128)(2,1)} %get-tuple-element.43), calls=%async_computation.3 | async-start | bytes 4194304 | tf_op jit(solution)/shard_map/all_to_all | solution.py:397
  24.3 0.9 slice.3
  25.3 3.5 %collective-permute-start = (bf16[3,64,512]{2,1,0:T(8,128)(2,1)S(1)}, bf16[3,64,512]{2,1,0:T(8,128)(2,1)S(1)}, u32[]{:S(2)}, u32[]{:S(2)}) collective-permute-start(bf16[3,64,512]{2,1,0:T(8,128)(2,1)S(1)} %slice.3), channel_id=1, source_target_pairs={{0,1},{1,2},{2,3},{4,5},{5,6},{6,7},{8,9},{9,10},{10,11},{12,13},{... | collective-permute-start | bytes 589832 | tf_op jit(solution)/shard_map/ppermute | solution.py:343
  28.8 1.6 collective-permute-start.1
  30.4 1.1 collective-permute-start.2
  31.5 1.7 collective-permute-start.3
  33.2 0.7 collective-permute-done.halo_ref
  34.0 0.7 copy-done.17
  34.6 12.3 %channelizer.3 = (bf16[8,16,64,128]{3,2,1,0:T(8,128)(2,1)}, bf16[8,8,64,128]{3,2,1,0:T(8,128)(2,1)}, bf16[8,2,64,128]{3,2,1,0:T(8,128)(2,1)}, bf16[8,2,64,128]{3...) custom-call(s32[1]{0:T(128)} %bitcast.where_ref, bf16[256,64,512]{2,1,0:T(8,128)(2,1)} %x_ref.3, ...), custom_call_target="tpu_custom_call" | custom-call | flops 2147483648 | bytes 12582912 | tf_op jit(solution)/shard_map/channelizer/pallas_call | solution.py:123
  47.0 4.7 %collective-permute-done.2.refs_2_.rest_3_ = bf16[8,2,64,128]{3,2,1,0:T(8,128)(2,1)S(1)} collective-permute-done((bf16[8,2,64,128]{3,2,1,0:T(8,128)(2,1)S(1)}, bf16[8,2,64,128]{3,2,1,0:T(8,128)(2,1)S(1)}, u32[]{:S(2)}, u32[]{:S(2)}) %collective-permute-start.2) | collective-permute-done | bytes 262176 | tf_op jit(solution)/shard_map/ppermute | solution.py:376
  51.7 0.7 copy-done.3
  52.4 0.1 copy-done.5
  52.6 1.4 copy-done
  53.9 4.3 %all-to-all-start.3 = ((bf16[8,16,64,128]{3,2,1,0:T(8,128)(2,1)}), bf16[8,16,64,128]{3,2,1,0:T(8,128)(2,1)}, u32[]{:S(2)}, u32[]{:S(2)}) async-start(bf16[8,16,64,128]{3,2,1,0:T(8,128)(2,1)} %hold.1), calls=%async_computation.4 | async-start | bytes 4194304 | tf_op jit(solution)/shard_map/all_to_all | solution.py:397
  58.3 0.0 reduce-scatter.5.cloned.1.call-start
  58.3 5.9 %collective-permute-start.4 = (bf16[8,2,64,128]{3,2,1,0:T(8,128)(2,1)}, bf16[8,2,64,128]{3,2,1,0:T(8,128)(2,1)S(1)}, u32[]{:S(2)}, u32[]{:S(2)}) collective-permute-start(bf16[8,2,64,128]{3,2,1,0:T(8,128)(2,1)} %get-tuple-element.36), channel_id=1, source_target_pairs={{0,1},{1,0},{2,3},{3,2},{4,5},{5,4},{6,7},{7,6},{8,9},{9,8},{10,11... | collective-permute-start | bytes 786440 | tf_op jit(solution)/shard_map/ppermute | solution.py:376
  64.2 2.0 collective-permute-start.5
  66.2 1.4 collective-permute-start.6
  67.7 9.1 %collective-permute-done.4.rest_5_ = bf16[8,2,64,128]{3,2,1,0:T(8,128)(2,1)S(1)} collective-permute-done((bf16[8,2,64,128]{3,2,1,0:T(8,128)(2,1)}, bf16[8,2,64,128]{3,2,1,0:T(8,128)(2,1)S(1)}, u32[]{:S(2)}, u32[]{:S(2)}) %collective-permute-start.4) | collective-permute-done | bytes 262176 | tf_op jit(solution)/shard_map/ppermute | solution.py:376
  76.8 8.8 %collective-permute-done.6.rest_7_ = bf16[8,2,64,128]{3,2,1,0:T(8,128)(2,1)S(1)} collective-permute-done((bf16[8,2,64,128]{3,2,1,0:T(8,128)(2,1)S(1)}, bf16[8,2,64,128]{3,2,1,0:T(8,128)(2,1)S(1)}, u32[]{:S(2)}, u32[]{:S(2)}) %collective-permute-start.6) | collective-permute-done | bytes 262176 | tf_op jit(solution)/shard_map/ppermute | solution.py:376
  85.6 0.7 copy-done.15
  86.3 11.1 %correlate.5 = (f32[8,128,512]{2,1,0:T(8,128)}, bf16[4,8,128,512]{3,2,1,0:T(8,128)(2,1)}) custom-call(s32[1]{0:T(128)} %bitcast.where_ref, bf16[8,1,16,64,128]{4,3,2,1,0:T(8,128)(2,1)} %bitcast.21, bf16[8,1,16,64,128]{4,3,2,1,0:T(8,128)(2,1)} %bitcast.12.rest_1_, bf16[8,2,64,128]{3,2,1,0:T(8,128)(2,1)} %copy-done.1, bf16[8,2,64,128]{3,2,1,0:T(8,128)(2,1)} %copy-done.3, ...), custom_call_target="tpu_custom_call" | custom-call | flops 4294967296 | bytes 8388608 | tf_op jit(solution)/shard_map/correlate/pallas_call | solution.py:229
  97.4 0.0 reduce-scatter.3.cloned.1.call-start
  97.5 1.1 copy-done.7
  98.6 0.3 copy-done.8
  98.9 0.2 pad_maximum_fusion
  99.1 30.5 %all_to_all.20.rest_0_ = bf16[8,2,8,64,128]{4,3,2,1,0:T(8,128)(2,1)} all-to-all(bf16[8,2,8,64,128]{4,3,2,1,0:T(8,128)(2,1)S(1)} %pad_maximum_fusion), channel_id=1, replica_groups=mesh['af'=8,'ta'=4] {'af'}, dimensions={0} | all-to-all | bytes 4194304 | tf_op jit(solution)/shard_map/all_to_all | solution.py:397
  129.6 6.7 %correlate.3 = (f32[4,128,512]{2,1,0:T(8,128)}, bf16[4,4,128,512]{3,2,1,0:T(8,128)(2,1)}, bf16[8,2,64,128]{3,2,1,0:T(8,128)(2,1)}) custom-call(s32[1]{0:T(128)} %bitcast.where_ref, bf16[8,2,8,64,128]{4,3,2,1,0:T(8,128)(2,1)} %all_to_all.20.rest_0_, bf16[8,2,64,128]{3,2,1,0:T(8,128)(2,1)} %get-tuple-element.28.rest_1_), custom_call_target="tpu_custom_call", output_to_operand_aliasing={{2}: (2, {})} | custom-call | flops 2147483648 | bytes 4194304 | tf_op jit(solution)/shard_map/correlate/pallas_call | solution.py:229
  136.4 0.0 reduce-scatter.3.cloned.1.call-update
  136.4 0.9 copy-done.9
  137.3 0.1 copy-done.2
  137.4 0.0 copy-done.4
  137.5 0.0 copy-done.6
  137.6 0.0 copy-done.10
  137.7 0.0 copy-done.12
  137.7 0.0 copy-done.14
  137.8 0.0 copy-done.16
  137.9 0.3 copy.9
  138.2 29.8 %all_to_all.21.rest_0_ = bf16[8,8,2,64,128]{4,3,2,1,0:T(8,128)(2,1)} all-to-all(bf16[8,8,2,64,128]{4,3,2,1,0:T(8,128)(2,1)S(1)} %copy.9), channel_id=1, replica_groups=mesh['af'=8,'ta'=4] {'af'}, dimensions={0} | all-to-all | bytes 4194304 | tf_op jit(solution)/shard_map/all_to_all | solution.py:397
  168.0 5.7 %correlate.4 = (f32[1,128,512]{2,1,0:T(8,128)}, bf16[1,128,512]{2,1,0:T(8,128)(2,1)}, bf16[1,128,512]{2,1,0:T(8,128)(2,1)}, bf16[1,128,512]{2,1,0:T(8,128)(2,1)}) custom-call(s32[1]{0:T(128)} %bitcast.where_ref, bf16[8,8,2,64,128]{4,3,2,1,0:T(8,128)(2,1)} %all_to_all.21.rest_0_), custom_call_target="tpu_custom_call" | custom-call | flops 2147483648 | bytes 2621440 | tf_op jit(solution)/shard_map/correlate/pallas_call | solution.py:229
  173.7 5.0 %collective-permute-start.7 = (bf16[1,128,512]{2,1,0:T(8,128)(2,1)}, bf16[1,128,512]{2,1,0:T(8,128)(2,1)S(1)}, u32[]{:S(2)}, u32[]{:S(2)}) collective-permute-start(bf16[1,128,512]{2,1,0:T(8,128)(2,1)} %get-tuple-element.40), channel_id=1, source_target_pairs={{0,1},{1,0},{2,3},{3,2},{4,5},{5,4},{6,7},{7,6},{8,9},{9,8},{10,11... | collective-permute-start | bytes 393224 | tf_op jit(solution)/shard_map/ppermute | solution.py:376
  178.7 2.0 collective-permute-start.8
  180.6 1.5 collective-permute-start.9
  182.1 3.2 %settle.2.refs_6_ = f32[128,16,512]{2,1,0:T(8,128)} custom-call(s32[1]{0:T(128)} %bitcast.where_ref, f32[8,128,512]{2,1,0:T(8,128)} %get-tuple-element.45.refs_0_, bf16[1,8,128,512]{3,2,1,0:T(8,128)(2,1)} %reduce-scatter.5.cloned.1.call-done.refs_1_), custom_call_target="tpu_custom_call" | custom-call | flops 524288 | bytes 5242880 | tf_op jit(solution)/shard_map/settle/pallas_call | solution.py:313
  185.2 6.7 %collective-permute-done.8.refs_4_ = bf16[1,128,512]{2,1,0:T(8,128)(2,1)S(1)} collective-permute-done((bf16[1,128,512]{2,1,0:T(8,128)(2,1)}, bf16[1,128,512]{2,1,0:T(8,128)(2,1)S(1)}, u32[]{:S(2)}, u32[]{:S(2)}) %collective-permute-start.8) | collective-permute-done | bytes 131104 | tf_op jit(solution)/shard_map/ppermute | solution.py:376
  192.0 34.0 %reduce-scatter.3.cloned.1.call-done.refs_1_ = bf16[1,4,128,512]{3,2,1,0:T(8,128)(2,1)} async-done(((bf16[4,4,128,512]{3,2,1,0:T(8,128)(2,1)}), bf16[1,4,128,512]{3,2,1,0:T(8,128)(2,1)}) %reduce-scatter.3.cloned.1.call-update) | async-done | bytes 524304 | tf_op jit(solution)/shard_map/reduce_scatter | solution.py:417
  226.1 3.0 %settle.3 = f32[128,16,512]{2,1,0:T(8,128)} custom-call(s32[1]{0:T(128)} %bitcast.where_ref, f32[4,128,512]{2,1,0:T(8,128)} %get-tuple-element.29.refs_0_, bf16[1,4,128,512]{3,2,1,0:T(8,128)(2,1)} %reduce-scatter.3.cloned.1.call-done.refs_1_, f32[1,128,512]{2,1,0:T(8,128)} %get-tuple-element.39.refs_2_, ...), custom_call_target="tpu_custom_call", output_to_operand_aliasing={{}: (7, {})} | custom-call | flops 524288 | bytes 5242880 | tf_op jit(solution)/shard_map/settle/pallas_call | solution.py:313
  (53 shorter events, 0.4 us)
Async XLA Ops:
  19.0 11.4 %copy-start.24 = (bf16[8,2,64,128]{3,2,1,0:T(8,128)(2,1)S(1)}, bf16[8,2,64,128]{3,2,1,0:T(8,128)(2,1)}, u32[]{:S(2)}) copy-start(bf16[8,2,64,128]{3,2,1,0:T(8,128)(2,1)} %get-tuple-element.33) | copy-start | bytes 786436
  19.0 12.5 %copy-start.23 = (bf16[8,2,64,128]{3,2,1,0:T(8,128)(2,1)S(1)}, bf16[8,2,64,128]{3,2,1,0:T(8,128)(2,1)}, u32[]{:S(2)}) copy-start(bf16[8,2,64,128]{3,2,1,0:T(8,128)(2,1)} %get-tuple-element.34) | copy-start | bytes 786436
  19.0 33.5 %all-to-all-start.2 = ((bf16[8,16,64,128]{3,2,1,0:T(8,128)(2,1)}), bf16[8,16,64,128]{3,2,1,0:T(8,128)(2,1)S(1)}, u32[]{:S(2)}, u32[]{:S(2)}) async-start(bf16[8,16,64,128]{3,2,1,0:T(8,128)(2,1)} %get-tuple-element.43), calls=%async_computation.3 | async-start | bytes 4194304 | tf_op jit(solution)/shard_map/all_to_all | solution.py:397
  25.3 8.7 %collective-permute-start = (bf16[3,64,512]{2,1,0:T(8,128)(2,1)S(1)}, bf16[3,64,512]{2,1,0:T(8,128)(2,1)S(1)}, u32[]{:S(2)}, u32[]{:S(2)}) collective-permute-start(bf16[3,64,512]{2,1,0:T(8,128)(2,1)S(1)} %slice.3), channel_id=1, source_target_pairs={{0,1},{1,2},{2,3},{4,5},{5,6},{6,7},{8,9},{9,10},{10,11},{12,13},{... | collective-permute-start | bytes 589832 | tf_op jit(solution)/shard_map/ppermute | solution.py:343
  28.8 18.2 %collective-permute-start.1 = (bf16[8,2,64,128]{3,2,1,0:T(8,128)(2,1)}, bf16[8,2,64,128]{3,2,1,0:T(8,128)(2,1)S(1)}, u32[]{:S(2)}, u32[]{:S(2)}) collective-permute-start(bf16[8,2,64,128]{3,2,1,0:T(8,128)(2,1)} %get-tuple-element.32), channel_id=1, source_target_pairs={{0,1},{1,0},{2,3},{3,2},{4,5},{5,4},{6,7},{7,6},{8,9},{9,8},{10,11... | collective-permute-start | bytes 786440 | tf_op jit(solution)/shard_map/ppermute | solution.py:376
  30.4 21.3 %collective-permute-start.2 = (bf16[8,2,64,128]{3,2,1,0:T(8,128)(2,1)S(1)}, bf16[8,2,64,128]{3,2,1,0:T(8,128)(2,1)S(1)}, u32[]{:S(2)}, u32[]{:S(2)}) collective-permute-start(bf16[8,2,64,128]{3,2,1,0:T(8,128)(2,1)S(1)} %copy-done.24), channel_id=1, source_target_pairs={{0,2},{1,3},{2,0},{3,1},{4,6},{5,7},{6,4},{7,5},{8,10},{9,11},{10,... | collective-permute-start | bytes 786440 | tf_op jit(solution)/shard_map/ppermute | solution.py:376
  31.5 20.2 %collective-permute-start.3 = (bf16[8,2,64,128]{3,2,1,0:T(8,128)(2,1)S(1)}, bf16[8,2,64,128]{3,2,1,0:T(8,128)(2,1)S(1)}, u32[]{:S(2)}, u32[]{:S(2)}) collective-permute-start(bf16[8,2,64,128]{3,2,1,0:T(8,128)(2,1)S(1)} %copy-done.23), channel_id=1, source_target_pairs={{0,3},{1,2},{2,1},{3,0},{4,7},{5,6},{6,5},{7,4},{8,11},{9,10},{10,... | collective-permute-start | bytes 786440 | tf_op jit(solution)/shard_map/ppermute | solution.py:376
  34.0 0.7 copy-start.17
  47.0 4.8 %copy-start.1 = (bf16[8,2,64,128]{3,2,1,0:T(8,128)(2,1)}, bf16[8,2,64,128]{3,2,1,0:T(8,128)(2,1)S(1)}, u32[]{:S(2)}) copy-start(bf16[8,2,64,128]{3,2,1,0:T(8,128)(2,1)S(1)} %collective-permute-done.1.refs_1_.rest_2_) | copy-start | bytes 786436
  51.7 0.7 copy-start.3
  51.7 0.8 copy-start.5
  52.5 11.7 %copy-start.22 = (bf16[8,2,64,128]{3,2,1,0:T(8,128)(2,1)S(1)}, bf16[8,2,64,128]{3,2,1,0:T(8,128)(2,1)}, u32[]{:S(2)}) copy-start(bf16[8,2,64,128]{3,2,1,0:T(8,128)(2,1)} %get-tuple-element.37) | copy-start | bytes 786436
  52.5 13.7 %copy-start.21 = (bf16[8,2,64,128]{3,2,1,0:T(8,128)(2,1)S(1)}, bf16[8,2,64,128]{3,2,1,0:T(8,128)(2,1)}, u32[]{:S(2)}) copy-start(bf16[8,2,64,128]{3,2,1,0:T(8,128)(2,1)} %get-tuple-element.38) | copy-start | bytes 786436
  52.5 1.4 copy-start
  53.9 31.7 %all-to-all-start.3 = ((bf16[8,16,64,128]{3,2,1,0:T(8,128)(2,1)}), bf16[8,16,64,128]{3,2,1,0:T(8,128)(2,1)}, u32[]{:S(2)}, u32[]{:S(2)}) async-start(bf16[8,16,64,128]{3,2,1,0:T(8,128)(2,1)} %hold.1), calls=%async_computation.4 | async-start | bytes 4194304 | tf_op jit(solution)/shard_map/all_to_all | solution.py:397
  58.3 123.8 %reduce-scatter.5.cloned.1.call-start = ((), (), s32[]{:S(2)}) async-start(), calls=%async_computation.7 | async-start | bytes 5242880 | tf_op jit(solution)/shard_map/reduce_scatter | solution.py:417
  58.3 18.5 %collective-permute-start.4 = (bf16[8,2,64,128]{3,2,1,0:T(8,128)(2,1)}, bf16[8,2,64,128]{3,2,1,0:T(8,128)(2,1)S(1)}, u32[]{:S(2)}, u32[]{:S(2)}) collective-permute-start(bf16[8,2,64,128]{3,2,1,0:T(8,128)(2,1)} %get-tuple-element.36), channel_id=1, source_target_pairs={{0,1},{1,0},{2,3},{3,2},{4,5},{5,4},{6,7},{7,6},{8,9},{9,8},{10,11... | collective-permute-start | bytes 786440 | tf_op jit(solution)/shard_map/ppermute | solution.py:376
  64.2 12.6 %collective-permute-start.5 = (bf16[8,2,64,128]{3,2,1,0:T(8,128)(2,1)S(1)}, bf16[8,2,64,128]{3,2,1,0:T(8,128)(2,1)S(1)}, u32[]{:S(2)}, u32[]{:S(2)}) collective-permute-start(bf16[8,2,64,128]{3,2,1,0:T(8,128)(2,1)S(1)} %copy-done.22), channel_id=1, source_target_pairs={{0,2},{1,3},{2,0},{3,1},{4,6},{5,7},{6,4},{7,5},{8,10},{9,11},{10,... | collective-permute-start | bytes 786440 | tf_op jit(solution)/shard_map/ppermute | solution.py:376
  66.2 19.4 %collective-permute-start.6 = (bf16[8,2,64,128]{3,2,1,0:T(8,128)(2,1)S(1)}, bf16[8,2,64,128]{3,2,1,0:T(8,128)(2,1)S(1)}, u32[]{:S(2)}, u32[]{:S(2)}) collective-permute-start(bf16[8,2,64,128]{3,2,1,0:T(8,128)(2,1)S(1)} %copy-done.21), channel_id=1, source_target_pairs={{0,3},{1,2},{2,1},{3,0},{4,7},{5,6},{6,5},{7,4},{8,11},{9,10},{10,... | collective-permute-start | bytes 786440 | tf_op jit(solution)/shard_map/ppermute | solution.py:376
  76.8 8.8 %copy-start.11 = (bf16[8,2,64,128]{3,2,1,0:T(8,128)(2,1)}, bf16[8,2,64,128]{3,2,1,0:T(8,128)(2,1)S(1)}, u32[]{:S(2)}) copy-start(bf16[8,2,64,128]{3,2,1,0:T(8,128)(2,1)S(1)} %collective-permute-done.4.rest_5_) | copy-start | bytes 786436
  76.8 8.8 %copy-start.13 = (bf16[8,2,64,128]{3,2,1,0:T(8,128)(2,1)}, bf16[8,2,64,128]{3,2,1,0:T(8,128)(2,1)S(1)}, u32[]{:S(2)}) copy-start(bf16[8,2,64,128]{3,2,1,0:T(8,128)(2,1)S(1)} %collective-permute-done.5.rest_6_) | copy-start | bytes 786436
  85.6 0.7 copy-start.15
  97.4 1.2 copy-start.7
  97.4 1.5 copy-start.8
  97.4 128.6 %reduce-scatter.3.cloned.1.call-start = ((), (), s32[]{:S(2)}) async-start(), calls=%async_computation.6 | async-start | bytes 2621440 | tf_op jit(solution)/shard_map/reduce_scatter | solution.py:417
  136.3 0.9 copy-start.9
  136.3 1.0 copy-start.2
  136.3 1.1 copy-start.4
  136.3 1.2 copy-start.6
  136.3 1.3 copy-start.10
  136.3 1.3 copy-start.12
  136.4 1.4 copy-start.14
  136.4 1.5 copy-start.16
  173.7 11.6 %collective-permute-start.7 = (bf16[1,128,512]{2,1,0:T(8,128)(2,1)}, bf16[1,128,512]{2,1,0:T(8,128)(2,1)S(1)}, u32[]{:S(2)}, u32[]{:S(2)}) collective-permute-start(bf16[1,128,512]{2,1,0:T(8,128)(2,1)} %get-tuple-element.40), channel_id=1, source_target_pairs={{0,1},{1,0},{2,3},{3,2},{4,5},{5,4},{6,7},{7,6},{8,9},{9,8},{10,11... | collective-permute-start | bytes 393224 | tf_op jit(solution)/shard_map/ppermute | solution.py:376
  178.7 13.3 %collective-permute-start.8 = (bf16[1,128,512]{2,1,0:T(8,128)(2,1)}, bf16[1,128,512]{2,1,0:T(8,128)(2,1)S(1)}, u32[]{:S(2)}, u32[]{:S(2)}) collective-permute-start(bf16[1,128,512]{2,1,0:T(8,128)(2,1)} %get-tuple-element.41), channel_id=1, source_target_pairs={{0,2},{1,3},{2,0},{3,1},{4,6},{5,7},{6,4},{7,5},{8,10},{9,11},{10,... | collective-permute-start | bytes 393224 | tf_op jit(solution)/shard_map/ppermute | solution.py:376
  180.6 11.4 %collective-permute-start.9 = (bf16[1,128,512]{2,1,0:T(8,128)(2,1)}, bf16[1,128,512]{2,1,0:T(8,128)(2,1)S(1)}, u32[]{:S(2)}, u32[]{:S(2)}) collective-permute-start(bf16[1,128,512]{2,1,0:T(8,128)(2,1)} %get-tuple-element.42), channel_id=1, source_target_pairs={{0,3},{1,2},{2,1},{3,0},{4,7},{5,6},{6,5},{7,4},{8,11},{9,10},{10,... | collective-permute-start | bytes 393224 | tf_op jit(solution)/shard_map/ppermute | solution.py:376
  185.2 40.8 %copy-start.18 = (bf16[1,128,512]{2,1,0:T(8,128)(2,1)}, bf16[1,128,512]{2,1,0:T(8,128)(2,1)S(1)}, u32[]{:S(2)}) copy-start(bf16[1,128,512]{2,1,0:T(8,128)(2,1)S(1)} %collective-permute-done.7.refs_3_) | copy-start | bytes 393220
  192.0 34.1 %copy-start.19 = (bf16[1,128,512]{2,1,0:T(8,128)(2,1)}, bf16[1,128,512]{2,1,0:T(8,128)(2,1)S(1)}, u32[]{:S(2)}) copy-start(bf16[1,128,512]{2,1,0:T(8,128)(2,1)S(1)} %collective-permute-done.8.refs_4_) | copy-start | bytes 393220
  192.0 34.1 %copy-start.20 = (bf16[1,128,512]{2,1,0:T(8,128)(2,1)}, bf16[1,128,512]{2,1,0:T(8,128)(2,1)S(1)}, u32[]{:S(2)}) copy-start(bf16[1,128,512]{2,1,0:T(8,128)(2,1)S(1)} %collective-permute-done.9.refs_5_) | copy-start | bytes 393220
Sparse Core Ops, SparseCore 0:
  97.5 81.6 reduce-scatter.4
  181.6 44.3 reduce-scatter.2

commit v5 on v4

--- a/solution.py
+++ b/solution.py
@@ -388,10 +388,9 @@
                 spectra[c] += [half[at]] + moving[1 - blocks :]
                 at += blocks
             else:
-                spectra[c].append(hold(half[at], moved) if moved and c == 0 else half[at])
+                spectra[c].append(hold(half[at], moved[:2]) if moved and c == 0 else half[at])
                 at += 1
-        moved = moving
-        tied[0] += moving
+        moved = moved[2:] + moving
 
     def turn(value):
         return lax.all_to_all(value, "af", split_axis=0, concat_axis=0, tiled=True)
@@ -414,6 +413,8 @@
             if c + 1 < count:
                 tied[c + 1] += came
         else:
+            if c == 0 and moved:
+                sent[0] = hold(sent[0], moved)
             came = [lax.psum_scatter(sent[0], "ta", scatter_dimension=0, tiled=True)]
         operands.append([own] + came)
     shape = (groups * inputs // blocks, local, groups * inputs)

time: 236 us -> 233 us (0.987)
  waiting for transfers between devices: 64.2 us -> 61.6 us
    ppermute x9, waiting for transfers between devices: 29.4 us -> 9.49 us  [partners(): lax.ppermute(value, 'ta', [(i, i ^ s + 1) for i in range(blocks)])]
    all_to_all x2, waiting for transfers between devices: 0.01 us -> 18.5 us  [turn(): return lax.all_to_all(value, 'af', split_axis=0, concat_axis=0, tiled=True)]
    reduce_scatter x2, waiting for transfers between devices: 34 us -> 31.2 us  [on_device(): came = [lax.psum_scatter(sent[0], 'ta', scatter_dimension=0, tiled=True)]]
    unnamed x57 -> x61, local copies, waits for them, and re-layouts: 6.47 us -> 6.67 us
  transfers between devices with their start and end apart: 14 -> 14, of which waited for: 6 -> 5; matrix products, arithmetic and copies ran while one was open for 1% -> 1% of each run, Pallas kernels for 12% -> 17%
where the time goes in v5:
time: 233 us; the launch traced here: 232 us
  waiting for transfers between devices  61.6 us (26%)
  blocking collectives  59.5 us (26%)
  Pallas kernels  54.4 us (23%)
  starting transfers between devices  34.7 us (15%)
  between operations  13.7 us (6%)
  local copies, waits for them, and re-layouts  7.94 us (3%)
    all_to_all x2, blocking collectives, turn(): return lax.all_to_all(value, 'af', split_axis=0, concat_axis=0, tiled=True)  59.5 us
    reduce_scatter x2, waiting for transfers between devices, on_device(): came = [lax.psum_scatter(sent[0], 'ta', scatter_dimension=0, tiled=True)]  31.2 us
    pallas_call x2, Pallas kernels, channelize(): pl.pallas_call(functools.partial(channelizer_body, widths, len(tables)),...  24.7 us
    pallas_call x3, Pallas kernels, correlate(): pl.pallas_call(functools.partial(correlate_body, inputs, scale, len(sourc...  23.5 us
    ppermute x9, starting transfers between devices, partners(): lax.ppermute(value, 'ta', [(i, i ^ s + 1) for i in range(blocks)])  21.5 us
    all_to_all x2, waiting for transfers between devices, turn(): return lax.all_to_all(value, 'af', split_axis=0, concat_axis=0, tiled=True)  18.5 us
    all_to_all x2, starting transfers between devices, turn(): return lax.all_to_all(value, 'af', split_axis=0, concat_axis=0, tiled=True)  9.68 us
    ppermute x9, waiting for transfers between devices, partners(): lax.ppermute(value, 'ta', [(i, i ^ s + 1) for i in range(blocks)])  9.49 us
  transfers between devices with their start and end apart: 14, of which 5 were waited for; matrix products, arithmetic and copies ran while one was open for 1% of the time, Pallas kernels for 17%

profile of v5, /device:TPU:0, one launch (start us, length us, event | category | flops | bytes accessed | tf_op | source)
XLA Modules:
  0.0 232.0 jit_solution(10457884988223388217)
XLA Ops:
  6.5 12.4 %channelizer.2 = (bf16[8,16,64,128]{3,2,1,0:T(8,128)(2,1)}, bf16[8,8,64,128]{3,2,1,0:T(8,128)(2,1)}, bf16[8,2,64,128]{3,2,1,0:T(8,128)(2,1)}, bf16[8,2,64,128]{3...) custom-call(s32[1]{0:T(128)} %bitcast.where_ref, bf16[256,64,512]{2,1,0:T(8,128)(2,1)} %x_ref.3, ...), custom_call_target="tpu_custom_call" | custom-call | flops 2147483648 | bytes 12582912 | tf_op jit(solution)/shard_map/channelizer/pallas_call | solution.py:123
  19.0 5.3 %all-to-all-start.2 = ((bf16[8,16,64,128]{3,2,1,0:T(8,128)(2,1)}), bf16[8,16,64,128]{3,2,1,0:T(8,128)(2,1)S(1)}, u32[]{:S(2)}, u32[]{:S(2)}) async-start(bf16[8,16,64,128]{3,2,1,0:T(8,128)(2,1)} %get-tuple-element.43), calls=%async_computation.3 | async-start | bytes 4194304 | tf_op jit(solution)/shard_map/all_to_all | solution.py:396
  24.3 0.9 slice.3
  25.2 3.5 %collective-permute-start = (bf16[3,64,512]{2,1,0:T(8,128)(2,1)S(1)}, bf16[3,64,512]{2,1,0:T(8,128)(2,1)S(1)}, u32[]{:S(2)}, u32[]{:S(2)}) collective-permute-start(bf16[3,64,512]{2,1,0:T(8,128)(2,1)S(1)} %slice.3), channel_id=1, source_target_pairs={{0,1},{1,2},{2,3},{4,5},{5,6},{6,7},{8,9},{9,10},{10,11},{12,13},{... | collective-permute-start | bytes 589832 | tf_op jit(solution)/shard_map/ppermute | solution.py:343
  28.7 1.6 collective-permute-start.1
  30.4 1.1 collective-permute-start.2
  31.5 2.4 %collective-permute-done.halo_ref = bf16[3,64,512]{2,1,0:T(8,128)(2,1)S(1)} collective-permute-done((bf16[3,64,512]{2,1,0:T(8,128)(2,1)S(1)}, bf16[3,64,512]{2,1,0:T(8,128)(2,1)S(1)}, u32[]{:S(2)}, u32[]{:S(2)}) %collective-permute-start) | collective-permute-done | bytes 196640 | tf_op jit(solution)/shard_map/ppermute | solution.py:343
  33.9 0.7 copy-done.17
  34.6 12.3 %channelizer.3 = (bf16[8,16,64,128]{3,2,1,0:T(8,128)(2,1)}, bf16[8,8,64,128]{3,2,1,0:T(8,128)(2,1)}, bf16[8,2,64,128]{3,2,1,0:T(8,128)(2,1)}, bf16[8,2,64,128]{3...) custom-call(s32[1]{0:T(128)} %bitcast.where_ref, bf16[256,64,512]{2,1,0:T(8,128)(2,1)} %x_ref.3, ...), custom_call_target="tpu_custom_call" | custom-call | flops 2147483648 | bytes 12582912 | tf_op jit(solution)/shard_map/channelizer/pallas_call | solution.py:123
  46.9 0.7 copy-done.1
  47.6 0.1 copy-done.3
  47.7 3.2 %all-to-all-done.2 = bf16[8,16,64,128]{3,2,1,0:T(8,128)(2,1)S(1)} async-done(((bf16[8,16,64,128]{3,2,1,0:T(8,128)(2,1)}), bf16[8,16,64,128]{3,2,1,0:T(8,128)(2,1)S(1)}, u32[]{:S(2)}, u32[]{:S(2)}) %all-to-all-start.2) | async-done | bytes 2097184 | tf_op jit(solution)/shard_map/all_to_all | solution.py:396
  50.9 1.3 copy-done
  52.2 4.4 %all-to-all-start.3 = ((bf16[8,16,64,128]{3,2,1,0:T(8,128)(2,1)}), bf16[8,16,64,128]{3,2,1,0:T(8,128)(2,1)}, u32[]{:S(2)}, u32[]{:S(2)}) async-start(bf16[8,16,64,128]{3,2,1,0:T(8,128)(2,1)} %hold.2), calls=%async_computation.4 | async-start | bytes 4194304 | tf_op jit(solution)/shard_map/all_to_all | solution.py:396
  56.6 0.0 reduce-scatter.5.cloned.1.call-start
  56.7 6.9 %collective-permute-start.3 = (bf16[8,2,64,128]{3,2,1,0:T(8,128)(2,1)S(1)}, bf16[8,2,64,128]{3,2,1,0:T(8,128)(2,1)S(1)}, u32[]{:S(2)}, u32[]{:S(2)}) collective-permute-start(bf16[8,2,64,128]{3,2,1,0:T(8,128)(2,1)S(1)} %copy-done.21), channel_id=1, source_target_pairs={{0,3},{1,2},{2,1},{3,0},{4,7},{5,6},{6,5},{7,4},{8,11},{9,10},{10,... | collective-permute-start | bytes 786440 | tf_op jit(solution)/shard_map/ppermute | solution.py:376
  63.6 0.6 collective-permute-start.5
  64.3 3.7 %collective-permute-start.6 = (bf16[8,2,64,128]{3,2,1,0:T(8,128)(2,1)S(1)}, bf16[8,2,64,128]{3,2,1,0:T(8,128)(2,1)S(1)}, u32[]{:S(2)}, u32[]{:S(2)}) collective-permute-start(bf16[8,2,64,128]{3,2,1,0:T(8,128)(2,1)S(1)} %copy-done.22), channel_id=1, source_target_pairs={{0,3},{1,2},{2,1},{3,0},{4,7},{5,6},{6,5},{7,4},{8,11},{9,10},{10,... | collective-permute-start | bytes 786440 | tf_op jit(solution)/shard_map/ppermute | solution.py:376
  68.0 15.3 %all-to-all-done.3 = bf16[8,16,64,128]{3,2,1,0:T(8,128)(2,1)} async-done(((bf16[8,16,64,128]{3,2,1,0:T(8,128)(2,1)}), bf16[8,16,64,128]{3,2,1,0:T(8,128)(2,1)}, u32[]{:S(2)}, u32[]{:S(2)}) %all-to-all-start.3) | async-done | bytes 2097184 | tf_op jit(solution)/shard_map/all_to_all | solution.py:396
  83.3 11.1 %correlate.5 = (f32[8,128,512]{2,1,0:T(8,128)}, bf16[4,8,128,512]{3,2,1,0:T(8,128)(2,1)}) custom-call(s32[1]{0:T(128)} %bitcast.where_ref, bf16[8,1,16,64,128]{4,3,2,1,0:T(8,128)(2,1)} %bitcast.21, bf16[8,1,16,64,128]{4,3,2,1,0:T(8,128)(2,1)} %bitcast.12.rest_1_), custom_call_target="tpu_custom_call" | custom-call | flops 4294967296 | bytes 8388608 | tf_op jit(solution)/shard_map/correlate/pallas_call | solution.py:229
  94.4 0.6 copy-done.11
  95.1 0.1 copy-done.5
  95.2 0.1 copy-done.7
  95.3 0.1 copy-done.9
  95.4 0.0 reduce-scatter.3.cloned.1.call-start
  95.5 1.1 copy-done.13
  96.6 0.3 copy-done.14
  97.0 0.2 pad_maximum_fusion
  97.2 29.8 %all_to_all.20.rest_0_ = bf16[8,2,8,64,128]{4,3,2,1,0:T(8,128)(2,1)} all-to-all(bf16[8,2,8,64,128]{4,3,2,1,0:T(8,128)(2,1)S(1)} %pad_maximum_fusion), channel_id=1, replica_groups=mesh['af'=8,'ta'=4] {'af'}, dimensions={0} | all-to-all | bytes 4194304 | tf_op jit(solution)/shard_map/all_to_all | solution.py:396
  126.9 6.7 %correlate.3 = (f32[4,128,512]{2,1,0:T(8,128)}, bf16[4,4,128,512]{3,2,1,0:T(8,128)(2,1)}, bf16[8,2,64,128]{3,2,1,0:T(8,128)(2,1)}) custom-call(s32[1]{0:T(128)} %bitcast.where_ref, bf16[8,2,8,64,128]{4,3,2,1,0:T(8,128)(2,1)} %all_to_all.20.rest_0_, bf16[8,2,64,128]{3,2,1,0:T(8,128)(2,1)} %get-tuple-element.28.rest_1_), custom_call_target="tpu_custom_call", output_to_operand_aliasing={{2}: (2, {})} | custom-call | flops 2147483648 | bytes 4194304 | tf_op jit(solution)/shard_map/correlate/pallas_call | solution.py:229
  133.7 0.0 reduce-scatter.3.cloned.1.call-update
  133.8 0.9 copy-done.15
  134.6 0.1 copy-done.2
  134.7 0.0 copy-done.4
  134.8 0.0 copy-done.12
  134.9 0.0 copy-done.16
  135.0 0.0 copy-done.6
  135.1 0.0 copy-done.8
  135.2 0.0 copy-done.10
  135.2 0.3 copy.10
  135.5 29.8 %all_to_all.21.rest_0_ = bf16[8,8,2,64,128]{4,3,2,1,0:T(8,128)(2,1)} all-to-all(bf16[8,8,2,64,128]{4,3,2,1,0:T(8,128)(2,1)S(1)} %copy.10), channel_id=1, replica_groups=mesh['af'=8,'ta'=4] {'af'}, dimensions={0} | all-to-all | bytes 4194304 | tf_op jit(solution)/shard_map/all_to_all | solution.py:396
  165.3 5.7 %correlate.4 = (f32[1,128,512]{2,1,0:T(8,128)}, bf16[1,128,512]{2,1,0:T(8,128)(2,1)}, bf16[1,128,512]{2,1,0:T(8,128)(2,1)}, bf16[1,128,512]{2,1,0:T(8,128)(2,1)}) custom-call(s32[1]{0:T(128)} %bitcast.where_ref, bf16[8,8,2,64,128]{4,3,2,1,0:T(8,128)(2,1)} %all_to_all.21.rest_0_), custom_call_target="tpu_custom_call" | custom-call | flops 2147483648 | bytes 2621440 | tf_op jit(solution)/shard_map/correlate/pallas_call | solution.py:229
  171.0 2.6 %collective-permute-start.7 = (bf16[1,128,512]{2,1,0:T(8,128)(2,1)}, bf16[1,128,512]{2,1,0:T(8,128)(2,1)S(1)}, u32[]{:S(2)}, u32[]{:S(2)}) collective-permute-start(bf16[1,128,512]{2,1,0:T(8,128)(2,1)} %get-tuple-element.40), channel_id=1, source_target_pairs={{0,1},{1,0},{2,3},{3,2},{4,5},{5,4},{6,7},{7,6},{8,9},{9,8},{10,11... | collective-permute-start | bytes 393224 | tf_op jit(solution)/shard_map/ppermute | solution.py:376
  173.5 4.8 %collective-permute-start.8 = (bf16[1,128,512]{2,1,0:T(8,128)(2,1)}, bf16[1,128,512]{2,1,0:T(8,128)(2,1)S(1)}, u32[]{:S(2)}, u32[]{:S(2)}) collective-permute-start(bf16[1,128,512]{2,1,0:T(8,128)(2,1)} %get-tuple-element.41), channel_id=1, source_target_pairs={{0,2},{1,3},{2,0},{3,1},{4,6},{5,7},{6,4},{7,5},{8,10},{9,11},{10,... | collective-permute-start | bytes 393224 | tf_op jit(solution)/shard_map/ppermute | solution.py:376
  178.4 3.2 %settle.2.refs_6_ = f32[128,16,512]{2,1,0:T(8,128)} custom-call(s32[1]{0:T(128)} %bitcast.where_ref, f32[8,128,512]{2,1,0:T(8,128)} %get-tuple-element.45.refs_0_, bf16[1,8,128,512]{3,2,1,0:T(8,128)(2,1)} %reduce-scatter.5.cloned.1.call-done.refs_1_), custom_call_target="tpu_custom_call" | custom-call | flops 524288 | bytes 5242880 | tf_op jit(solution)/shard_map/settle/pallas_call | solution.py:313
  181.5 9.5 %collective-permute-done.8.refs_4_ = bf16[1,128,512]{2,1,0:T(8,128)(2,1)S(1)} collective-permute-done((bf16[1,128,512]{2,1,0:T(8,128)(2,1)}, bf16[1,128,512]{2,1,0:T(8,128)(2,1)S(1)}, u32[]{:S(2)}, u32[]{:S(2)}) %collective-permute-start.8) | collective-permute-done | bytes 131104 | tf_op jit(solution)/shard_map/ppermute | solution.py:376
  191.0 31.2 %reduce-scatter.3.cloned.1.call-done.refs_1_ = bf16[1,4,128,512]{3,2,1,0:T(8,128)(2,1)} async-done(((bf16[4,4,128,512]{3,2,1,0:T(8,128)(2,1)}), bf16[1,4,128,512]{3,2,1,0:T(8,128)(2,1)}) %reduce-scatter.3.cloned.1.call-update) | async-done | bytes 524304 | tf_op jit(solution)/shard_map/reduce_scatter | solution.py:418
  222.2 3.0 %settle.3 = f32[128,16,512]{2,1,0:T(8,128)} custom-call(s32[1]{0:T(128)} %bitcast.where_ref, f32[4,128,512]{2,1,0:T(8,128)} %get-tuple-element.29.refs_0_, bf16[1,4,128,512]{3,2,1,0:T(8,128)(2,1)} %reduce-scatter.3.cloned.1.call-done.refs_1_, f32[1,128,512]{2,1,0:T(8,128)} %get-tuple-element.39.refs_2_, ...), custom_call_target="tpu_custom_call", output_to_operand_aliasing={{}: (7, {})} | custom-call | flops 524288 | bytes 5242880 | tf_op jit(solution)/shard_map/settle/pallas_call | solution.py:313
  (58 shorter events, 0.4 us)
Async XLA Ops:
  18.9 9.8 %copy-start.26 = (bf16[8,2,64,128]{3,2,1,0:T(8,128)(2,1)S(1)}, bf16[8,2,64,128]{3,2,1,0:T(8,128)(2,1)}, u32[]{:S(2)}) copy-start(bf16[8,2,64,128]{3,2,1,0:T(8,128)(2,1)} %get-tuple-element.32) | copy-start | bytes 786436
  19.0 11.4 %copy-start.25 = (bf16[8,2,64,128]{3,2,1,0:T(8,128)(2,1)S(1)}, bf16[8,2,64,128]{3,2,1,0:T(8,128)(2,1)}, u32[]{:S(2)}) copy-start(bf16[8,2,64,128]{3,2,1,0:T(8,128)(2,1)} %get-tuple-element.33) | copy-start | bytes 786436
  19.0 32.0 %all-to-all-start.2 = ((bf16[8,16,64,128]{3,2,1,0:T(8,128)(2,1)}), bf16[8,16,64,128]{3,2,1,0:T(8,128)(2,1)S(1)}, u32[]{:S(2)}, u32[]{:S(2)}) async-start(bf16[8,16,64,128]{3,2,1,0:T(8,128)(2,1)} %get-tuple-element.43), calls=%async_computation.3 | async-start | bytes 4194304 | tf_op jit(solution)/shard_map/all_to_all | solution.py:396
  25.2 8.7 %collective-permute-start = (bf16[3,64,512]{2,1,0:T(8,128)(2,1)S(1)}, bf16[3,64,512]{2,1,0:T(8,128)(2,1)S(1)}, u32[]{:S(2)}, u32[]{:S(2)}) collective-permute-start(bf16[3,64,512]{2,1,0:T(8,128)(2,1)S(1)} %slice.3), channel_id=1, source_target_pairs={{0,1},{1,2},{2,3},{4,5},{5,6},{6,7},{8,9},{9,10},{10,11},{12,13},{... | collective-permute-start | bytes 589832 | tf_op jit(solution)/shard_map/ppermute | solution.py:343
  28.7 18.2 %collective-permute-start.1 = (bf16[8,2,64,128]{3,2,1,0:T(8,128)(2,1)S(1)}, bf16[8,2,64,128]{3,2,1,0:T(8,128)(2,1)S(1)}, u32[]{:S(2)}, u32[]{:S(2)}) collective-permute-start(bf16[8,2,64,128]{3,2,1,0:T(8,128)(2,1)S(1)} %copy-done.26), channel_id=1, source_target_pairs={{0,1},{1,0},{2,3},{3,2},{4,5},{5,4},{6,7},{7,6},{8,9},{9,8},{10,11... | collective-permute-start | bytes 786440 | tf_op jit(solution)/shard_map/ppermute | solution.py:376
  30.4 16.5 %collective-permute-start.2 = (bf16[8,2,64,128]{3,2,1,0:T(8,128)(2,1)S(1)}, bf16[8,2,64,128]{3,2,1,0:T(8,128)(2,1)S(1)}, u32[]{:S(2)}, u32[]{:S(2)}) collective-permute-start(bf16[8,2,64,128]{3,2,1,0:T(8,128)(2,1)S(1)} %copy-done.25), channel_id=1, source_target_pairs={{0,2},{1,3},{2,0},{3,1},{4,6},{5,7},{6,4},{7,5},{8,10},{9,11},{10,... | collective-permute-start | bytes 786440 | tf_op jit(solution)/shard_map/ppermute | solution.py:376
  33.9 0.7 copy-start.17
  46.9 0.7 copy-start.1
  46.9 0.8 copy-start.3
  47.7 9.0 %copy-start.21 = (bf16[8,2,64,128]{3,2,1,0:T(8,128)(2,1)S(1)}, bf16[8,2,64,128]{3,2,1,0:T(8,128)(2,1)}, u32[]{:S(2)}) copy-start(bf16[8,2,64,128]{3,2,1,0:T(8,128)(2,1)} %get-tuple-element.34) | copy-start | bytes 786436
  47.7 15.9 %copy-start.24 = (bf16[8,2,64,128]{3,2,1,0:T(8,128)(2,1)S(1)}, bf16[8,2,64,128]{3,2,1,0:T(8,128)(2,1)}, u32[]{:S(2)}) copy-start(bf16[8,2,64,128]{3,2,1,0:T(8,128)(2,1)} %get-tuple-element.36) | copy-start | bytes 786436
  47.7 15.9 %copy-start.23 = (bf16[8,2,64,128]{3,2,1,0:T(8,128)(2,1)S(1)}, bf16[8,2,64,128]{3,2,1,0:T(8,128)(2,1)}, u32[]{:S(2)}) copy-start(bf16[8,2,64,128]{3,2,1,0:T(8,128)(2,1)} %get-tuple-element.37) | copy-start | bytes 786436
  47.7 16.6 %copy-start.22 = (bf16[8,2,64,128]{3,2,1,0:T(8,128)(2,1)S(1)}, bf16[8,2,64,128]{3,2,1,0:T(8,128)(2,1)}, u32[]{:S(2)}) copy-start(bf16[8,2,64,128]{3,2,1,0:T(8,128)(2,1)} %get-tuple-element.38) | copy-start | bytes 786436
  50.9 1.3 copy-start
  52.2 31.0 %all-to-all-start.3 = ((bf16[8,16,64,128]{3,2,1,0:T(8,128)(2,1)}), bf16[8,16,64,128]{3,2,1,0:T(8,128)(2,1)}, u32[]{:S(2)}, u32[]{:S(2)}) async-start(bf16[8,16,64,128]{3,2,1,0:T(8,128)(2,1)} %hold.2), calls=%async_computation.4 | async-start | bytes 4194304 | tf_op jit(solution)/shard_map/all_to_all | solution.py:396
  56.6 121.8 %reduce-scatter.5.cloned.1.call-start = ((), (), s32[]{:S(2)}) async-start(), calls=%async_computation.7 | async-start | bytes 5242880 | tf_op jit(solution)/shard_map/reduce_scatter | solution.py:418
  56.7 37.7 %collective-permute-start.3 = (bf16[8,2,64,128]{3,2,1,0:T(8,128)(2,1)S(1)}, bf16[8,2,64,128]{3,2,1,0:T(8,128)(2,1)S(1)}, u32[]{:S(2)}, u32[]{:S(2)}) collective-permute-start(bf16[8,2,64,128]{3,2,1,0:T(8,128)(2,1)S(1)} %copy-done.21), channel_id=1, source_target_pairs={{0,3},{1,2},{2,1},{3,0},{4,7},{5,6},{6,5},{7,4},{8,11},{9,10},{10,... | collective-permute-start | bytes 786440 | tf_op jit(solution)/shard_map/ppermute | solution.py:376
  63.6 30.7 %collective-permute-start.4 = (bf16[8,2,64,128]{3,2,1,0:T(8,128)(2,1)S(1)}, bf16[8,2,64,128]{3,2,1,0:T(8,128)(2,1)S(1)}, u32[]{:S(2)}, u32[]{:S(2)}) collective-permute-start(bf16[8,2,64,128]{3,2,1,0:T(8,128)(2,1)S(1)} %copy-done.24), channel_id=1, source_target_pairs={{0,1},{1,0},{2,3},{3,2},{4,5},{5,4},{6,7},{7,6},{8,9},{9,8},{10,11... | collective-permute-start | bytes 786440 | tf_op jit(solution)/shard_map/ppermute | solution.py:376
  63.6 30.8 %collective-permute-start.5 = (bf16[8,2,64,128]{3,2,1,0:T(8,128)(2,1)S(1)}, bf16[8,2,64,128]{3,2,1,0:T(8,128)(2,1)S(1)}, u32[]{:S(2)}, u32[]{:S(2)}) collective-permute-start(bf16[8,2,64,128]{3,2,1,0:T(8,128)(2,1)S(1)} %copy-done.23), channel_id=1, source_target_pairs={{0,2},{1,3},{2,0},{3,1},{4,6},{5,7},{6,4},{7,5},{8,10},{9,11},{10,... | collective-permute-start | bytes 786440 | tf_op jit(solution)/shard_map/ppermute | solution.py:376
  64.3 30.1 %collective-permute-start.6 = (bf16[8,2,64,128]{3,2,1,0:T(8,128)(2,1)S(1)}, bf16[8,2,64,128]{3,2,1,0:T(8,128)(2,1)S(1)}, u32[]{:S(2)}, u32[]{:S(2)}) collective-permute-start(bf16[8,2,64,128]{3,2,1,0:T(8,128)(2,1)S(1)} %copy-done.22), channel_id=1, source_target_pairs={{0,3},{1,2},{2,1},{3,0},{4,7},{5,6},{6,5},{7,4},{8,11},{9,10},{10,... | collective-permute-start | bytes 786440 | tf_op jit(solution)/shard_map/ppermute | solution.py:376
  94.4 0.7 copy-start.11
  94.4 0.8 copy-start.5
  94.4 0.9 copy-start.7
  94.4 1.0 copy-start.9
  95.4 1.2 copy-start.13
  95.4 1.5 copy-start.14
  95.4 126.8 %reduce-scatter.3.cloned.1.call-start = ((), (), s32[]{:S(2)}) async-start(), calls=%async_computation.6 | async-start | bytes 2621440 | tf_op jit(solution)/shard_map/reduce_scatter | solution.py:418
  133.7 0.9 copy-start.15
  133.7 1.0 copy-start.2
  133.7 1.1 copy-start.4
  133.7 1.2 copy-start.12
  133.7 1.2 copy-start.16
  133.7 1.3 copy-start.6
  133.7 1.4 copy-start.8
  133.7 1.4 copy-start.10
  171.0 10.6 %collective-permute-start.7 = (bf16[1,128,512]{2,1,0:T(8,128)(2,1)}, bf16[1,128,512]{2,1,0:T(8,128)(2,1)S(1)}, u32[]{:S(2)}, u32[]{:S(2)}) collective-permute-start(bf16[1,128,512]{2,1,0:T(8,128)(2,1)} %get-tuple-element.40), channel_id=1, source_target_pairs={{0,1},{1,0},{2,3},{3,2},{4,5},{5,4},{6,7},{7,6},{8,9},{9,8},{10,11... | collective-permute-start | bytes 393224 | tf_op jit(solution)/shard_map/ppermute | solution.py:376
  173.5 17.5 %collective-permute-start.8 = (bf16[1,128,512]{2,1,0:T(8,128)(2,1)}, bf16[1,128,512]{2,1,0:T(8,128)(2,1)S(1)}, u32[]{:S(2)}, u32[]{:S(2)}) collective-permute-start(bf16[1,128,512]{2,1,0:T(8,128)(2,1)} %get-tuple-element.41), channel_id=1, source_target_pairs={{0,2},{1,3},{2,0},{3,1},{4,6},{5,7},{6,4},{7,5},{8,10},{9,11},{10,... | collective-permute-start | bytes 393224 | tf_op jit(solution)/shard_map/ppermute | solution.py:376
  178.4 12.7 %collective-permute-start.9 = (bf16[1,128,512]{2,1,0:T(8,128)(2,1)}, bf16[1,128,512]{2,1,0:T(8,128)(2,1)S(1)}, u32[]{:S(2)}, u32[]{:S(2)}) collective-permute-start(bf16[1,128,512]{2,1,0:T(8,128)(2,1)} %get-tuple-element.42), channel_id=1, source_target_pairs={{0,3},{1,2},{2,1},{3,0},{4,7},{5,6},{6,5},{7,4},{8,11},{9,10},{10,... | collective-permute-start | bytes 393224 | tf_op jit(solution)/shard_map/ppermute | solution.py:376
  181.5 40.7 %copy-start.18 = (bf16[1,128,512]{2,1,0:T(8,128)(2,1)}, bf16[1,128,512]{2,1,0:T(8,128)(2,1)S(1)}, u32[]{:S(2)}) copy-start(bf16[1,128,512]{2,1,0:T(8,128)(2,1)S(1)} %collective-permute-done.7.refs_3_) | copy-start | bytes 393220
  191.0 31.2 %copy-start.19 = (bf16[1,128,512]{2,1,0:T(8,128)(2,1)}, bf16[1,128,512]{2,1,0:T(8,128)(2,1)S(1)}, u32[]{:S(2)}) copy-start(bf16[1,128,512]{2,1,0:T(8,128)(2,1)S(1)} %collective-permute-done.8.refs_4_) | copy-start | bytes 393220
  191.0 31.2 %copy-start.20 = (bf16[1,128,512]{2,1,0:T(8,128)(2,1)}, bf16[1,128,512]{2,1,0:T(8,128)(2,1)S(1)}, u32[]{:S(2)}) copy-start(bf16[1,128,512]{2,1,0:T(8,128)(2,1)S(1)} %collective-permute-done.9.refs_5_) | copy-start | bytes 393220
Sparse Core Ops, SparseCore 0:
  95.6 79.4 reduce-scatter.4
  177.4 44.7 reduce-scatter.2

commit v6 on v5

--- a/solution.py
+++ b/solution.py
@@ -388,9 +388,9 @@
                 spectra[c] += [half[at]] + moving[1 - blocks :]
                 at += blocks
             else:
-                spectra[c].append(hold(half[at], moved[:2]) if moved and c == 0 else half[at])
+                spectra[c].append(hold(half[at], moved[::2]) if moved and c == 0 else half[at])
                 at += 1
-        moved = moved[2:] + moving
+        moved = moved[1:2] + moving
 
     def turn(value):
         return lax.all_to_all(value, "af", split_axis=0, concat_axis=0, tiled=True)

time: 233 us -> 230 us (0.987)
  starting transfers between devices: 34.7 us -> 28.8 us
  waiting for transfers between devices: 61.6 us -> 64.5 us
    ppermute x9, starting transfers between devices: 21.5 us -> 15.5 us  [partners(): lax.ppermute(value, 'ta', [(i, i ^ s + 1) for i in range(blocks)])]
    all_to_all x2, waiting for transfers between devices: 18.5 us -> 22.8 us  [turn(): return lax.all_to_all(value, 'af', split_axis=0, concat_axis=0, tiled=True)]
where the time goes in v6:
time: 230 us; the launch traced here: 229 us
  waiting for transfers between devices  64.5 us (28%)
  blocking collectives  59.5 us (26%)
  Pallas kernels  54.4 us (24%)
  starting transfers between devices  28.8 us (13%)
  between operations  13.7 us (6%)
  local copies, waits for them, and re-layouts  7.92 us (3%)
    all_to_all x2, blocking collectives, turn(): return lax.all_to_all(value, 'af', split_axis=0, concat_axis=0, tiled=True)  59.5 us
    reduce_scatter x2, waiting for transfers between devices, on_device(): came = [lax.psum_scatter(sent[0], 'ta', scatter_dimension=0, tiled=True)]  32 us
    pallas_call x2, Pallas kernels, channelize(): pl.pallas_call(functools.partial(channelizer_body, widths, len(tables)),...  24.7 us
    pallas_call x3, Pallas kernels, correlate(): pl.pallas_call(functools.partial(correlate_body, inputs, scale, len(sourc...  23.5 us
    all_to_all x2, waiting for transfers between devices, turn(): return lax.all_to_all(value, 'af', split_axis=0, concat_axis=0, tiled=True)  22.8 us
    ppermute x9, starting transfers between devices, partners(): lax.ppermute(value, 'ta', [(i, i ^ s + 1) for i in range(blocks)])  15.5 us
    all_to_all x2, starting transfers between devices, turn(): return lax.all_to_all(value, 'af', split_axis=0, concat_axis=0, tiled=True)  9.68 us
    ppermute x9, waiting for transfers between devices, partners(): lax.ppermute(value, 'ta', [(i, i ^ s + 1) for i in range(blocks)])  8.67 us
  transfers between devices with their start and end apart: 14, of which 5 were waited for; matrix products, arithmetic and copies ran while one was open for 1% of the time, Pallas kernels for 17%

profile of v6, /device:TPU:0, one launch (start us, length us, event | category | flops | bytes accessed | tf_op | source)
XLA Modules:
  0.0 229.0 jit_solution(5287285011527043549)
XLA Ops:
  6.5 12.4 %channelizer.2 = (bf16[8,16,64,128]{3,2,1,0:T(8,128)(2,1)}, bf16[8,8,64,128]{3,2,1,0:T(8,128)(2,1)}, bf16[8,2,64,128]{3,2,1,0:T(8,128)(2,1)}, bf16[8,2,64,128]{3...) custom-call(s32[1]{0:T(128)} %bitcast.where_ref, bf16[256,64,512]{2,1,0:T(8,128)(2,1)} %x_ref.3, ...), custom_call_target="tpu_custom_call" | custom-call | flops 2147483648 | bytes 12582912 | tf_op jit(solution)/shard_map/channelizer/pallas_call | solution.py:123
  19.0 5.3 %all-to-all-start.2 = ((bf16[8,16,64,128]{3,2,1,0:T(8,128)(2,1)}), bf16[8,16,64,128]{3,2,1,0:T(8,128)(2,1)S(1)}, u32[]{:S(2)}, u32[]{:S(2)}) async-start(bf16[8,16,64,128]{3,2,1,0:T(8,128)(2,1)} %get-tuple-element.43), calls=%async_computation.3 | async-start | bytes 4194304 | tf_op jit(solution)/shard_map/all_to_all | solution.py:396
  24.3 0.9 slice.3
  25.2 3.5 %collective-permute-start = (bf16[3,64,512]{2,1,0:T(8,128)(2,1)S(1)}, bf16[3,64,512]{2,1,0:T(8,128)(2,1)S(1)}, u32[]{:S(2)}, u32[]{:S(2)}) collective-permute-start(bf16[3,64,512]{2,1,0:T(8,128)(2,1)S(1)} %slice.3), channel_id=1, source_target_pairs={{0,1},{1,2},{2,3},{4,5},{5,6},{6,7},{8,9},{9,10},{10,11},{12,13},{... | collective-permute-start | bytes 589832 | tf_op jit(solution)/shard_map/ppermute | solution.py:343
  28.7 1.6 collective-permute-start.1
  30.4 2.5 %collective-permute-start.3 = (bf16[8,2,64,128]{3,2,1,0:T(8,128)(2,1)S(1)}, bf16[8,2,64,128]{3,2,1,0:T(8,128)(2,1)S(1)}, u32[]{:S(2)}, u32[]{:S(2)}) collective-permute-start(bf16[8,2,64,128]{3,2,1,0:T(8,128)(2,1)S(1)} %copy-done.25), channel_id=1, source_target_pairs={{0,3},{1,2},{2,1},{3,0},{4,7},{5,6},{6,5},{7,4},{8,11},{9,10},{10,... | collective-permute-start | bytes 786440 | tf_op jit(solution)/shard_map/ppermute | solution.py:376
  32.8 1.1 collective-permute-done.halo_ref
  33.9 0.7 copy-done.17
  34.6 12.3 %channelizer.3 = (bf16[8,16,64,128]{3,2,1,0:T(8,128)(2,1)}, bf16[8,8,64,128]{3,2,1,0:T(8,128)(2,1)}, bf16[8,2,64,128]{3,2,1,0:T(8,128)(2,1)}, bf16[8,2,64,128]{3...) custom-call(s32[1]{0:T(128)} %bitcast.where_ref, bf16[256,64,512]{2,1,0:T(8,128)(2,1)} %x_ref.3, ...), custom_call_target="tpu_custom_call" | custom-call | flops 2147483648 | bytes 12582912 | tf_op jit(solution)/shard_map/channelizer/pallas_call | solution.py:123
  47.0 0.7 copy-done.3
  47.6 0.1 copy-done.1
  47.7 3.2 %all-to-all-done.2 = bf16[8,16,64,128]{3,2,1,0:T(8,128)(2,1)S(1)} async-done(((bf16[8,16,64,128]{3,2,1,0:T(8,128)(2,1)}), bf16[8,16,64,128]{3,2,1,0:T(8,128)(2,1)S(1)}, u32[]{:S(2)}, u32[]{:S(2)}) %all-to-all-start.2) | async-done | bytes 2097184 | tf_op jit(solution)/shard_map/all_to_all | solution.py:396
  50.9 1.3 copy-done
  52.2 4.4 %all-to-all-start.3 = ((bf16[8,16,64,128]{3,2,1,0:T(8,128)(2,1)}), bf16[8,16,64,128]{3,2,1,0:T(8,128)(2,1)}, u32[]{:S(2)}, u32[]{:S(2)}) async-start(bf16[8,16,64,128]{3,2,1,0:T(8,128)(2,1)} %hold.2), calls=%async_computation.4 | async-start | bytes 4194304 | tf_op jit(solution)/shard_map/all_to_all | solution.py:396
  56.6 0.0 reduce-scatter.5.cloned.1.call-start
  56.7 2.7 %collective-permute-start.2 = (bf16[8,2,64,128]{3,2,1,0:T(8,128)(2,1)S(1)}, bf16[8,2,64,128]{3,2,1,0:T(8,128)(2,1)S(1)}, u32[]{:S(2)}, u32[]{:S(2)}) collective-permute-start(bf16[8,2,64,128]{3,2,1,0:T(8,128)(2,1)S(1)} %copy-done.21), channel_id=1, source_target_pairs={{0,2},{1,3},{2,0},{3,1},{4,6},{5,7},{6,4},{7,5},{8,10},{9,11},{10,... | collective-permute-start | bytes 786440 | tf_op jit(solution)/shard_map/ppermute | solution.py:376
  59.3 1.6 collective-permute-start.4
  60.9 0.3 collective-permute-start.5
  61.2 2.5 %collective-permute-start.6 = (bf16[8,2,64,128]{3,2,1,0:T(8,128)(2,1)S(1)}, bf16[8,2,64,128]{3,2,1,0:T(8,128)(2,1)S(1)}, u32[]{:S(2)}, u32[]{:S(2)}) collective-permute-start(bf16[8,2,64,128]{3,2,1,0:T(8,128)(2,1)S(1)} %copy-done.22), channel_id=1, source_target_pairs={{0,3},{1,2},{2,1},{3,0},{4,7},{5,6},{6,5},{7,4},{8,11},{9,10},{10,... | collective-permute-start | bytes 786440 | tf_op jit(solution)/shard_map/ppermute | solution.py:376
  63.7 19.5 %all-to-all-done.3 = bf16[8,16,64,128]{3,2,1,0:T(8,128)(2,1)} async-done(((bf16[8,16,64,128]{3,2,1,0:T(8,128)(2,1)}), bf16[8,16,64,128]{3,2,1,0:T(8,128)(2,1)}, u32[]{:S(2)}, u32[]{:S(2)}) %all-to-all-start.3) | async-done | bytes 2097184 | tf_op jit(solution)/shard_map/all_to_all | solution.py:396
  83.3 11.1 %correlate.5 = (f32[8,128,512]{2,1,0:T(8,128)}, bf16[4,8,128,512]{3,2,1,0:T(8,128)(2,1)}) custom-call(s32[1]{0:T(128)} %bitcast.where_ref, bf16[8,1,16,64,128]{4,3,2,1,0:T(8,128)(2,1)} %bitcast.21, bf16[8,1,16,64,128]{4,3,2,1,0:T(8,128)(2,1)} %bitcast.12.rest_1_), custom_call_target="tpu_custom_call" | custom-call | flops 4294967296 | bytes 8388608 | tf_op jit(solution)/shard_map/correlate/pallas_call | solution.py:229
  94.4 0.6 copy-done.11
  95.1 0.1 copy-done.5
  95.2 0.1 copy-done.7
  95.3 0.1 copy-done.9
  95.4 0.0 reduce-scatter.3.cloned.1.call-start
  95.5 1.1 copy-done.13
  96.6 0.3 copy-done.14
  97.0 0.2 pad_maximum_fusion
  97.2 29.8 %all_to_all.20.rest_0_ = bf16[8,2,8,64,128]{4,3,2,1,0:T(8,128)(2,1)} all-to-all(bf16[8,2,8,64,128]{4,3,2,1,0:T(8,128)(2,1)S(1)} %pad_maximum_fusion), channel_id=1, replica_groups=mesh['af'=8,'ta'=4] {'af'}, dimensions={0} | all-to-all | bytes 4194304 | tf_op jit(solution)/shard_map/all_to_all | solution.py:396
  126.9 6.7 %correlate.3 = (f32[4,128,512]{2,1,0:T(8,128)}, bf16[4,4,128,512]{3,2,1,0:T(8,128)(2,1)}, bf16[8,2,64,128]{3,2,1,0:T(8,128)(2,1)}) custom-call(s32[1]{0:T(128)} %bitcast.where_ref, bf16[8,2,8,64,128]{4,3,2,1,0:T(8,128)(2,1)} %all_to_all.20.rest_0_, bf16[8,2,64,128]{3,2,1,0:T(8,128)(2,1)} %get-tuple-element.28.rest_1_), custom_call_target="tpu_custom_call", output_to_operand_aliasing={{2}: (2, {})} | custom-call | flops 2147483648 | bytes 4194304 | tf_op jit(solution)/shard_map/correlate/pallas_call | solution.py:229
  133.8 0.9 copy-done.15
  134.7 0.1 copy-done.4
  134.8 0.0 copy-done.2
  134.9 0.0 copy-done.16
  135.0 0.0 copy-done.6
  135.1 0.0 copy-done.8
  135.2 0.0 copy-done.10
  135.2 0.3 copy.10
  135.5 29.8 %all_to_all.21.rest_0_ = bf16[8,8,2,64,128]{4,3,2,1,0:T(8,128)(2,1)} all-to-all(bf16[8,8,2,64,128]{4,3,2,1,0:T(8,128)(2,1)S(1)} %copy.10), channel_id=1, replica_groups=mesh['af'=8,'ta'=4] {'af'}, dimensions={0} | all-to-all | bytes 4194304 | tf_op jit(solution)/shard_map/all_to_all | solution.py:396
  165.3 5.7 %correlate.4 = (f32[1,128,512]{2,1,0:T(8,128)}, bf16[1,128,512]{2,1,0:T(8,128)(2,1)}, bf16[1,128,512]{2,1,0:T(8,128)(2,1)}, bf16[1,128,512]{2,1,0:T(8,128)(2,1)}) custom-call(s32[1]{0:T(128)} %bitcast.where_ref, bf16[8,8,2,64,128]{4,3,2,1,0:T(8,128)(2,1)} %all_to_all.21.rest_0_), custom_call_target="tpu_custom_call" | custom-call | flops 2147483648 | bytes 2621440 | tf_op jit(solution)/shard_map/correlate/pallas_call | solution.py:229
  171.0 1.5 collective-permute-start.7
  172.5 2.7 %collective-permute-start.8 = (bf16[1,128,512]{2,1,0:T(8,128)(2,1)}, bf16[1,128,512]{2,1,0:T(8,128)(2,1)S(1)}, u32[]{:S(2)}, u32[]{:S(2)}) collective-permute-start(bf16[1,128,512]{2,1,0:T(8,128)(2,1)} %get-tuple-element.41), channel_id=1, source_target_pairs={{0,2},{1,3},{2,0},{3,1},{4,6},{5,7},{6,4},{7,5},{8,10},{9,11},{10,... | collective-permute-start | bytes 393224 | tf_op jit(solution)/shard_map/ppermute | solution.py:376
  175.1 0.2 collective-permute-start.9
  175.4 3.2 %settle.2.refs_6_ = f32[128,16,512]{2,1,0:T(8,128)} custom-call(s32[1]{0:T(128)} %bitcast.where_ref, f32[8,128,512]{2,1,0:T(8,128)} %get-tuple-element.45.refs_0_, bf16[1,8,128,512]{3,2,1,0:T(8,128)(2,1)} %reduce-scatter.5.cloned.1.call-done.refs_1_), custom_call_target="tpu_custom_call" | custom-call | flops 524288 | bytes 5242880 | tf_op jit(solution)/shard_map/settle/pallas_call | solution.py:313
  178.5 8.7 %collective-permute-done.8.refs_4_ = bf16[1,128,512]{2,1,0:T(8,128)(2,1)S(1)} collective-permute-done((bf16[1,128,512]{2,1,0:T(8,128)(2,1)}, bf16[1,128,512]{2,1,0:T(8,128)(2,1)S(1)}, u32[]{:S(2)}, u32[]{:S(2)}) %collective-permute-start.8) | collective-permute-done | bytes 131104 | tf_op jit(solution)/shard_map/ppermute | solution.py:376
  187.2 32.0 %reduce-scatter.3.cloned.1.call-done.refs_1_ = bf16[1,4,128,512]{3,2,1,0:T(8,128)(2,1)} async-done(((bf16[4,4,128,512]{3,2,1,0:T(8,128)(2,1)}), bf16[1,4,128,512]{3,2,1,0:T(8,128)(2,1)}) %reduce-scatter.3.cloned.1.call-update) | async-done | bytes 524304 | tf_op jit(solution)/shard_map/reduce_scatter | solution.py:418
  219.2 3.0 %settle.3 = f32[128,16,512]{2,1,0:T(8,128)} custom-call(s32[1]{0:T(128)} %bitcast.where_ref, f32[4,128,512]{2,1,0:T(8,128)} %get-tuple-element.29.refs_0_, bf16[1,4,128,512]{3,2,1,0:T(8,128)(2,1)} %reduce-scatter.3.cloned.1.call-done.refs_1_, f32[1,128,512]{2,1,0:T(8,128)} %get-tuple-element.39.refs_2_, ...), custom_call_target="tpu_custom_call", output_to_operand_aliasing={{}: (7, {})} | custom-call | flops 524288 | bytes 5242880 | tf_op jit(solution)/shard_map/settle/pallas_call | solution.py:313
  (58 shorter events, 0.4 us)
Async XLA Ops:
  18.9 9.8 %copy-start.26 = (bf16[8,2,64,128]{3,2,1,0:T(8,128)(2,1)S(1)}, bf16[8,2,64,128]{3,2,1,0:T(8,128)(2,1)}, u32[]{:S(2)}) copy-start(bf16[8,2,64,128]{3,2,1,0:T(8,128)(2,1)} %get-tuple-element.32) | copy-start | bytes 786436
  19.0 11.4 %copy-start.25 = (bf16[8,2,64,128]{3,2,1,0:T(8,128)(2,1)S(1)}, bf16[8,2,64,128]{3,2,1,0:T(8,128)(2,1)}, u32[]{:S(2)}) copy-start(bf16[8,2,64,128]{3,2,1,0:T(8,128)(2,1)} %get-tuple-element.34) | copy-start | bytes 786436
  19.0 32.0 %all-to-all-start.2 = ((bf16[8,16,64,128]{3,2,1,0:T(8,128)(2,1)}), bf16[8,16,64,128]{3,2,1,0:T(8,128)(2,1)S(1)}, u32[]{:S(2)}, u32[]{:S(2)}) async-start(bf16[8,16,64,128]{3,2,1,0:T(8,128)(2,1)} %get-tuple-element.43), calls=%async_computation.3 | async-start | bytes 4194304 | tf_op jit(solution)/shard_map/all_to_all | solution.py:396
  25.2 8.7 %collective-permute-start = (bf16[3,64,512]{2,1,0:T(8,128)(2,1)S(1)}, bf16[3,64,512]{2,1,0:T(8,128)(2,1)S(1)}, u32[]{:S(2)}, u32[]{:S(2)}) collective-permute-start(bf16[3,64,512]{2,1,0:T(8,128)(2,1)S(1)} %slice.3), channel_id=1, source_target_pairs={{0,1},{1,2},{2,3},{4,5},{5,6},{6,7},{8,9},{9,10},{10,11},{12,13},{... | collective-permute-start | bytes 589832 | tf_op jit(solution)/shard_map/ppermute | solution.py:343
  28.7 18.2 %collective-permute-start.1 = (bf16[8,2,64,128]{3,2,1,0:T(8,128)(2,1)S(1)}, bf16[8,2,64,128]{3,2,1,0:T(8,128)(2,1)S(1)}, u32[]{:S(2)}, u32[]{:S(2)}) collective-permute-start(bf16[8,2,64,128]{3,2,1,0:T(8,128)(2,1)S(1)} %copy-done.26), channel_id=1, source_target_pairs={{0,1},{1,0},{2,3},{3,2},{4,5},{5,4},{6,7},{7,6},{8,9},{9,8},{10,11... | collective-permute-start | bytes 786440 | tf_op jit(solution)/shard_map/ppermute | solution.py:376
  30.4 16.6 %collective-permute-start.3 = (bf16[8,2,64,128]{3,2,1,0:T(8,128)(2,1)S(1)}, bf16[8,2,64,128]{3,2,1,0:T(8,128)(2,1)S(1)}, u32[]{:S(2)}, u32[]{:S(2)}) collective-permute-start(bf16[8,2,64,128]{3,2,1,0:T(8,128)(2,1)S(1)} %copy-done.25), channel_id=1, source_target_pairs={{0,3},{1,2},{2,1},{3,0},{4,7},{5,6},{6,5},{7,4},{8,11},{9,10},{10,... | collective-permute-start | bytes 786440 | tf_op jit(solution)/shard_map/ppermute | solution.py:376
  33.9 0.7 copy-start.17
  46.9 0.7 copy-start.3
  46.9 0.8 copy-start.1
  47.7 9.0 %copy-start.21 = (bf16[8,2,64,128]{3,2,1,0:T(8,128)(2,1)S(1)}, bf16[8,2,64,128]{3,2,1,0:T(8,128)(2,1)}, u32[]{:S(2)}) copy-start(bf16[8,2,64,128]{3,2,1,0:T(8,128)(2,1)} %get-tuple-element.33) | copy-start | bytes 786436
  47.7 11.6 %copy-start.24 = (bf16[8,2,64,128]{3,2,1,0:T(8,128)(2,1)S(1)}, bf16[8,2,64,128]{3,2,1,0:T(8,128)(2,1)}, u32[]{:S(2)}) copy-start(bf16[8,2,64,128]{3,2,1,0:T(8,128)(2,1)} %get-tuple-element.36) | copy-start | bytes 786436
  47.7 13.2 %copy-start.23 = (bf16[8,2,64,128]{3,2,1,0:T(8,128)(2,1)S(1)}, bf16[8,2,64,128]{3,2,1,0:T(8,128)(2,1)}, u32[]{:S(2)}) copy-start(bf16[8,2,64,128]{3,2,1,0:T(8,128)(2,1)} %get-tuple-element.37) | copy-start | bytes 786436
  47.7 13.5 %copy-start.22 = (bf16[8,2,64,128]{3,2,1,0:T(8,128)(2,1)S(1)}, bf16[8,2,64,128]{3,2,1,0:T(8,128)(2,1)}, u32[]{:S(2)}) copy-start(bf16[8,2,64,128]{3,2,1,0:T(8,128)(2,1)} %get-tuple-element.38) | copy-start | bytes 786436
  50.9 1.3 copy-start
  52.2 31.0 %all-to-all-start.3 = ((bf16[8,16,64,128]{3,2,1,0:T(8,128)(2,1)}), bf16[8,16,64,128]{3,2,1,0:T(8,128)(2,1)}, u32[]{:S(2)}, u32[]{:S(2)}) async-start(bf16[8,16,64,128]{3,2,1,0:T(8,128)(2,1)} %hold.2), calls=%async_computation.4 | async-start | bytes 4194304 | tf_op jit(solution)/shard_map/all_to_all | solution.py:396
  56.6 118.7 %reduce-scatter.5.cloned.1.call-start = ((), (), s32[]{:S(2)}) async-start(), calls=%async_computation.7 | async-start | bytes 5242880 | tf_op jit(solution)/shard_map/reduce_scatter | solution.py:418
  56.7 37.7 %collective-permute-start.2 = (bf16[8,2,64,128]{3,2,1,0:T(8,128)(2,1)S(1)}, bf16[8,2,64,128]{3,2,1,0:T(8,128)(2,1)S(1)}, u32[]{:S(2)}, u32[]{:S(2)}) collective-permute-start(bf16[8,2,64,128]{3,2,1,0:T(8,128)(2,1)S(1)} %copy-done.21), channel_id=1, source_target_pairs={{0,2},{1,3},{2,0},{3,1},{4,6},{5,7},{6,4},{7,5},{8,10},{9,11},{10,... | collective-permute-start | bytes 786440 | tf_op jit(solution)/shard_map/ppermute | solution.py:376
  59.3 35.0 %collective-permute-start.4 = (bf16[8,2,64,128]{3,2,1,0:T(8,128)(2,1)S(1)}, bf16[8,2,64,128]{3,2,1,0:T(8,128)(2,1)S(1)}, u32[]{:S(2)}, u32[]{:S(2)}) collective-permute-start(bf16[8,2,64,128]{3,2,1,0:T(8,128)(2,1)S(1)} %copy-done.24), channel_id=1, source_target_pairs={{0,1},{1,0},{2,3},{3,2},{4,5},{5,4},{6,7},{7,6},{8,9},{9,8},{10,11... | collective-permute-start | bytes 786440 | tf_op jit(solution)/shard_map/ppermute | solution.py:376
  60.9 33.5 %collective-permute-start.5 = (bf16[8,2,64,128]{3,2,1,0:T(8,128)(2,1)S(1)}, bf16[8,2,64,128]{3,2,1,0:T(8,128)(2,1)S(1)}, u32[]{:S(2)}, u32[]{:S(2)}) collective-permute-start(bf16[8,2,64,128]{3,2,1,0:T(8,128)(2,1)S(1)} %copy-done.23), channel_id=1, source_target_pairs={{0,2},{1,3},{2,0},{3,1},{4,6},{5,7},{6,4},{7,5},{8,10},{9,11},{10,... | collective-permute-start | bytes 786440 | tf_op jit(solution)/shard_map/ppermute | solution.py:376
  61.2 33.2 %collective-permute-start.6 = (bf16[8,2,64,128]{3,2,1,0:T(8,128)(2,1)S(1)}, bf16[8,2,64,128]{3,2,1,0:T(8,128)(2,1)S(1)}, u32[]{:S(2)}, u32[]{:S(2)}) collective-permute-start(bf16[8,2,64,128]{3,2,1,0:T(8,128)(2,1)S(1)} %copy-done.22), channel_id=1, source_target_pairs={{0,3},{1,2},{2,1},{3,0},{4,7},{5,6},{6,5},{7,4},{8,11},{9,10},{10,... | collective-permute-start | bytes 786440 | tf_op jit(solution)/shard_map/ppermute | solution.py:376
  94.4 0.7 copy-start.11
  94.4 0.8 copy-start.5
  94.4 0.9 copy-start.7
  94.4 1.0 copy-start.9
  95.4 1.2 copy-start.13
  95.4 1.5 copy-start.14
  95.4 123.8 %reduce-scatter.3.cloned.1.call-start = ((), (), s32[]{:S(2)}) async-start(), calls=%async_computation.6 | async-start | bytes 2621440 | tf_op jit(solution)/shard_map/reduce_scatter | solution.py:418
  133.7 0.9 copy-start.15
  133.7 1.0 copy-start.4
  133.7 1.1 copy-start.12
  133.7 1.2 copy-start.2
  133.7 1.2 copy-start.16
  133.7 1.3 copy-start.6
  133.7 1.4 copy-start.8
  133.8 1.4 copy-start.10
  171.0 7.6 %collective-permute-start.7 = (bf16[1,128,512]{2,1,0:T(8,128)(2,1)}, bf16[1,128,512]{2,1,0:T(8,128)(2,1)S(1)}, u32[]{:S(2)}, u32[]{:S(2)}) collective-permute-start(bf16[1,128,512]{2,1,0:T(8,128)(2,1)} %get-tuple-element.40), channel_id=1, source_target_pairs={{0,1},{1,0},{2,3},{3,2},{4,5},{5,4},{6,7},{7,6},{8,9},{9,8},{10,11... | collective-permute-start | bytes 393224 | tf_op jit(solution)/shard_map/ppermute | solution.py:376
  172.5 14.7 %collective-permute-start.8 = (bf16[1,128,512]{2,1,0:T(8,128)(2,1)}, bf16[1,128,512]{2,1,0:T(8,128)(2,1)S(1)}, u32[]{:S(2)}, u32[]{:S(2)}) collective-permute-start(bf16[1,128,512]{2,1,0:T(8,128)(2,1)} %get-tuple-element.41), channel_id=1, source_target_pairs={{0,2},{1,3},{2,0},{3,1},{4,6},{5,7},{6,4},{7,5},{8,10},{9,11},{10,... | collective-permute-start | bytes 393224 | tf_op jit(solution)/shard_map/ppermute | solution.py:376
  175.1 12.0 %collective-permute-start.9 = (bf16[1,128,512]{2,1,0:T(8,128)(2,1)}, bf16[1,128,512]{2,1,0:T(8,128)(2,1)S(1)}, u32[]{:S(2)}, u32[]{:S(2)}) collective-permute-start(bf16[1,128,512]{2,1,0:T(8,128)(2,1)} %get-tuple-element.42), channel_id=1, source_target_pairs={{0,3},{1,2},{2,1},{3,0},{4,7},{5,6},{6,5},{7,4},{8,11},{9,10},{10,... | collective-permute-start | bytes 393224 | tf_op jit(solution)/shard_map/ppermute | solution.py:376
  178.5 40.7 %copy-start.18 = (bf16[1,128,512]{2,1,0:T(8,128)(2,1)}, bf16[1,128,512]{2,1,0:T(8,128)(2,1)S(1)}, u32[]{:S(2)}) copy-start(bf16[1,128,512]{2,1,0:T(8,128)(2,1)S(1)} %collective-permute-done.7.refs_3_) | copy-start | bytes 393220
  187.2 32.0 %copy-start.19 = (bf16[1,128,512]{2,1,0:T(8,128)(2,1)}, bf16[1,128,512]{2,1,0:T(8,128)(2,1)S(1)}, u32[]{:S(2)}) copy-start(bf16[1,128,512]{2,1,0:T(8,128)(2,1)S(1)} %collective-permute-done.8.refs_4_) | copy-start | bytes 393220
  187.2 32.0 %copy-start.20 = (bf16[1,128,512]{2,1,0:T(8,128)(2,1)}, bf16[1,128,512]{2,1,0:T(8,128)(2,1)S(1)}, u32[]{:S(2)}) copy-start(bf16[1,128,512]{2,1,0:T(8,128)(2,1)S(1)} %collective-permute-done.9.refs_5_) | copy-start | bytes 393220
Sparse Core Ops, SparseCore 0:
  95.6 76.7 reduce-scatter.4
  174.7 44.4 reduce-scatter.2

commit v7 on v6

--- a/solution.py
+++ b/solution.py
@@ -13,7 +13,7 @@
 TAPS = 4
 LANES = 128
 ROWS = 16
-PAD = 8
+PAD = 4
 PER = (2, 1)
 VMEM = 60 * 1024 * 1024
 

time: 230 us -> 229 us (level)
  no operation moved by 1% of the time
where the time goes in v7:
time: 229 us; the launch traced here: 228 us
  waiting for transfers between devices  65.4 us (29%)
  blocking collectives  59.5 us (26%)
  Pallas kernels  52.7 us (23%)
  starting transfers between devices  28.8 us (13%)
  between operations  13.7 us (6%)
  local copies, waits for them, and re-layouts  7.92 us (3%)
    all_to_all x2, blocking collectives, turn(): return lax.all_to_all(value, 'af', split_axis=0, concat_axis=0, tiled=True)  59.5 us
    reduce_scatter x2, waiting for transfers between devices, on_device(): came = [lax.psum_scatter(sent[0], 'ta', scatter_dimension=0, tiled=True)]  32 us
    all_to_all x2, waiting for transfers between devices, turn(): return lax.all_to_all(value, 'af', split_axis=0, concat_axis=0, tiled=True)  23.6 us
    pallas_call x3, Pallas kernels, correlate(): pl.pallas_call(functools.partial(correlate_body, inputs, scale, len(sourc...  23.4 us
    pallas_call x2, Pallas kernels, channelize(): pl.pallas_call(functools.partial(channelizer_body, widths, len(tables)),...  23.1 us
    ppermute x9, starting transfers between devices, partners(): lax.ppermute(value, 'ta', [(i, i ^ s + 1) for i in range(blocks)])  15.5 us
    all_to_all x2, starting transfers between devices, turn(): return lax.all_to_all(value, 'af', split_axis=0, concat_axis=0, tiled=True)  9.68 us
    ppermute x9, waiting for transfers between devices, partners(): lax.ppermute(value, 'ta', [(i, i ^ s + 1) for i in range(blocks)])  8.73 us
  transfers between devices with their start and end apart: 14, of which 5 were waited for; matrix products, arithmetic and copies ran while one was open for 1% of the time, Pallas kernels for 17%

profile of v7, /device:TPU:0, one launch (start us, length us, event | category | flops | bytes accessed | tf_op | source)
XLA Modules:
  0.0 228.2 jit_solution(15511653490264120368)
XLA Ops:
  6.5 11.6 %channelizer.2 = (bf16[8,16,64,128]{3,2,1,0:T(8,128)(2,1)}, bf16[8,8,64,128]{3,2,1,0:T(8,128)(2,1)}, bf16[8,2,64,128]{3,2,1,0:T(8,128)(2,1)}, bf16[8,2,64,128]{3...) custom-call(s32[1]{0:T(128)} %bitcast.where_ref, bf16[256,64,512]{2,1,0:T(8,128)(2,1)} %x_ref.3, ...), custom_call_target="tpu_custom_call" | custom-call | flops 2147483648 | bytes 12582912 | tf_op jit(solution)/shard_map/channelizer/pallas_call | solution.py:123
  18.1 5.3 %all-to-all-start.2 = ((bf16[8,16,64,128]{3,2,1,0:T(8,128)(2,1)}), bf16[8,16,64,128]{3,2,1,0:T(8,128)(2,1)S(1)}, u32[]{:S(2)}, u32[]{:S(2)}) async-start(bf16[8,16,64,128]{3,2,1,0:T(8,128)(2,1)} %get-tuple-element.43), calls=%async_computation.3 | async-start | bytes 4194304 | tf_op jit(solution)/shard_map/all_to_all | solution.py:396
  23.5 0.9 slice.3
  24.4 3.5 %collective-permute-start = (bf16[3,64,512]{2,1,0:T(8,128)(2,1)S(1)}, bf16[3,64,512]{2,1,0:T(8,128)(2,1)S(1)}, u32[]{:S(2)}, u32[]{:S(2)}) collective-permute-start(bf16[3,64,512]{2,1,0:T(8,128)(2,1)S(1)} %slice.3), channel_id=1, source_target_pairs={{0,1},{1,2},{2,3},{4,5},{5,6},{6,7},{8,9},{9,10},{10,11},{12,13},{... | collective-permute-start | bytes 589832 | tf_op jit(solution)/shard_map/ppermute | solution.py:343
  27.9 1.6 collective-permute-start.1
  29.5 2.5 %collective-permute-start.3 = (bf16[8,2,64,128]{3,2,1,0:T(8,128)(2,1)S(1)}, bf16[8,2,64,128]{3,2,1,0:T(8,128)(2,1)S(1)}, u32[]{:S(2)}, u32[]{:S(2)}) collective-permute-start(bf16[8,2,64,128]{3,2,1,0:T(8,128)(2,1)S(1)} %copy-done.25), channel_id=1, source_target_pairs={{0,3},{1,2},{2,1},{3,0},{4,7},{5,6},{6,5},{7,4},{8,11},{9,10},{10,... | collective-permute-start | bytes 786440 | tf_op jit(solution)/shard_map/ppermute | solution.py:376
  32.0 1.1 collective-permute-done.halo_ref
  33.1 0.7 copy-done.17
  33.8 11.5 %channelizer.3 = (bf16[8,16,64,128]{3,2,1,0:T(8,128)(2,1)}, bf16[8,8,64,128]{3,2,1,0:T(8,128)(2,1)}, bf16[8,2,64,128]{3,2,1,0:T(8,128)(2,1)}, bf16[8,2,64,128]{3...) custom-call(s32[1]{0:T(128)} %bitcast.where_ref, bf16[256,64,512]{2,1,0:T(8,128)(2,1)} %x_ref.3, ...), custom_call_target="tpu_custom_call" | custom-call | flops 2147483648 | bytes 12582912 | tf_op jit(solution)/shard_map/channelizer/pallas_call | solution.py:123
  45.3 0.7 copy-done.3
  46.0 0.1 copy-done.1
  46.1 4.0 %all-to-all-done.2 = bf16[8,16,64,128]{3,2,1,0:T(8,128)(2,1)S(1)} async-done(((bf16[8,16,64,128]{3,2,1,0:T(8,128)(2,1)}), bf16[8,16,64,128]{3,2,1,0:T(8,128)(2,1)S(1)}, u32[]{:S(2)}, u32[]{:S(2)}) %all-to-all-start.2) | async-done | bytes 2097184 | tf_op jit(solution)/shard_map/all_to_all | solution.py:396
  50.1 1.3 copy-done
  51.4 4.4 %all-to-all-start.3 = ((bf16[8,16,64,128]{3,2,1,0:T(8,128)(2,1)}), bf16[8,16,64,128]{3,2,1,0:T(8,128)(2,1)}, u32[]{:S(2)}, u32[]{:S(2)}) async-start(bf16[8,16,64,128]{3,2,1,0:T(8,128)(2,1)} %hold.2), calls=%async_computation.4 | async-start | bytes 4194304 | tf_op jit(solution)/shard_map/all_to_all | solution.py:396
  55.8 0.0 reduce-scatter.5.cloned.1.call-start
  55.9 2.7 %collective-permute-start.2 = (bf16[8,2,64,128]{3,2,1,0:T(8,128)(2,1)S(1)}, bf16[8,2,64,128]{3,2,1,0:T(8,128)(2,1)S(1)}, u32[]{:S(2)}, u32[]{:S(2)}) collective-permute-start(bf16[8,2,64,128]{3,2,1,0:T(8,128)(2,1)S(1)} %copy-done.21), channel_id=1, source_target_pairs={{0,2},{1,3},{2,0},{3,1},{4,6},{5,7},{6,4},{7,5},{8,10},{9,11},{10,... | collective-permute-start | bytes 786440 | tf_op jit(solution)/shard_map/ppermute | solution.py:376
  58.5 1.6 collective-permute-start.4
  60.1 0.3 collective-permute-start.5
  60.4 2.5 %collective-permute-start.6 = (bf16[8,2,64,128]{3,2,1,0:T(8,128)(2,1)S(1)}, bf16[8,2,64,128]{3,2,1,0:T(8,128)(2,1)S(1)}, u32[]{:S(2)}, u32[]{:S(2)}) collective-permute-start(bf16[8,2,64,128]{3,2,1,0:T(8,128)(2,1)S(1)} %copy-done.22), channel_id=1, source_target_pairs={{0,3},{1,2},{2,1},{3,0},{4,7},{5,6},{6,5},{7,4},{8,11},{9,10},{10,... | collective-permute-start | bytes 786440 | tf_op jit(solution)/shard_map/ppermute | solution.py:376
  62.9 19.5 %all-to-all-done.3 = bf16[8,16,64,128]{3,2,1,0:T(8,128)(2,1)} async-done(((bf16[8,16,64,128]{3,2,1,0:T(8,128)(2,1)}), bf16[8,16,64,128]{3,2,1,0:T(8,128)(2,1)}, u32[]{:S(2)}, u32[]{:S(2)}) %all-to-all-start.3) | async-done | bytes 2097184 | tf_op jit(solution)/shard_map/all_to_all | solution.py:396
  82.4 11.0 %correlate.5 = (f32[8,128,512]{2,1,0:T(8,128)}, bf16[4,8,128,512]{3,2,1,0:T(8,128)(2,1)}) custom-call(s32[1]{0:T(128)} %bitcast.where_ref, bf16[8,1,16,64,128]{4,3,2,1,0:T(8,128)(2,1)} %bitcast.21, bf16[8,1,16,64,128]{4,3,2,1,0:T(8,128)(2,1)} %bitcast.12.rest_1_), custom_call_target="tpu_custom_call" | custom-call | flops 4294967296 | bytes 8388608 | tf_op jit(solution)/shard_map/correlate/pallas_call | solution.py:229
  93.6 0.6 copy-done.11
  94.2 0.1 copy-done.5
  94.3 0.1 copy-done.7
  94.4 0.1 copy-done.9
  94.6 0.0 reduce-scatter.3.cloned.1.call-start
  94.6 1.1 copy-done.13
  95.8 0.3 copy-done.14
  96.1 0.2 pad_maximum_fusion
  96.3 29.8 %all_to_all.20.rest_0_ = bf16[8,2,8,64,128]{4,3,2,1,0:T(8,128)(2,1)} all-to-all(bf16[8,2,8,64,128]{4,3,2,1,0:T(8,128)(2,1)S(1)} %pad_maximum_fusion), channel_id=1, replica_groups=mesh['af'=8,'ta'=4] {'af'}, dimensions={0} | all-to-all | bytes 4194304 | tf_op jit(solution)/shard_map/all_to_all | solution.py:396
  126.1 6.7 %correlate.3 = (f32[4,128,512]{2,1,0:T(8,128)}, bf16[4,4,128,512]{3,2,1,0:T(8,128)(2,1)}, bf16[8,2,64,128]{3,2,1,0:T(8,128)(2,1)}) custom-call(s32[1]{0:T(128)} %bitcast.where_ref, bf16[8,2,8,64,128]{4,3,2,1,0:T(8,128)(2,1)} %all_to_all.20.rest_0_, bf16[8,2,64,128]{3,2,1,0:T(8,128)(2,1)} %get-tuple-element.28.rest_1_), custom_call_target="tpu_custom_call", output_to_operand_aliasing={{2}: (2, {})} | custom-call | flops 2147483648 | bytes 4194304 | tf_op jit(solution)/shard_map/correlate/pallas_call | solution.py:229
  132.9 0.9 copy-done.15
  133.8 0.1 copy-done.4
  134.0 0.0 copy-done.2
  134.0 0.0 copy-done.16
  134.1 0.0 copy-done.6
  134.2 0.0 copy-done.8
  134.3 0.0 copy-done.10
  134.4 0.3 copy.10
  134.7 29.8 %all_to_all.21.rest_0_ = bf16[8,8,2,64,128]{4,3,2,1,0:T(8,128)(2,1)} all-to-all(bf16[8,8,2,64,128]{4,3,2,1,0:T(8,128)(2,1)S(1)} %copy.10), channel_id=1, replica_groups=mesh['af'=8,'ta'=4] {'af'}, dimensions={0} | all-to-all | bytes 4194304 | tf_op jit(solution)/shard_map/all_to_all | solution.py:396
  164.4 5.7 %correlate.4 = (f32[1,128,512]{2,1,0:T(8,128)}, bf16[1,128,512]{2,1,0:T(8,128)(2,1)}, bf16[1,128,512]{2,1,0:T(8,128)(2,1)}, bf16[1,128,512]{2,1,0:T(8,128)(2,1)}) custom-call(s32[1]{0:T(128)} %bitcast.where_ref, bf16[8,8,2,64,128]{4,3,2,1,0:T(8,128)(2,1)} %all_to_all.21.rest_0_), custom_call_target="tpu_custom_call" | custom-call | flops 2147483648 | bytes 2621440 | tf_op jit(solution)/shard_map/correlate/pallas_call | solution.py:229
  170.1 1.6 collective-permute-start.7
  171.7 2.7 %collective-permute-start.8 = (bf16[1,128,512]{2,1,0:T(8,128)(2,1)}, bf16[1,128,512]{2,1,0:T(8,128)(2,1)S(1)}, u32[]{:S(2)}, u32[]{:S(2)}) collective-permute-start(bf16[1,128,512]{2,1,0:T(8,128)(2,1)} %get-tuple-element.41), channel_id=1, source_target_pairs={{0,2},{1,3},{2,0},{3,1},{4,6},{5,7},{6,4},{7,5},{8,10},{9,11},{10,... | collective-permute-start | bytes 393224 | tf_op jit(solution)/shard_map/ppermute | solution.py:376
  174.3 0.1 collective-permute-start.9
  174.5 3.2 %settle.2.refs_6_ = f32[128,16,512]{2,1,0:T(8,128)} custom-call(s32[1]{0:T(128)} %bitcast.where_ref, f32[8,128,512]{2,1,0:T(8,128)} %get-tuple-element.45.refs_0_, bf16[1,8,128,512]{3,2,1,0:T(8,128)(2,1)} %reduce-scatter.5.cloned.1.call-done.refs_1_), custom_call_target="tpu_custom_call" | custom-call | flops 524288 | bytes 5242880 | tf_op jit(solution)/shard_map/settle/pallas_call | solution.py:313
  177.6 8.7 %collective-permute-done.8.refs_4_ = bf16[1,128,512]{2,1,0:T(8,128)(2,1)S(1)} collective-permute-done((bf16[1,128,512]{2,1,0:T(8,128)(2,1)}, bf16[1,128,512]{2,1,0:T(8,128)(2,1)S(1)}, u32[]{:S(2)}, u32[]{:S(2)}) %collective-permute-start.8) | collective-permute-done | bytes 131104 | tf_op jit(solution)/shard_map/ppermute | solution.py:376
  186.4 32.0 %reduce-scatter.3.cloned.1.call-done.refs_1_ = bf16[1,4,128,512]{3,2,1,0:T(8,128)(2,1)} async-done(((bf16[4,4,128,512]{3,2,1,0:T(8,128)(2,1)}), bf16[1,4,128,512]{3,2,1,0:T(8,128)(2,1)}) %reduce-scatter.3.cloned.1.call-update) | async-done | bytes 524304 | tf_op jit(solution)/shard_map/reduce_scatter | solution.py:418
  218.4 3.0 %settle.3 = f32[128,16,512]{2,1,0:T(8,128)} custom-call(s32[1]{0:T(128)} %bitcast.where_ref, f32[4,128,512]{2,1,0:T(8,128)} %get-tuple-element.29.refs_0_, bf16[1,4,128,512]{3,2,1,0:T(8,128)(2,1)} %reduce-scatter.3.cloned.1.call-done.refs_1_, f32[1,128,512]{2,1,0:T(8,128)} %get-tuple-element.39.refs_2_, ...), custom_call_target="tpu_custom_call", output_to_operand_aliasing={{}: (7, {})} | custom-call | flops 524288 | bytes 5242880 | tf_op jit(solution)/shard_map/settle/pallas_call | solution.py:313
  (58 shorter events, 0.4 us)
Async XLA Ops:
  18.1 9.8 %copy-start.26 = (bf16[8,2,64,128]{3,2,1,0:T(8,128)(2,1)S(1)}, bf16[8,2,64,128]{3,2,1,0:T(8,128)(2,1)}, u32[]{:S(2)}) copy-start(bf16[8,2,64,128]{3,2,1,0:T(8,128)(2,1)} %get-tuple-element.32) | copy-start | bytes 786436
  18.1 11.4 %copy-start.25 = (bf16[8,2,64,128]{3,2,1,0:T(8,128)(2,1)S(1)}, bf16[8,2,64,128]{3,2,1,0:T(8,128)(2,1)}, u32[]{:S(2)}) copy-start(bf16[8,2,64,128]{3,2,1,0:T(8,128)(2,1)} %get-tuple-element.34) | copy-start | bytes 786436
  18.1 32.0 %all-to-all-start.2 = ((bf16[8,16,64,128]{3,2,1,0:T(8,128)(2,1)}), bf16[8,16,64,128]{3,2,1,0:T(8,128)(2,1)S(1)}, u32[]{:S(2)}, u32[]{:S(2)}) async-start(bf16[8,16,64,128]{3,2,1,0:T(8,128)(2,1)} %get-tuple-element.43), calls=%async_computation.3 | async-start | bytes 4194304 | tf_op jit(solution)/shard_map/all_to_all | solution.py:396
  24.4 8.7 %collective-permute-start = (bf16[3,64,512]{2,1,0:T(8,128)(2,1)S(1)}, bf16[3,64,512]{2,1,0:T(8,128)(2,1)S(1)}, u32[]{:S(2)}, u32[]{:S(2)}) collective-permute-start(bf16[3,64,512]{2,1,0:T(8,128)(2,1)S(1)} %slice.3), channel_id=1, source_target_pairs={{0,1},{1,2},{2,3},{4,5},{5,6},{6,7},{8,9},{9,10},{10,11},{12,13},{... | collective-permute-start | bytes 589832 | tf_op jit(solution)/shard_map/ppermute | solution.py:343
  27.9 17.4 %collective-permute-start.1 = (bf16[8,2,64,128]{3,2,1,0:T(8,128)(2,1)S(1)}, bf16[8,2,64,128]{3,2,1,0:T(8,128)(2,1)S(1)}, u32[]{:S(2)}, u32[]{:S(2)}) collective-permute-start(bf16[8,2,64,128]{3,2,1,0:T(8,128)(2,1)S(1)} %copy-done.26), channel_id=1, source_target_pairs={{0,1},{1,0},{2,3},{3,2},{4,5},{5,4},{6,7},{7,6},{8,9},{9,8},{10,11... | collective-permute-start | bytes 786440 | tf_op jit(solution)/shard_map/ppermute | solution.py:376
  29.5 15.7 %collective-permute-start.3 = (bf16[8,2,64,128]{3,2,1,0:T(8,128)(2,1)S(1)}, bf16[8,2,64,128]{3,2,1,0:T(8,128)(2,1)S(1)}, u32[]{:S(2)}, u32[]{:S(2)}) collective-permute-start(bf16[8,2,64,128]{3,2,1,0:T(8,128)(2,1)S(1)} %copy-done.25), channel_id=1, source_target_pairs={{0,3},{1,2},{2,1},{3,0},{4,7},{5,6},{6,5},{7,4},{8,11},{9,10},{10,... | collective-permute-start | bytes 786440 | tf_op jit(solution)/shard_map/ppermute | solution.py:376
  33.1 0.7 copy-start.17
  45.3 0.7 copy-start.3
  45.3 0.8 copy-start.1
  46.1 9.8 %copy-start.21 = (bf16[8,2,64,128]{3,2,1,0:T(8,128)(2,1)S(1)}, bf16[8,2,64,128]{3,2,1,0:T(8,128)(2,1)}, u32[]{:S(2)}) copy-start(bf16[8,2,64,128]{3,2,1,0:T(8,128)(2,1)} %get-tuple-element.33) | copy-start | bytes 786436
  46.1 12.4 %copy-start.24 = (bf16[8,2,64,128]{3,2,1,0:T(8,128)(2,1)S(1)}, bf16[8,2,64,128]{3,2,1,0:T(8,128)(2,1)}, u32[]{:S(2)}) copy-start(bf16[8,2,64,128]{3,2,1,0:T(8,128)(2,1)} %get-tuple-element.36) | copy-start | bytes 786436
  46.1 14.0 %copy-start.23 = (bf16[8,2,64,128]{3,2,1,0:T(8,128)(2,1)S(1)}, bf16[8,2,64,128]{3,2,1,0:T(8,128)(2,1)}, u32[]{:S(2)}) copy-start(bf16[8,2,64,128]{3,2,1,0:T(8,128)(2,1)} %get-tuple-element.37) | copy-start | bytes 786436
  46.1 14.4 %copy-start.22 = (bf16[8,2,64,128]{3,2,1,0:T(8,128)(2,1)S(1)}, bf16[8,2,64,128]{3,2,1,0:T(8,128)(2,1)}, u32[]{:S(2)}) copy-start(bf16[8,2,64,128]{3,2,1,0:T(8,128)(2,1)} %get-tuple-element.38) | copy-start | bytes 786436
  50.1 1.3 copy-start
  51.4 31.0 %all-to-all-start.3 = ((bf16[8,16,64,128]{3,2,1,0:T(8,128)(2,1)}), bf16[8,16,64,128]{3,2,1,0:T(8,128)(2,1)}, u32[]{:S(2)}, u32[]{:S(2)}) async-start(bf16[8,16,64,128]{3,2,1,0:T(8,128)(2,1)} %hold.2), calls=%async_computation.4 | async-start | bytes 4194304 | tf_op jit(solution)/shard_map/all_to_all | solution.py:396
  55.8 118.7 %reduce-scatter.5.cloned.1.call-start = ((), (), s32[]{:S(2)}) async-start(), calls=%async_computation.7 | async-start | bytes 5242880 | tf_op jit(solution)/shard_map/reduce_scatter | solution.py:418
  55.9 37.6 %collective-permute-start.2 = (bf16[8,2,64,128]{3,2,1,0:T(8,128)(2,1)S(1)}, bf16[8,2,64,128]{3,2,1,0:T(8,128)(2,1)S(1)}, u32[]{:S(2)}, u32[]{:S(2)}) collective-permute-start(bf16[8,2,64,128]{3,2,1,0:T(8,128)(2,1)S(1)} %copy-done.21), channel_id=1, source_target_pairs={{0,2},{1,3},{2,0},{3,1},{4,6},{5,7},{6,4},{7,5},{8,10},{9,11},{10,... | collective-permute-start | bytes 786440 | tf_op jit(solution)/shard_map/ppermute | solution.py:376
  58.5 35.0 %collective-permute-start.4 = (bf16[8,2,64,128]{3,2,1,0:T(8,128)(2,1)S(1)}, bf16[8,2,64,128]{3,2,1,0:T(8,128)(2,1)S(1)}, u32[]{:S(2)}, u32[]{:S(2)}) collective-permute-start(bf16[8,2,64,128]{3,2,1,0:T(8,128)(2,1)S(1)} %copy-done.24), channel_id=1, source_target_pairs={{0,1},{1,0},{2,3},{3,2},{4,5},{5,4},{6,7},{7,6},{8,9},{9,8},{10,11... | collective-permute-start | bytes 786440 | tf_op jit(solution)/shard_map/ppermute | solution.py:376
  60.1 33.4 %collective-permute-start.5 = (bf16[8,2,64,128]{3,2,1,0:T(8,128)(2,1)S(1)}, bf16[8,2,64,128]{3,2,1,0:T(8,128)(2,1)S(1)}, u32[]{:S(2)}, u32[]{:S(2)}) collective-permute-start(bf16[8,2,64,128]{3,2,1,0:T(8,128)(2,1)S(1)} %copy-done.23), channel_id=1, source_target_pairs={{0,2},{1,3},{2,0},{3,1},{4,6},{5,7},{6,4},{7,5},{8,10},{9,11},{10,... | collective-permute-start | bytes 786440 | tf_op jit(solution)/shard_map/ppermute | solution.py:376
  60.4 33.1 %collective-permute-start.6 = (bf16[8,2,64,128]{3,2,1,0:T(8,128)(2,1)S(1)}, bf16[8,2,64,128]{3,2,1,0:T(8,128)(2,1)S(1)}, u32[]{:S(2)}, u32[]{:S(2)}) collective-permute-start(bf16[8,2,64,128]{3,2,1,0:T(8,128)(2,1)S(1)} %copy-done.22), channel_id=1, source_target_pairs={{0,3},{1,2},{2,1},{3,0},{4,7},{5,6},{6,5},{7,4},{8,11},{9,10},{10,... | collective-permute-start | bytes 786440 | tf_op jit(solution)/shard_map/ppermute | solution.py:376
  93.5 0.7 copy-start.11
  93.5 0.8 copy-start.5
  93.5 0.9 copy-start.7
  93.5 1.0 copy-start.9
  94.6 1.2 copy-start.13
  94.6 1.5 copy-start.14
  94.6 123.8 %reduce-scatter.3.cloned.1.call-start = ((), (), s32[]{:S(2)}) async-start(), calls=%async_computation.6 | async-start | bytes 2621440 | tf_op jit(solution)/shard_map/reduce_scatter | solution.py:418
  132.8 0.9 copy-start.15
  132.8 1.0 copy-start.4
  132.8 1.1 copy-start.12
  132.8 1.2 copy-start.2
  132.8 1.2 copy-start.16
  132.8 1.3 copy-start.6
  132.9 1.4 copy-start.8
  132.9 1.4 copy-start.10
  170.1 7.6 %collective-permute-start.7 = (bf16[1,128,512]{2,1,0:T(8,128)(2,1)}, bf16[1,128,512]{2,1,0:T(8,128)(2,1)S(1)}, u32[]{:S(2)}, u32[]{:S(2)}) collective-permute-start(bf16[1,128,512]{2,1,0:T(8,128)(2,1)} %get-tuple-element.40), channel_id=1, source_target_pairs={{0,1},{1,0},{2,3},{3,2},{4,5},{5,4},{6,7},{7,6},{8,9},{9,8},{10,11... | collective-permute-start | bytes 393224 | tf_op jit(solution)/shard_map/ppermute | solution.py:376
  171.7 14.7 %collective-permute-start.8 = (bf16[1,128,512]{2,1,0:T(8,128)(2,1)}, bf16[1,128,512]{2,1,0:T(8,128)(2,1)S(1)}, u32[]{:S(2)}, u32[]{:S(2)}) collective-permute-start(bf16[1,128,512]{2,1,0:T(8,128)(2,1)} %get-tuple-element.41), channel_id=1, source_target_pairs={{0,2},{1,3},{2,0},{3,1},{4,6},{5,7},{6,4},{7,5},{8,10},{9,11},{10,... | collective-permute-start | bytes 393224 | tf_op jit(solution)/shard_map/ppermute | solution.py:376
  174.3 12.0 %collective-permute-start.9 = (bf16[1,128,512]{2,1,0:T(8,128)(2,1)}, bf16[1,128,512]{2,1,0:T(8,128)(2,1)S(1)}, u32[]{:S(2)}, u32[]{:S(2)}) collective-permute-start(bf16[1,128,512]{2,1,0:T(8,128)(2,1)} %get-tuple-element.42), channel_id=1, source_target_pairs={{0,3},{1,2},{2,1},{3,0},{4,7},{5,6},{6,5},{7,4},{8,11},{9,10},{10,... | collective-permute-start | bytes 393224 | tf_op jit(solution)/shard_map/ppermute | solution.py:376
  177.6 40.7 %copy-start.18 = (bf16[1,128,512]{2,1,0:T(8,128)(2,1)}, bf16[1,128,512]{2,1,0:T(8,128)(2,1)S(1)}, u32[]{:S(2)}) copy-start(bf16[1,128,512]{2,1,0:T(8,128)(2,1)S(1)} %collective-permute-done.7.refs_3_) | copy-start | bytes 393220
  186.3 32.0 %copy-start.19 = (bf16[1,128,512]{2,1,0:T(8,128)(2,1)}, bf16[1,128,512]{2,1,0:T(8,128)(2,1)S(1)}, u32[]{:S(2)}) copy-start(bf16[1,128,512]{2,1,0:T(8,128)(2,1)S(1)} %collective-permute-done.8.refs_4_) | copy-start | bytes 393220
  186.4 32.0 %copy-start.20 = (bf16[1,128,512]{2,1,0:T(8,128)(2,1)}, bf16[1,128,512]{2,1,0:T(8,128)(2,1)S(1)}, u32[]{:S(2)}) copy-start(bf16[1,128,512]{2,1,0:T(8,128)(2,1)S(1)} %collective-permute-done.9.refs_5_) | copy-start | bytes 393220
Sparse Core Ops, SparseCore 0:
  94.7 76.7 reduce-scatter.4
  173.9 44.4 reduce-scatter.2
